TPU v7x, 256 devices: a whole 4x4x8 slice. The times are simulated.
256 devices in a mesh: rows: 16 (over z, core), hid: 16 (over y, x).
Axes of the slice: x: 4, y: 4, z: 8, core: 2. Of those that a mesh axis runs over, the one named last changes fastest.
Arguments:
- q_latent: bfloat16 [512, 128, 512], P(('rows', 'hid')), may hold values from -450 to 450
- q_rope: bfloat16 [512, 64, 128], P(('rows', 'hid')), may hold values from -4 to 4
- latent_cache: bfloat16 [512, 3072, 512], P(('rows', 'hid')), may hold values from -8 to 8
- rope_cache: bfloat16 [512, 64, 3072], P(('rows', 'hid')), may hold values from -4 to 4
- indices: int32 [512, 2048], P(('rows', 'hid')), may hold values from 0 to 3071, as said below
- w_uv: bfloat16 [128, 512, 128], P('hid'), may hold values from -2 to 2
- w_out: bfloat16 [16384, 7168], P('hid', 'rows'), may hold values from -0.09375 to 0.09375
- residual: bfloat16 [512, 7168], P(None, 'rows'), may hold values from -64 to 64
- norm_gain: bfloat16 [7168], P('rows'), may hold values from 0.099609375 to 1.8984375
- w_gate: bfloat16 [7168, 18432], P('rows', 'hid'), may hold values from -0.0625 to 0.0625
- w_up: bfloat16 [7168, 18432], P('rows', 'hid'), may hold values from -0.0625 to 0.0625
- w_down: bfloat16 [18432, 7168], P('hid', 'rows'), may hold values from -0.046875 to 0.046875
Outputs:
- layer_out: bfloat16 [512, 7168], P('hid', 'rows')
Inputs may be any that keep to these rules, and one draw needn't show every extreme that they name: Each query's 2048 indices are distinct rows of its own sequence's cache.
All inputs are finite; a program needn't handle non-finite values.
Results may differ from a plain program's by a relative error of at most 0.02.
Values may be sent and summed in bfloat16 or wider, within the bound.
No kernel may reach another device: no remote copies, remote signals or barrier semaphores. Data moves between devices by JAX's collectives and lax.ppermute only.
A program may use at most 64 MiB of HBM per device.

v0:
```python
import math

import jax
import jax.numpy as jnp
from jax import lax
from jax.sharding import PartitionSpec as P

D = 7168
ROPE = 64
VDIM = 128


def attend_row(query_lat, query_rope, lat_rows, rope_rows, chosen):
    picked = jnp.take(lat_rows, chosen, axis=0)
    picked_rope = jnp.take(rope_rows, chosen, axis=1)
    scores = jnp.dot(query_lat, picked.T, preferred_element_type=jnp.float32)
    scores = scores + jnp.dot(query_rope.T, picked_rope, preferred_element_type=jnp.float32)
    scores = scores * (1.0 / math.sqrt(VDIM + ROPE))
    weights = jax.nn.softmax(scores, axis=-1).astype(jnp.bfloat16)
    return jnp.dot(weights, picked, preferred_element_type=jnp.float32).astype(jnp.bfloat16)


def gated(gate, upper, rstd):
    return (jax.nn.silu(gate * rstd[:, None]) * (upper * rstd[:, None])).astype(jnp.bfloat16)


def body(
    q_latent,
    q_rope,
    latent_cache,
    rope_cache,
    indices,
    w_uv,
    w_out,
    residual,
    norm_gain,
    w_gate,
    w_up,
    w_down,
):
    context = jax.vmap(attend_row)(q_latent, q_rope, latent_cache, rope_cache, indices)
    moved = lax.all_to_all(context, "hid", split_axis=1, concat_axis=0, tiled=True)
    heads_out = jnp.einsum("bhl,hlv->bhv", moved, w_uv, preferred_element_type=jnp.float32).astype(
        jnp.bfloat16
    )
    flat_heads = heads_out.reshape(heads_out.shape[0], heads_out.shape[1] * heads_out.shape[2])
    partial_attn = jnp.dot(
        lax.all_gather(flat_heads, "rows", axis=0, tiled=True),
        w_out,
        preferred_element_type=jnp.float32,
    )
    attn = lax.psum(partial_attn.astype(jnp.bfloat16), "hid").astype(jnp.float32)
    mid = (residual.astype(jnp.float32) + attn).astype(jnp.bfloat16)
    mid_wide = mid.astype(jnp.float32)
    squares = jnp.sum(mid_wide * mid_wide, axis=1)
    scaled = (mid_wide * norm_gain.astype(jnp.float32)[None, :]).astype(jnp.bfloat16)
    gate_part = jnp.dot(scaled, w_gate, preferred_element_type=jnp.float32)
    upper_part = jnp.dot(scaled, w_up, preferred_element_type=jnp.float32)
    gate, upper, total_sq = (
        lax.psum(gate_part.astype(jnp.bfloat16), "rows").astype(jnp.float32),
        lax.psum(upper_part.astype(jnp.bfloat16), "rows").astype(jnp.float32),
        lax.psum(squares.astype(jnp.bfloat16), "rows").astype(jnp.float32),
    )
    hidden = gated(gate, upper, lax.rsqrt(total_sq / D + 1e-06))
    block_rows = hidden.shape[0] // lax.axis_size("hid")
    down = lax.psum_scatter(
        jnp.dot(hidden, w_down, preferred_element_type=jnp.float32).astype(jnp.bfloat16),
        "hid",
        scatter_dimension=0,
        tiled=True,
    ).astype(jnp.float32)
    own_mid = lax.dynamic_slice_in_dim(mid_wide, lax.axis_index("hid") * block_rows, block_rows, 0)
    return (own_mid + down).astype(jnp.bfloat16)


def solution(mesh):
    placed = (
        P(("rows", "hid"), None, None),
        P(("rows", "hid"), None, None),
        P(("rows", "hid"), None, None),
        P(("rows", "hid"), None, None),
        P(("rows", "hid"), None),
        P("hid", None, None),
        P("hid", "rows"),
        P(None, "rows"),
        P("rows"),
        P("rows", "hid"),
        P("rows", "hid"),
        P("hid", "rows"),
    )
    return jax.shard_map(
        body, mesh=mesh, in_specs=placed, out_specs=P("hid", "rows"), check_vma=False
    )
```

profile of v0, /device:TPU:1, one launch (start us, length us, event | category | flops | bytes accessed | tf_op | source)
XLA Modules:
  0.0 499.2 jit_solution(18012036673317952660)
XLA Ops:
  6.5 0.0 copy-start
  6.5 0.0 all-gather.2.cloned.1.call-start
  6.5 0.8 compare_and_fusion
  7.4 0.7 fusion.16
  8.1 1.8 copy.35
  9.9 40.5 %gather_fusion.1 = bf16[4096,64]{1,0:T(8,128)(2,1)} fusion(bf16[2,64,3072]{1,2,0:T(8,128)(2,1)S(1)} %copy.35, s32[4096]{0:T(1024)S(1)} %bitcast.36), kind=kCustom, calls=%fused_computation.1 | custom fusion | bytes 1081344 | tf_op jit(solution)/shard_map/vmap(jit(_take))/gather | solution.py:15
  50.5 2.3 copy.36
  52.8 75.5 %gather_fusion = bf16[4096,512]{1,0:T(8,128)(2,1)} fusion(bf16[2,3072,512]{2,1,0:T(8,128)(2,1)} %param.14, s32[4096]{0:T(1024)S(1)} %bitcast.37), kind=kCustom, calls=%fused_computation | custom fusion | bytes 8421376 | tf_op jit(solution)/shard_map/vmap(jit(_take))/gather | solution.py:14
  128.3 0.0 copy-done.8
  128.3 4.0 fusion.2
  132.3 0.0 copy-done.1
  132.3 0.0 copy-done.4
  132.3 0.5 fusion.6
  132.9 0.6 fusion.24
  133.5 3.8 fusion.9
  137.3 0.0 copy-start.7
  137.3 0.3 copy.38
  137.6 14.9 %all_to_all.18 = bf16[2,128,512]{2,0,1:T(2,128)(2,1)S(1)} all-to-all(bf16[2,128,512]{2,0,1:T(2,128)(2,1)S(1)} %copy.38), channel_id=1, replica_groups=mesh['rows'=16,'hid'=16] {'hid'}, dimensions={1} | all-to-all | bytes 524288 | tf_op jit(solution)/shard_map/all_to_all | solution.py:42
  152.5 0.2 copy.52
  152.7 0.1 all_to_all.16
  152.8 0.0 copy-done
  152.8 0.3 fusion.10
  153.1 0.0 copy-start.5
  153.1 0.0 copy-start.3
  153.1 0.6 copy.53
  153.8 0.0 all-gather.2.cloned.1.call-update
  153.8 0.0 all-reduce.4.cloned.1.call-start
  153.8 39.6 %all-gather.2.cloned.1.call-done = bf16[512,1024]{1,0:T(8,128)(2,1)} async-done(((bf16[32,1024]{1,0:T(8,128)(2,1)}), bf16[512,1024]{1,0:T(8,128)(2,1)}) %all-gather.2.cloned.1.call-update) | async-done | bytes 1048592 | tf_op jit(solution)/shard_map/all_gather | solution.py:48
  193.4 0.0 copy-done.7
  193.4 2.8 convolution_convert_fusion.3
  196.2 0.0 all-reduce.4.cloned.1.call-update
  196.2 0.0 all-reduce.6.cloned.1.call-start
  196.2 0.0 copy-done.5
  196.3 0.0 copy-done.3
  196.3 0.2 copy.34
  196.5 92.4 %all-reduce.4.cloned.1.call-done = bf16[512,448]{1,0:T(8,128)(2,1)} async-done(((bf16[512,448]{1,0:T(8,128)(2,1)}), bf16[512,448]{1,0:T(8,128)(2,1)}) %all-reduce.4.cloned.1.call-update) | async-done | bytes 458768 | tf_op jit(solution)/shard_map/psum | solution.py:52
  288.9 3.4 convolution_convert_fusion.1
  292.3 0.0 copy-done.2
  292.3 1.9 convolution_convert_fusion
  294.2 0.0 all-reduce.6.cloned.1.call-update
  294.2 0.0 reduce-scatter.4.cloned.1.call-start
  294.2 0.3 fusion.12
  294.5 25.4 %psum.30 = bf16[512]{0:T(512)(128)(2,1)S(1)} all-reduce(bf16[512]{0:T(512)(128)(2,1)S(1)} %get-tuple-element.8), channel_id=1, replica_groups=mesh['rows'=16,'hid'=16] {'rows'}, use_global_device_ids=true, to_apply=%region_5.6 | all-reduce | flops 512 | bytes 2048 | tf_op jit(solution)/shard_map/psum | solution.py:62
  319.9 91.2 %all-reduce.6.cloned.1.call-done = (bf16[512,1152]{1,0:T(8,128)(2,1)}, bf16[512,1152]{1,0:T(8,128)(2,1)}) async-done(((bf16[512,1152]{1,0:T(8,128)(2,1)}, bf16[512,1152]{1,0:T(8,128)(2,1)}), (bf16[512,1152]{1,0:T(8,128)(2,1)}, bf16[512,1152]{1,0:T(8,128)(2,1)})) %all-reduce.6.cloned.1.call-update) | async-done | bytes 2359312 | tf_op jit(solution)/shard_map/psum | solution.py:61
  411.1 3.8 convolution_convert_fusion.2
  414.9 0.0 reduce-scatter.4.cloned.1.call-update
  415.0 76.3 %reduce-scatter.4.cloned.1.call-done = bf16[32,448]{1,0:T(8,128)(2,1)} async-done(((bf16[512,448]{1,0:T(8,128)(2,1)}), bf16[32,448]{1,0:T(8,128)(2,1)}) %reduce-scatter.4.cloned.1.call-update) | async-done | bytes 28688 | tf_op jit(solution)/shard_map/reduce_scatter | solution.py:66
  491.3 1.4 add_convert_fusion.1
  (9 shorter events, 0.0 us)
Async XLA Ops:
  6.5 146.3 %copy-start = (bf16[8,512,128]{2,1,0:T(8,128)(2,1)S(1)}, bf16[8,512,128]{2,1,0:T(8,128)(2,1)}, u32[]{:S(2)}) copy-start(bf16[8,512,128]{2,1,0:T(8,128)(2,1)} %param.17) | copy-start | bytes 3145732
  6.5 186.9 %all-gather.2.cloned.1.call-start = ((), (), s32[]{:S(2)}) async-start(), calls=%async_computation.2 | async-start | bytes 1114112 | tf_op jit(solution)/shard_map/all_gather | solution.py:48
  52.8 75.5 %copy-start.8 = (bf16[2,128,512]{2,1,0:T(8,128)(2,1)S(1)}, bf16[2,128,512]{2,1,0:T(8,128)(2,1)}, u32[]{:S(2)}) copy-start(bf16[2,128,512]{2,1,0:T(8,128)(2,1)} %param.12) | copy-start | bytes 786436
  128.3 4.0 copy-start.1
  128.3 4.0 copy-start.4
  137.3 56.1 %copy-start.7 = (bf16[1024,448]{0,1:T(8,128)(2,1)S(1)}, bf16[1024,448]{0,1:T(8,128)(2,1)}, u32[]{:S(2)}) copy-start(bf16[1024,448]{0,1:T(8,128)(2,1)} %param.18) | copy-start | bytes 2752516
  153.1 43.1 %copy-start.5 = (bf16[448]{0:T(512)(128)(2,1)S(1)}, bf16[448]{0:T(512)(128)(2,1)}, u32[]{:S(2)}) copy-start(bf16[448]{0:T(512)(128)(2,1)} %param.20) | copy-start | bytes 2692
  153.1 43.2 %copy-start.3 = (bf16[512,448]{0,1:T(8,128)(2,1)S(1)}, bf16[512,448]{0,1:T(8,128)(2,1)}, u32[]{:S(2)}) copy-start(bf16[512,448]{0,1:T(8,128)(2,1)} %param.19) | copy-start | bytes 1376260
  153.8 135.1 %all-reduce.4.cloned.1.call-start = ((), (), s32[]{:S(2)}) async-start(), calls=%async_computation.3 | async-start | bytes 1048576 | tf_op jit(solution)/shard_map/psum | solution.py:52
  196.2 214.9 %all-reduce.6.cloned.1.call-start = ((), (), s32[]{:S(2)}) async-start(), calls=%async_computation.5 | async-start | bytes 4718592 | tf_op jit(solution)/shard_map/psum | solution.py:61
  288.9 3.4 copy-start.2
  288.9 3.4 copy-start.6
  294.2 197.1 %reduce-scatter.4.cloned.1.call-start = ((), (), s32[]{:S(2)}) async-start(), calls=%async_computation.4 | async-start | bytes 557056 | tf_op jit(solution)/shard_map/reduce_scatter | solution.py:66
Sparse Core Ops, SparseCore 0:
  153.9 39.4 all-gather.1
  196.6 92.2 all-reduce.3
  294.3 116.7 all-reduce.5
  415.1 76.1 reduce-scatter.3
where the time goes:
time: 501 us; the launch traced here: 499 us
  waiting for transfers between devices  300 us (60%)
  local copies, waits for them, and re-layouts  122 us (24%)
  blocking collectives  40.3 us (8%)
  matrix products  20.5 us (4%)
  between operations  13.3 us (3%)
    psum x1, waiting for transfers between devices, body(): lax.psum(partial_attn.astype(jnp.bfloat16), 'hid').astype(jnp.float32)  92.4 us
    psum x1, waiting for transfers between devices, body(): lax.psum(upper_part.astype(jnp.bfloat16), 'rows').astype(jnp.float32)  91.2 us
    reduce_scatter x1, waiting for transfers between devices, body(): lax.psum_scatter(jnp.dot(hidden, w_down, preferred_element_type=jnp.float...  76.3 us
    gather x1, local copies, waits for them, and re-layouts, attend_row(): picked = jnp.take(lat_rows, chosen, axis=0)  75.5 us
    gather x2, local copies, waits for them, and re-layouts, attend_row(): picked_rope = jnp.take(rope_rows, chosen, axis=1)  42.9 us
    all_gather x1, waiting for transfers between devices, body(): lax.all_gather(flat_heads, 'rows', axis=0, tiled=True)  39.6 us
    psum x1, blocking collectives, body(): lax.psum(squares.astype(jnp.bfloat16), 'rows').astype(jnp.float32)  25.4 us
    all_to_all x1, blocking collectives, body(): lax.all_to_all(context, 'hid', split_axis=1, concat_axis=0, tiled=True)  14.9 us
  transfers between devices with their start and end apart: 4, of which 4 were waited for; matrix products, arithmetic and copies ran while one was open for 0% of the time, Pallas kernels for 0%

commit v1 on v0

v1 whole, which is shorter than its diff:
```python
import functools
import math

import jax
import jax.numpy as jnp
from jax import lax
from jax.experimental import pallas as pl
from jax.experimental.pallas import tpu as pltpu
from jax.sharding import Mesh
from jax.sharding import PartitionSpec as P

D = 7168
ROPE = 64
VDIM = 128
LAT = 512
HEADS = 128
CTX = 3072
F32 = jnp.float32
BF16 = jnp.bfloat16
HID = ("y", "x")
LAYER = ("core", "y", "x")
LANES = 128
EXP2_SCALE = math.log2(math.e) / math.sqrt(VDIM + ROPE)


def dot(a, b, dims=((1,), (0,))):
    return lax.dot_general(a, b, (dims, ((), ())), preferred_element_type=F32)


def iota(shape, dim):
    return lax.broadcasted_iota(jnp.int32, shape, dim)


def whole(n):
    return [pl.BlockSpec(memory_space=pltpu.VMEM)] * n


def smem():
    return pl.BlockSpec(memory_space=pltpu.SMEM)


def params(mib):
    return pltpu.CompilerParams(vmem_limit_bytes=mib * 2**20)


def cost(flops, nbytes):
    return pl.CostEstimate(flops=flops, bytes_accessed=nbytes, transcendentals=0)


def attend_kernel(idx_ref, ql_ref, qr_ref, lat_ref, rope_ref, out_ref, scores, both):
    seq = pl.program_id(0)
    idx = idx_ref[0]
    groups = CTX // LANES
    high = (iota((32, idx.shape[1]), 0) == lax.shift_right_logical(idx, 7)).astype(F32).astype(BF16)
    low = (iota((LANES, idx.shape[1]), 0) == (idx & 127)).astype(F32).astype(BF16)
    count = dot(high, low, ((1,), (1,)))
    bias = jnp.where(count > 0.5, 0.0, -1e30)

    q_lat = ql_ref[0]
    q_rope = qr_ref[0]
    step = 512
    top = jnp.full((HEADS, LANES), -3e38, F32)
    for at in range(0, CTX, step):
        part = dot(q_lat, lat_ref[0, at : at + step, :], ((1,), (1,)))
        part = part + dot(q_rope, rope_ref[0, :, at : at + step], ((0,), (0,)))
        for j in range(step // LANES):
            g = at // LANES + j
            piece = part[:, j * LANES : (j + 1) * LANES] + bias[g : g + 1, :]
            scores[:, g * LANES : (g + 1) * LANES] = piece
            top = jnp.maximum(top, piece)
    peak = jnp.max(top, axis=1, keepdims=True)
    total = jnp.zeros((HEADS, LANES), F32)
    acc = jnp.zeros((HEADS, LAT), F32)
    for at in range(0, CTX, step):
        e = jnp.exp2((scores[:, at : at + step] - peak) * EXP2_SCALE)
        for j in range(step // LANES):
            total = total + e[:, j * LANES : (j + 1) * LANES]
        acc = acc + dot(e.astype(BF16), lat_ref[0, at : at + step, :])
    norm = jnp.sum(total, axis=1, keepdims=True)
    both[pl.ds(pl.multiple_of(seq * HEADS, HEADS), HEADS), :] = (acc / norm).astype(BF16)

    @pl.when(seq == 1)
    def _():
        row = iota((256, 256), 0)
        col = iota((256, 256), 1)
        i, s, h, c = row & 3, (row >> 2) & 1, (row >> 3) & 15, row >> 7
        pick = (col == s * HEADS + h * 8 + c * 4 + i).astype(F32).astype(BF16)
        out_ref[...] = dot(pick, both[...]).astype(BF16)


def attend(idx, q_lat, q_rope, lat, rope):
    return pl.pallas_call(
        attend_kernel,
        grid=(2,),
        in_specs=[
            pl.BlockSpec((1, 1, idx.shape[2]), lambda s: (s, 0, 0)),
            pl.BlockSpec((1, HEADS, LAT), lambda s: (s, 0, 0)),
            pl.BlockSpec((1, ROPE, HEADS), lambda s: (s, 0, 0)),
            pl.BlockSpec((1, CTX, LAT), lambda s: (s, 0, 0)),
            pl.BlockSpec((1, ROPE, CTX), lambda s: (s, 0, 0)),
        ],
        out_specs=pl.BlockSpec((256, LAT), lambda s: (0, 0)),
        out_shape=jax.ShapeDtypeStruct((256, LAT), BF16),
        scratch_shapes=[pltpu.VMEM((HEADS, CTX), F32), pltpu.VMEM((256, LAT), BF16)],
        compiler_params=params(24),
        cost_estimate=cost(1_800_000_000, 8_000_000),
        name="attend",
    )(idx, q_lat, q_rope, lat, rope)


def heads_kernel(core_ref, x_ref, w_ref, out_ref):
    core = core_ref[0]
    row = iota((256, 256), 0)
    col = iota((256, 256), 1)
    pick = (col == (row & 63) * 4 + (row >> 6)).astype(F32).astype(BF16)
    sorted_rows = dot(pick, x_ref[...]).astype(BF16)
    for i in range(4):
        part = dot(sorted_rows[i * 64 : (i + 1) * 64], w_ref[core * 4 + i]).astype(BF16)
        for k in range(8):
            out_ref[k, :, i * VDIM : (i + 1) * VDIM] = part


def heads(core, x, w_uv):
    return pl.pallas_call(
        heads_kernel,
        in_specs=[smem()] + whole(2),
        out_specs=whole(1)[0],
        out_shape=jax.ShapeDtypeStruct((8, 64, 512), BF16),
        compiler_params=params(16),
        cost_estimate=cost(100_000_000, 2_000_000),
        name="heads",
    )(core, x, w_uv)


def project_kernel(core_ref, own_ref, other_ref, w_ref, out_ref):
    core = core_ref[0]
    mine = pl.ds(pl.multiple_of(core * 512, 512), 512)
    theirs = pl.ds(pl.multiple_of((1 - core) * 512, 512), 512)
    total = dot(own_ref[...], w_ref[mine, :]) + dot(other_ref[...], w_ref[theirs, :])
    out_ref[...] = total.astype(BF16)


def project(core, own, other, w_out):
    return pl.pallas_call(
        project_kernel,
        in_specs=[smem()] + whole(3),
        out_specs=whole(1)[0],
        out_shape=jax.ShapeDtypeStruct((512, w_out.shape[1]), BF16),
        compiler_params=params(16),
        cost_estimate=cost(470_000_000, 3_000_000),
        name="project",
    )(core, own, other, w_out)


def middle_kernel(place_ref, parts_ref, res_ref, gain_ref, mid_ref, out_ref):
    rows, cols = mid_ref.shape
    total = parts_ref[0].astype(F32)
    for k in range(1, parts_ref.shape[0]):
        total = total + parts_ref[k].astype(F32)
    res = res_ref[pl.ds(pl.multiple_of(place_ref[0] * rows, rows), rows), :]
    mid = (res.astype(F32) + total).astype(BF16)
    mid_ref[...] = mid
    wide = mid.astype(F32)
    squares = jnp.sum(wide * wide, axis=1, keepdims=True)
    upper = squares.astype(BF16).astype(F32)
    lane = iota((rows, 512 - cols), 1)
    extra = jnp.where(lane == 0, upper, jnp.where(lane == 1, squares - upper, 0.0)).astype(BF16)
    scaled = (wide * gain_ref[...].astype(F32)).astype(BF16)
    for k in range(out_ref.shape[0]):
        out_ref[k, :, :cols] = scaled
        out_ref[k, :, cols:] = extra


def middle(place, parts, residual, gain):
    rows, cols = parts.shape[1:]
    return pl.pallas_call(
        middle_kernel,
        in_specs=[smem()] + whole(3),
        out_specs=whole(2),
        out_shape=[
            jax.ShapeDtypeStruct((rows, cols), BF16),
            jax.ShapeDtypeStruct((16, rows, 512), BF16),
        ],
        compiler_params=params(16),
        cost_estimate=cost(1_000_000, 1_500_000),
        name="middle",
    )(place, parts, residual, gain)


def widen_kernel(core_ref, own_ref, other_ref, g_own, g_other, u_own, u_other, out_ref):
    core = core_ref[0]
    deep = g_own.shape[0]
    full = pl.ds(pl.multiple_of(core * 640, LANES), 512)
    own = own_ref[:, :deep]
    other = other_ref[:, :deep]
    chunk = out_ref.shape[1]

    def put(at, width, value):
        value = value.astype(BF16)
        for z in range(8):
            out_ref[z, :, at : at + width] = value[z * chunk : (z + 1) * chunk]

    put(0, 512, dot(own, g_own[:, full]) + dot(other, g_other[:, full]))
    put(512, 512, dot(own, u_own[:, full]) + dot(other, u_other[:, full]))
    gate = dot(own, g_own[:, 512:640]) + dot(other, g_other[:, 512:640])
    upper = dot(own, u_own[:, 512:640]) + dot(other, u_other[:, 512:640])
    first = core == 0
    straight = jnp.where(first, gate, upper)
    turned = pltpu.roll(jnp.where(first, upper, gate), 64, 1)
    lane = iota(gate.shape, 1)
    front = jnp.where(first, 64, 128)
    back = jnp.where(first, 0, 64)
    put(1024, LANES, jnp.where((lane >= back) & (lane < front), straight, turned))
    squares = jnp.sum(own_ref[:, deep:].astype(F32), axis=1, keepdims=True) + jnp.sum(
        other_ref[:, deep:].astype(F32), axis=1, keepdims=True
    )
    high = squares.astype(BF16).astype(F32)
    put(1152, LANES, jnp.where(lane == 0, high, jnp.where(lane == 1, squares - high, 0.0)))


def widen(core, own, other, *weights):
    return pl.pallas_call(
        widen_kernel,
        in_specs=[smem()] + whole(6),
        out_specs=whole(1)[0],
        out_shape=jax.ShapeDtypeStruct((8, 64, 1280), BF16),
        compiler_params=params(24),
        cost_estimate=cost(1_100_000_000, 6_000_000),
        name="widen",
    )(core, own, other, *weights)


def gated(gate, upper):
    return gate / (1.0 + jnp.exp(-gate)) * upper


def hidden_kernel(core_ref, parts_ref, out_ref):
    def total(at, width):
        value = parts_ref[0, :, at : at + width].astype(F32)
        for k in range(1, parts_ref.shape[0]):
            value = value + parts_ref[k, :, at : at + width].astype(F32)
        return value

    squares = jnp.sum(total(1152, LANES), axis=1, keepdims=True)
    rstd = lax.rsqrt(squares / D + 1e-06)
    full = gated(total(0, 512) * rstd, total(512, 512) * rstd).astype(BF16)
    mixed = total(1024, LANES) * rstd
    value = gated(mixed, pltpu.roll(mixed, 64, 1))
    first = core_ref[0] == 0
    lane = iota(value.shape, 1)
    begin = jnp.where(first, 0, 64)
    value = jnp.where(first, value, pltpu.roll(value, 64, 1))
    value = jnp.where((lane >= begin) & (lane < begin + 64), value, 0.0).astype(BF16)
    for k in range(out_ref.shape[0]):
        out_ref[k, :, :512] = full
        out_ref[k, :, 512:] = value


def make_hidden(core, parts):
    return pl.pallas_call(
        hidden_kernel,
        in_specs=[smem()] + whole(1),
        out_specs=whole(1)[0],
        out_shape=jax.ShapeDtypeStruct((8, 64, 640), BF16),
        compiler_params=params(16),
        cost_estimate=cost(5_000_000, 2_000_000),
        name="hidden",
    )(core, parts)


def down_kernel(core_ref, own_ref, other_ref, w_ref, out_ref):
    core = core_ref[0]
    mine = pl.ds(pl.multiple_of(core * 640, LANES), 512)
    theirs = pl.ds(pl.multiple_of((1 - core) * 640, LANES), 512)
    total = dot(own_ref[:, :512], w_ref[mine, :]) + dot(other_ref[:, :512], w_ref[theirs, :])
    total = total + dot(own_ref[:, 512:] + other_ref[:, 512:], w_ref[512:640, :])
    out_ref[...] = total.astype(BF16)


def down(core, own, other, w_down):
    return pl.pallas_call(
        down_kernel,
        in_specs=[smem()] + whole(3),
        out_specs=whole(1)[0],
        out_shape=jax.ShapeDtypeStruct((512, w_down.shape[1]), BF16),
        compiler_params=params(16),
        cost_estimate=cost(550_000_000, 3_500_000),
        name="down",
    )(core, own, other, w_down)


def last_kernel(parts_ref, mid_ref, out_ref):
    total = parts_ref[0].astype(F32)
    for k in range(1, parts_ref.shape[0]):
        total = total + parts_ref[k].astype(F32)
    out_ref[...] = (mid_ref[...].astype(F32) + total).astype(BF16)


def last(parts, mid):
    return pl.pallas_call(
        last_kernel,
        in_specs=whole(2),
        out_specs=whole(1)[0],
        out_shape=jax.ShapeDtypeStruct(mid.shape, BF16),
        compiler_params=params(16),
        cost_estimate=cost(1_000_000, 1_000_000),
        name="last",
    )(parts, mid)


def exchange(x, axes):
    return lax.all_to_all(x, axes, split_axis=0, concat_axis=0, tiled=True)


def swap(x):
    return lax.ppermute(x, "core", [(0, 1), (1, 0)])


def body(
    q_latent,
    q_rope,
    latent_cache,
    rope_cache,
    indices,
    w_uv,
    w_out,
    residual,
    norm_gain,
    w_gate,
    w_up,
    w_down,
):
    core = lax.axis_index("core").astype(jnp.int32).reshape(1)
    place = lax.axis_index(HID).astype(jnp.int32).reshape(1)
    gate_other = swap(w_gate)
    up_other = swap(w_up)

    context = attend(indices[:, None, :], q_latent, q_rope, latent_cache, rope_cache)
    moved = exchange(context.reshape(32, 8, LAT), LAYER).reshape(256, LAT)
    flat = exchange(heads(core, moved, w_uv), "z").reshape(512, 512)
    partial = project(core, flat, swap(flat), w_out)
    parts = exchange(partial.reshape(16, 32, -1), HID)
    mid, scaled = middle(place, parts, residual, norm_gain[None, :])
    scaled = exchange(scaled, HID).reshape(512, 512)
    wide = widen(core, scaled, swap(scaled), w_gate, gate_other, w_up, up_other)
    hidden = make_hidden(core, exchange(wide, "z"))
    hidden = exchange(hidden, "z").reshape(512, 640)
    outer = down(core, hidden, swap(hidden), w_down)
    return last(exchange(outer.reshape(16, 32, -1), HID), mid)


def solution(mesh):
    axes = Mesh(mesh.devices.reshape(8, 2, 4, 4), ("z", "core", "y", "x"))
    rows = ("z", "core")
    every = ("z", "core", "y", "x")
    placed = (
        P(every, None, None),
        P(every, None, None),
        P(every, None, None),
        P(every, None, None),
        P(every, None),
        P(HID, None, None),
        P(HID, rows),
        P(None, rows),
        P(rows),
        P(rows, HID),
        P(rows, HID),
        P(HID, rows),
    )
    return jax.shard_map(
        body, mesh=axes, in_specs=placed, out_specs=P(HID, rows), check_vma=False
    )
```

time: 501 us -> 174 us (0.35)
  waiting for transfers between devices: 300 us -> 19.3 us
  local copies, waits for them, and re-layouts: 122 us -> 9.94 us
  blocking collectives: 40.3 us -> 110 us
  matrix products: 20.5 us -> 0 us
  starting transfers between devices: 0.13 us -> 19.8 us
  Pallas kernels: 0 us -> 14.1 us
  between operations: 13.3 us -> 0.16 us
    psum x2 -> x0, waiting for transfers between devices: 184 us -> none  [the longest x1 92.4 us: body(): lax.psum(partial_attn.astype(jnp.bfloat16), 'hid').astype(jnp.float32)]
    gather x3 -> x0, local copies, waits for them, and re-layouts: 118 us -> none  [the longest x1 75.5 us: attend_row(): picked = jnp.take(lat_rows, chosen, axis=0)]
    all_to_all x1 -> x5, blocking collectives: 14.9 us -> 110 us  [exchange(): return lax.all_to_all(x, axes, split_axis=0, concat_axis=0, tiled=True)]
    reduce_scatter x1 -> x0, waiting for transfers between devices: 76.3 us -> none  [body(): lax.psum_scatter(jnp.dot(hidden, w_down, preferred_element_type=jnp.float...]
    all_gather x1 -> x0, waiting for transfers between devices: 39.6 us -> none  [body(): lax.all_gather(flat_heads, 'rows', axis=0, tiled=True)]
    psum x1 -> x0, blocking collectives: 25.4 us -> none  [body(): lax.psum(squares.astype(jnp.bfloat16), 'rows').astype(jnp.float32)]
    dot_general x8 -> x0, matrix products: 20.5 us -> none  [the longest x1 4 us: attend_row(): scores = jnp.dot(query_lat, picked.T, preferred_element_type=jnp.float32)]
    all_to_all x0 -> x2, waiting for transfers between devices: none -> 16.8 us  [exchange(): return lax.all_to_all(x, axes, split_axis=0, concat_axis=0, tiled=True)]
  transfers between devices with their start and end apart: 4 -> 7, of which waited for: 4 -> 4; matrix products, arithmetic and copies ran while one was open for 0% -> 2% of each run, Pallas kernels for 0% -> 0%
where the time goes in v1:
time: 174 us; the launch traced here: 173 us
  blocking collectives  110 us (63%)
  starting transfers between devices  19.8 us (11%)
  waiting for transfers between devices  19.3 us (11%)
  Pallas kernels  14.1 us (8%)
  local copies, waits for them, and re-layouts  9.94 us (6%)
    all_to_all x5, blocking collectives, exchange(): return lax.all_to_all(x, axes, split_axis=0, concat_axis=0, tiled=True)  110 us
    all_to_all x2, waiting for transfers between devices, exchange(): return lax.all_to_all(x, axes, split_axis=0, concat_axis=0, tiled=True)  16.8 us
    all_to_all x2, starting transfers between devices, exchange(): return lax.all_to_all(x, axes, split_axis=0, concat_axis=0, tiled=True)  12.4 us
    unnamed x21, local copies, waits for them, and re-layouts  9.21 us
    ppermute x5, starting transfers between devices, swap(): return lax.ppermute(x, 'core', [(0, 1), (1, 0)])  7.47 us
    pallas_call x1, Pallas kernels, attend(): pl.pallas_call(attend_kernel, grid=(2,), in_specs=[pl.BlockSpec((1, 1, id...  6.65 us
  transfers between devices with their start and end apart: 7, of which 4 were waited for; matrix products, arithmetic and copies ran while one was open for 2% of the time, Pallas kernels for 0%

profile of v1, /device:TPU:1, one launch (start us, length us, event | category | flops | bytes accessed | tf_op | source)
XLA Modules:
  0.0 173.4 jit_solution(12003648515225002168)
XLA Ops:
  0.0 0.7 broadcast_in_dim.6.idx_ref
  0.7 0.0 copy-start
  0.7 2.8 %copy-done = bf16[2,3072,512]{2,1,0:T(8,128)(2,1)S(1)} copy-done((bf16[2,3072,512]{2,1,0:T(8,128)(2,1)S(1)}, bf16[2,3072,512]{2,1,0:T(8,128)(2,1)}, u32[]{:S(2)}) %copy-start) | copy-done | bytes 6291480
  3.5 0.0 copy-start.4
  3.5 1.1 copy-done.4
  4.7 0.0 copy-start.5
  4.7 0.9 copy-done.5
  5.6 0.0 copy-start.6
  5.6 0.8 copy-done.6
  6.4 0.0 copy-start.1
  6.4 6.7 %attend.1 = bf16[256,512]{1,0:T(8,128)(2,1)} custom-call(s32[2,1,2048]{2,1,0:T(1,128)S(1)} %broadcast_in_dim.6.idx_ref, bf16[2,128,512]{2,1,0:T(8,128)(2,1)S(1)} %copy-done.5, bf16[2,64,128]{2,1,0:T(8,128)(2,1)S(1)} %copy-done.6, bf16[2,3072,512]{2,1,0:T(8,128)(2,1)S(1)} %copy-done, bf16[2,64,3072]{2,1,0:T(8,128)(2,1)S(1)} %copy-done.4), custom_call_target="tpu_custom_call" | custom-call | flops 1800000000 | bytes 8000000 | tf_op jit(solution)/shard_map/attend/pallas_call | solution.py:92
  13.0 8.6 %all-to-all-start = ((bf16[32,8,512]{2,1,0:T(8,128)(2,1)}), bf16[32,8,512]{2,1,0:T(8,128)(2,1)S(1)}, u32[]{:S(2)}, u32[]{:S(2)}) async-start(bf16[32,8,512]{2,1,0:T(8,128)(2,1)} %bitcast.2), calls=%async_computation | async-start | bytes 524288 | tf_op jit(solution)/shard_map/all_to_all | solution.py:312
  21.6 8.3 %all-to-all-done = bf16[32,8,512]{2,1,0:T(8,128)(2,1)S(1)} async-done(((bf16[32,8,512]{2,1,0:T(8,128)(2,1)}), bf16[32,8,512]{2,1,0:T(8,128)(2,1)S(1)}, u32[]{:S(2)}, u32[]{:S(2)}) %all-to-all-start) | async-done | bytes 262176 | tf_op jit(solution)/shard_map/all_to_all | solution.py:312
  29.9 0.0 copy-done.1
  29.9 0.4 heads.1
  30.3 0.0 copy-start.7
  30.3 23.6 %all_to_all.35 = bf16[8,64,512]{2,1,0:T(8,128)(2,1)S(1)} all-to-all(bf16[8,64,512]{2,1,0:T(8,128)(2,1)S(1)} %heads.1), channel_id=1, replica_groups=mesh['z'=8,'core'=2,'y'=4,'x'=4] {'z'}, dimensions={0} | all-to-all | bytes 1048576 | tf_op jit(solution)/shard_map/all_to_all | solution.py:312
  53.9 3.0 %collective-permute-start = (bf16[512,512]{1,0:T(8,128)(2,1)S(1)}, bf16[512,512]{1,0:T(8,128)(2,1)S(1)}, u32[]{:S(2)}, u32[]{:S(2)}) collective-permute-start(bf16[512,512]{1,0:T(8,128)(2,1)S(1)} %bitcast.14), channel_id=1, source_target_pairs={{0,16},{16,0},{1,17},{17,1},{2,18},{18,2},{3,19},{19,3},{4,20},{20... | collective-permute-start | bytes 1572872 | tf_op jit(solution)/shard_map/ppermute | solution.py:316
  56.9 0.0 copy-done.7
  56.9 0.5 copy.13.w_ref
  57.4 0.0 copy-start.2
  57.4 1.0 collective-permute-done.other_ref
  58.4 1.5 project.1
  59.9 0.0 copy-start.8
  59.9 3.8 %all-to-all-start.2 = ((bf16[16,32,448]{2,1,0:T(8,128)(2,1)}), bf16[16,32,448]{2,1,0:T(8,128)(2,1)S(1)}, u32[]{:S(2)}, u32[]{:S(2)}) async-start(bf16[16,32,448]{2,1,0:T(8,128)(2,1)} %bitcast.5), calls=%async_computation.2 | async-start | bytes 1048576 | tf_op jit(solution)/shard_map/all_to_all | solution.py:312
  63.7 0.0 copy-done.2
  63.7 0.7 collective-permute-start.2
  64.5 0.1 collective-permute-start.3
  64.6 1.3 copy.14.res_ref
  65.9 0.0 copy-done.8
  65.9 8.5 %all-to-all-done.2.parts_ref = bf16[16,32,448]{2,1,0:T(8,128)(2,1)S(1)} async-done(((bf16[16,32,448]{2,1,0:T(8,128)(2,1)}), bf16[16,32,448]{2,1,0:T(8,128)(2,1)S(1)}, u32[]{:S(2)}, u32[]{:S(2)}) %all-to-all-start.2) | async-done | bytes 458784 | tf_op jit(solution)/shard_map/all_to_all | solution.py:312
  74.4 0.3 middle.1
  74.7 13.4 %all_to_all.36 = bf16[16,32,512]{2,1,0:T(8,128)(2,1)S(1)} all-to-all(bf16[16,32,512]{2,1,0:T(8,128)(2,1)S(1)} %get-tuple-element.7), channel_id=1, replica_groups=mesh['z'=8,'core'=2,'y'=4,'x'=4] {'y','x'}, dimensions={0} | all-to-all | bytes 1048576 | tf_op jit(solution)/shard_map/all_to_all | solution.py:312
  88.1 2.3 %collective-permute-start.1 = (bf16[512,512]{1,0:T(8,128)(2,1)S(1)}, bf16[512,512]{1,0:T(8,128)(2,1)S(1)}, u32[]{:S(2)}, u32[]{:S(2)}) collective-permute-start(bf16[512,512]{1,0:T(8,128)(2,1)S(1)} %bitcast.11), channel_id=1, source_target_pairs={{0,16},{16,0},{1,17},{17,1},{2,18},{18,2},{3,19},{19,3},{4,20},{20... | collective-permute-start | bytes 1572872 | tf_op jit(solution)/shard_map/ppermute | solution.py:316
  90.5 0.0 collective-permute-done.2.g_other
  90.5 0.0 collective-permute-done.3.u_other
  90.5 1.5 collective-permute-done.1.other_ref
  92.0 0.0 copy-done.3
  92.0 3.4 %widen.1 = bf16[8,64,1280]{2,1,0:T(8,128)(2,1)S(1)} custom-call(s32[1]{0:T(128)} %bitcast.core_ref, bf16[512,512]{1,0:T(8,128)(2,1)S(1)} %bitcast.12, bf16[512,512]{1,0:T(8,128)(2,1)S(1)} %collective-permute-done.1.other_ref, bf16[448,1152]{1,0:T(8,128)(2,1)S(1)} %copy-done.2, bf16[448,1152]{1,0:T(8,128)(2,1)} %collective-permute-done.2.g_other, ...), custom_call_target="tpu_custom_call" | custom-call | flops 1100000000 | bytes 6000000 | tf_op jit(solution)/shard_map/widen/pallas_call | solution.py:222
  95.4 37.2 %all_to_all.37.parts_ref = bf16[8,64,1280]{2,1,0:T(8,128)(2,1)S(1)} all-to-all(bf16[8,64,1280]{2,1,0:T(8,128)(2,1)S(1)} %widen.1), channel_id=1, replica_groups=mesh['z'=8,'core'=2,'y'=4,'x'=4] {'z'}, dimensions={0} | all-to-all | bytes 2621440 | tf_op jit(solution)/shard_map/all_to_all | solution.py:312
  132.7 0.4 hidden.1
  133.0 22.3 %all_to_all.38 = bf16[8,64,640]{2,1,0:T(8,128)(2,1)S(1)} all-to-all(bf16[8,64,640]{2,1,0:T(8,128)(2,1)S(1)} %hidden.1), channel_id=1, replica_groups=mesh['z'=8,'core'=2,'y'=4,'x'=4] {'z'}, dimensions={0} | all-to-all | bytes 1310720 | tf_op jit(solution)/shard_map/all_to_all | solution.py:312
  155.4 1.3 collective-permute-start.4
  156.7 1.7 %copy.15.w_ref = bf16[1152,448]{1,0:T(8,128)(2,1)S(1)} copy(bf16[1152,448]{0,1:T(8,128)(2,1)} %param.23) | data formatting | bytes 2064384 | tf_op args[11]
  158.4 0.0 collective-permute-done.4.other_ref
  158.4 0.8 down.1
  159.3 13.4 %all_to_all.39.parts_ref = bf16[16,32,448]{2,1,0:T(8,128)(2,1)S(1)} all-to-all(bf16[16,32,448]{2,1,0:T(8,128)(2,1)S(1)} %bitcast.13), channel_id=1, replica_groups=mesh['z'=8,'core'=2,'y'=4,'x'=4] {'y','x'}, dimensions={0} | all-to-all | bytes 917504 | tf_op jit(solution)/shard_map/all_to_all | solution.py:312
  172.7 0.7 last.1
  (2 shorter events, 0.0 us)
Async XLA Ops:
  0.7 2.8 %copy-start = (bf16[2,3072,512]{2,1,0:T(8,128)(2,1)S(1)}, bf16[2,3072,512]{2,1,0:T(8,128)(2,1)}, u32[]{:S(2)}) copy-start(bf16[2,3072,512]{2,1,0:T(8,128)(2,1)} %lat_ref.1) | copy-start | bytes 18874372
  3.5 1.1 copy-start.4
  4.7 0.9 copy-start.5
  5.6 0.8 copy-start.6
  6.4 23.6 %copy-start.1 = (bf16[8,512,128]{2,1,0:T(8,128)(2,1)S(1)}, bf16[8,512,128]{2,1,0:T(8,128)(2,1)}, u32[]{:S(2)}) copy-start(bf16[8,512,128]{2,1,0:T(8,128)(2,1)} %w_ref.3) | copy-start | bytes 3145732
  13.0 16.9 %all-to-all-start = ((bf16[32,8,512]{2,1,0:T(8,128)(2,1)}), bf16[32,8,512]{2,1,0:T(8,128)(2,1)S(1)}, u32[]{:S(2)}, u32[]{:S(2)}) async-start(bf16[32,8,512]{2,1,0:T(8,128)(2,1)} %bitcast.2), calls=%async_computation | async-start | bytes 524288 | tf_op jit(solution)/shard_map/all_to_all | solution.py:312
  30.3 26.6 %copy-start.7 = (bf16[1024,448]{0,1:T(8,128)(2,1)S(1)}, bf16[1024,448]{0,1:T(8,128)(2,1)}, u32[]{:S(2)}) copy-start(bf16[1024,448]{0,1:T(8,128)(2,1)} %param.18) | copy-start | bytes 2752516
  53.9 4.5 %collective-permute-start = (bf16[512,512]{1,0:T(8,128)(2,1)S(1)}, bf16[512,512]{1,0:T(8,128)(2,1)S(1)}, u32[]{:S(2)}, u32[]{:S(2)}) collective-permute-start(bf16[512,512]{1,0:T(8,128)(2,1)S(1)} %bitcast.14), channel_id=1, source_target_pairs={{0,16},{16,0},{1,17},{17,1},{2,18},{18,2},{3,19},{19,3},{4,20},{20... | collective-permute-start | bytes 1572872 | tf_op jit(solution)/shard_map/ppermute | solution.py:316
  57.4 6.3 %copy-start.2 = (bf16[448,1152]{1,0:T(8,128)(2,1)S(1)}, bf16[448,1152]{1,0:T(8,128)(2,1)}, u32[]{:S(2)}) copy-start(bf16[448,1152]{1,0:T(8,128)(2,1)} %g_own.1) | copy-start | bytes 3096580
  59.9 5.9 %copy-start.8 = (bf16[448]{0:T(512)(128)(2,1)S(1)}, bf16[448]{0:T(512)(128)(2,1)}, u32[]{:S(2)}) copy-start(bf16[448]{0:T(512)(128)(2,1)} %param.20) | copy-start | bytes 2692
  59.9 14.5 %all-to-all-start.2 = ((bf16[16,32,448]{2,1,0:T(8,128)(2,1)}), bf16[16,32,448]{2,1,0:T(8,128)(2,1)S(1)}, u32[]{:S(2)}, u32[]{:S(2)}) async-start(bf16[16,32,448]{2,1,0:T(8,128)(2,1)} %bitcast.5), calls=%async_computation.2 | async-start | bytes 1048576 | tf_op jit(solution)/shard_map/all_to_all | solution.py:312
  63.7 26.7 %collective-permute-start.2 = (bf16[448,1152]{1,0:T(8,128)(2,1)S(1)}, bf16[448,1152]{1,0:T(8,128)(2,1)}, u32[]{:S(2)}, u32[]{:S(2)}) collective-permute-start(bf16[448,1152]{1,0:T(8,128)(2,1)S(1)} %copy-done.2), channel_id=1, source_target_pairs={{0,16},{16,0},{1,17},{17,1},{2,18},{18,2},{3,19},{19,3},{4,20},{20... | collective-permute-start | bytes 3096584 | tf_op jit(solution)/shard_map/ppermute | solution.py:316
  64.5 26.0 %collective-permute-start.3 = (bf16[448,1152]{1,0:T(8,128)(2,1)}, bf16[448,1152]{1,0:T(8,128)(2,1)}, u32[]{:S(2)}, u32[]{:S(2)}) collective-permute-start(bf16[448,1152]{1,0:T(8,128)(2,1)} %u_own.1), channel_id=1, source_target_pairs={{0,16},{16,0},{1,17},{17,1},{2,18},{18,2},{3,19},{19,3},{4,20},{20... | collective-permute-start | bytes 3096584 | tf_op jit(solution)/shard_map/ppermute | solution.py:316
  64.6 27.4 %copy-start.3 = (bf16[448,1152]{1,0:T(8,128)(2,1)S(1)}, bf16[448,1152]{1,0:T(8,128)(2,1)}, u32[]{:S(2)}) copy-start(bf16[448,1152]{1,0:T(8,128)(2,1)} %u_own.1) | copy-start | bytes 3096580
  88.1 3.9 %collective-permute-start.1 = (bf16[512,512]{1,0:T(8,128)(2,1)S(1)}, bf16[512,512]{1,0:T(8,128)(2,1)S(1)}, u32[]{:S(2)}, u32[]{:S(2)}) collective-permute-start(bf16[512,512]{1,0:T(8,128)(2,1)S(1)} %bitcast.11), channel_id=1, source_target_pairs={{0,16},{16,0},{1,17},{17,1},{2,18},{18,2},{3,19},{19,3},{4,20},{20... | collective-permute-start | bytes 1572872 | tf_op jit(solution)/shard_map/ppermute | solution.py:316
  155.4 3.1 %collective-permute-start.4 = (bf16[512,640]{1,0:T(8,128)(2,1)S(1)}, bf16[512,640]{1,0:T(8,128)(2,1)S(1)}, u32[]{:S(2)}, u32[]{:S(2)}) collective-permute-start(bf16[512,640]{1,0:T(8,128)(2,1)S(1)} %bitcast.9), channel_id=1, source_target_pairs={{0,16},{16,0},{1,17},{17,1},{2,18},{18,2},{3,19},{19,3},{4,20},{20... | collective-permute-start | bytes 1966088 | tf_op jit(solution)/shard_map/ppermute | solution.py:316

commit v2 on v1

--- a/solution.py
+++ b/solution.py
@@ -49,7 +49,7 @@
 
 def attend_kernel(idx_ref, ql_ref, qr_ref, lat_ref, rope_ref, out_ref, scores, both):
     seq = pl.program_id(0)
-    idx = idx_ref[0]
+    idx = idx_ref[pl.ds(seq, 1), :]
     groups = CTX // LANES
     high = (iota((32, idx.shape[1]), 0) == lax.shift_right_logical(idx, 7)).astype(F32).astype(BF16)
     low = (iota((LANES, idx.shape[1]), 0) == (idx & 127)).astype(F32).astype(BF16)
@@ -93,7 +93,7 @@
         attend_kernel,
         grid=(2,),
         in_specs=[
-            pl.BlockSpec((1, 1, idx.shape[2]), lambda s: (s, 0, 0)),
+            pl.BlockSpec(idx.shape, lambda s: (0, 0)),
             pl.BlockSpec((1, HEADS, LAT), lambda s: (s, 0, 0)),
             pl.BlockSpec((1, ROPE, HEADS), lambda s: (s, 0, 0)),
             pl.BlockSpec((1, CTX, LAT), lambda s: (s, 0, 0)),
@@ -102,7 +102,7 @@
         out_specs=pl.BlockSpec((256, LAT), lambda s: (0, 0)),
         out_shape=jax.ShapeDtypeStruct((256, LAT), BF16),
         scratch_shapes=[pltpu.VMEM((HEADS, CTX), F32), pltpu.VMEM((256, LAT), BF16)],
-        compiler_params=params(24),
+        compiler_params=params(58),
         cost_estimate=cost(1_800_000_000, 8_000_000),
         name="attend",
     )(idx, q_lat, q_rope, lat, rope)
@@ -132,24 +132,26 @@
     )(core, x, w_uv)
 
 
-def project_kernel(core_ref, own_ref, other_ref, w_ref, out_ref):
-    core = core_ref[0]
-    mine = pl.ds(pl.multiple_of(core * 512, 512), 512)
-    theirs = pl.ds(pl.multiple_of((1 - core) * 512, 512), 512)
-    total = dot(own_ref[...], w_ref[mine, :]) + dot(other_ref[...], w_ref[theirs, :])
-    out_ref[...] = total.astype(BF16)
-
-
-def project(core, own, other, w_out):
-    return pl.pallas_call(
-        project_kernel,
-        in_specs=[smem()] + whole(3),
-        out_specs=whole(1)[0],
-        out_shape=jax.ShapeDtypeStruct((512, w_out.shape[1]), BF16),
-        compiler_params=params(16),
-        cost_estimate=cost(470_000_000, 3_000_000),
-        name="project",
-    )(core, own, other, w_out)
+def project_kernel(turn, core_ref, heads_ref, w_ref, *rest):
+    half = core_ref[0] if turn == 0 else 1 - core_ref[0]
+    rows = pl.ds(pl.multiple_of(half * 512, 512), 512)
+    total = dot(heads_ref[...], w_ref[:, rows], ((1,), (1,)))
+    if turn == 1:
+        total = total + rest[0][...]
+    rest[-1][...] = total.astype(rest[-1].dtype)
+
+
+def project(core, own, w_out, before=None):
+    turn = 0 if before is None else 1
+    return pl.pallas_call(
+        functools.partial(project_kernel, turn),
+        in_specs=[smem()] + whole(2 + turn),
+        out_specs=whole(1)[0],
+        out_shape=jax.ShapeDtypeStruct((512, w_out.shape[0]), BF16 if turn else F32),
+        compiler_params=params(16),
+        cost_estimate=cost(240_000_000, 2_000_000),
+        name="project" + "ab"[turn],
+    )(core, own, w_out, *([before] if turn else []))
 
 
 def middle_kernel(place_ref, parts_ref, res_ref, gain_ref, mid_ref, out_ref):
@@ -187,106 +189,210 @@
     )(place, parts, residual, gain)
 
 
-def widen_kernel(core_ref, own_ref, other_ref, g_own, g_other, u_own, u_other, out_ref):
-    core = core_ref[0]
-    deep = g_own.shape[0]
-    full = pl.ds(pl.multiple_of(core * 640, LANES), 512)
+def first_kernel(core_ref, own_ref, g_ref, u_ref, out_ref):
+    deep = g_ref.shape[0]
+    full = pl.ds(pl.multiple_of(core_ref[0] * 640, LANES), 512)
     own = own_ref[:, :deep]
-    other = other_ref[:, :deep]
-    chunk = out_ref.shape[1]
-
-    def put(at, width, value):
-        value = value.astype(BF16)
-        for z in range(8):
-            out_ref[z, :, at : at + width] = value[z * chunk : (z + 1) * chunk]
-
-    put(0, 512, dot(own, g_own[:, full]) + dot(other, g_other[:, full]))
-    put(512, 512, dot(own, u_own[:, full]) + dot(other, u_other[:, full]))
-    gate = dot(own, g_own[:, 512:640]) + dot(other, g_other[:, 512:640])
-    upper = dot(own, u_own[:, 512:640]) + dot(other, u_other[:, 512:640])
-    first = core == 0
-    straight = jnp.where(first, gate, upper)
-    turned = pltpu.roll(jnp.where(first, upper, gate), 64, 1)
+    out_ref[:, 0:512] = dot(own, g_ref[:, full])
+    out_ref[:, 512:1024] = dot(own, u_ref[:, full])
+    out_ref[:, 1024:1152] = dot(own, g_ref[:, 512:640])
+    out_ref[:, 1152:1280] = dot(own, u_ref[:, 512:640])
+
+
+def first(core, own, gate, upper):
+    return pl.pallas_call(
+        first_kernel,
+        in_specs=[smem()] + whole(3),
+        out_specs=whole(1)[0],
+        out_shape=jax.ShapeDtypeStruct((512, 1280), F32),
+        compiler_params=params(16),
+        cost_estimate=cost(560_000_000, 5_000_000),
+        name="first",
+    )(core, own, gate, upper)
+
+
+def widen_kernel(takes, core_ref, z_ref, part_ref, own_ref, other_ref, g_ref, u_ref, out_ref):
+    deep = g_ref.shape[0]
+    low = core_ref[0] == 0
+    full = pl.ds(pl.multiple_of(core_ref[0] * 640, LANES), 512)
+    wide = out_ref.dtype == F32
+
+    def rows_of(ref, columns):
+        pieces = []
+        for far, begin, rows in takes:
+            at = lax.rem(z_ref[0] + far, 8) * 64 + begin
+            pieces.append(ref[pl.ds(pl.multiple_of(at, 32), rows), columns])
+        return jnp.concatenate(pieces, axis=0)
+
+    other = rows_of(other_ref, slice(0, deep))
+
+    def put(block, value):
+        value = value.astype(out_ref.dtype)
+        at = source = 0
+        for _, _, rows in takes:
+            for j in range(value.shape[1] // LANES):
+                begin = at + (block + j) * rows
+                out_ref[begin : begin + rows] = value[
+                    source : source + rows, j * LANES : (j + 1) * LANES
+                ]
+            at += 9 * rows + 16
+            source += rows
+
+    put(0, rows_of(part_ref, slice(0, 512)) + dot(other, g_ref[:, full]))
+    put(4, rows_of(part_ref, slice(512, 1024)) + dot(other, u_ref[:, full]))
+    gate = rows_of(part_ref, slice(1024, 1152)) + dot(other, g_ref[:, 512:640])
+    upper = rows_of(part_ref, slice(1152, 1280)) + dot(other, u_ref[:, 512:640])
+    straight = jnp.where(low, gate, upper)
+    turned = pltpu.roll(jnp.where(low, upper, gate), 64, 1)
     lane = iota(gate.shape, 1)
-    front = jnp.where(first, 64, 128)
-    back = jnp.where(first, 0, 64)
-    put(1024, LANES, jnp.where((lane >= back) & (lane < front), straight, turned))
-    squares = jnp.sum(own_ref[:, deep:].astype(F32), axis=1, keepdims=True) + jnp.sum(
-        other_ref[:, deep:].astype(F32), axis=1, keepdims=True
-    )
-    high = squares.astype(BF16).astype(F32)
-    put(1152, LANES, jnp.where(lane == 0, high, jnp.where(lane == 1, squares - high, 0.0)))
-
-
-def widen(core, own, other, *weights):
-    return pl.pallas_call(
-        widen_kernel,
-        in_specs=[smem()] + whole(6),
-        out_specs=whole(1)[0],
-        out_shape=jax.ShapeDtypeStruct((8, 64, 1280), BF16),
-        compiler_params=params(24),
-        cost_estimate=cost(1_100_000_000, 6_000_000),
+    begin = jnp.where(low, 0, 64)
+    put(8, jnp.where((lane >= begin) & (lane < begin + 64), straight, turned))
+    extra = slice(deep, 512)
+    squares = jnp.sum(rows_of(own_ref, extra).astype(F32), axis=1, keepdims=True)
+    squares = squares + jnp.sum(rows_of(other_ref, extra).astype(F32), axis=1, keepdims=True)
+    at = source = 0
+    for _, first_row, rows in takes:
+        same = iota((rows, LANES), 0) + first_row == iota((rows, LANES), 1)
+        line = jnp.where(same, squares[source : source + rows], 0.0)
+        line = jnp.sum(line, axis=0, keepdims=True)
+        out_ref[at + 9 * rows : at + 9 * rows + 16] = tile_of(line, wide).astype(out_ref.dtype)
+        at += 9 * rows + 16
+        source += rows
+
+
+def tile_of(line, wide):
+    row = iota((16, LANES), 0)
+    high = line if wide else line.astype(BF16).astype(F32)
+    return jnp.where(row == 0, high, jnp.where(row == 1, line - high, 0.0))
+
+
+def widen(takes, kind, core, z, part, own, other, gate, upper):
+    rows = sum(9 * n + 16 for _, _, n in takes)
+    return pl.pallas_call(
+        functools.partial(widen_kernel, takes),
+        in_specs=[smem(), smem()] + whole(5),
+        out_specs=whole(1)[0],
+        out_shape=jax.ShapeDtypeStruct((rows, LANES), kind),
+        compiler_params=params(16),
+        cost_estimate=cost(200_000_000, 6_000_000),
         name="widen",
-    )(core, own, other, *weights)
+    )(core, z, part, own, other, gate, upper)
+
+
+BLOCK = 592
+TO_LOWER = ((7, 0, 64), (2, 0, 64), (4, 0, 32))
+TO_UPPER = ((1, 0, 64), (6, 0, 64), (4, 32, 32))
+TO_KEEP = ((0, 0, 64), (5, 0, 64), (3, 0, 64))
+
+
+def merge_kernel(keep_ref, above_ref, below_ref, stay_ref, down_ref, up_ref):
+    def block(ref, k):
+        return ref[k * BLOCK : (k + 1) * BLOCK].astype(F32)
+
+    stay_ref[...] = block(keep_ref, 0) + block(above_ref, 0) + block(below_ref, 0)
+    for out_ref, k, full_ref, half_ref, shift in (
+        (down_ref, 1, below_ref, above_ref, 0),
+        (up_ref, 2, above_ref, below_ref, 32),
+    ):
+        total = block(keep_ref, k) + block(full_ref, 1)
+        half = half_ref[2 * BLOCK :].astype(F32)
+        for j in range(9):
+            at = j * 64
+            out_ref[at + 32 - shift : at + 64 - shift] = total[
+                at + 32 - shift : at + 64 - shift
+            ].astype(BF16)
+            value = total[at + shift : at + shift + 32] + half[j * 32 : (j + 1) * 32]
+            out_ref[at + shift : at + shift + 32] = value.astype(BF16)
+        line = jnp.sum(total[576:592] + half[288:304], axis=0, keepdims=True)
+        out_ref[576:592] = tile_of(line, False).astype(BF16)
+
+
+def merge(keep, above, below):
+    shapes = [jax.ShapeDtypeStruct((BLOCK, LANES), kind) for kind in (F32, BF16, BF16)]
+    return pl.pallas_call(
+        merge_kernel,
+        in_specs=whole(3),
+        out_specs=whole(3),
+        out_shape=shapes,
+        compiler_params=params(16),
+        cost_estimate=cost(5_000_000, 3_000_000),
+        name="merge",
+    )(keep, above, below)
 
 
 def gated(gate, upper):
     return gate / (1.0 + jnp.exp(-gate)) * upper
 
 
-def hidden_kernel(core_ref, parts_ref, out_ref):
-    def total(at, width):
-        value = parts_ref[0, :, at : at + width].astype(F32)
-        for k in range(1, parts_ref.shape[0]):
-            value = value + parts_ref[k, :, at : at + width].astype(F32)
-        return value
-
-    squares = jnp.sum(total(1152, LANES), axis=1, keepdims=True)
+def hidden_kernel(stay_ref, above_ref, below_ref, out_ref):
+    chunk = 64
+
+    def total(at, rows):
+        value = above_ref[at : at + rows].astype(F32) + below_ref[at : at + rows].astype(F32)
+        return stay_ref[at : at + rows] + value
+
+    line = jnp.sum(total(576, 16), axis=0, keepdims=True)
+    same = iota((chunk, LANES), 0) == iota((chunk, LANES), 1)
+    squares = jnp.sum(jnp.where(same, line, 0.0), axis=1, keepdims=True)
     rstd = lax.rsqrt(squares / D + 1e-06)
-    full = gated(total(0, 512) * rstd, total(512, 512) * rstd).astype(BF16)
-    mixed = total(1024, LANES) * rstd
+
+    def put(at, value):
+        value = value.astype(BF16)
+        for k in range(out_ref.shape[0]):
+            out_ref[k, at : at + value.shape[0]] = value
+
+    for j in range(4):
+        gate = total(j * chunk, chunk) * rstd
+        put(j * chunk, gated(gate, total((4 + j) * chunk, chunk) * rstd))
+    mixed = total(8 * chunk, chunk) * rstd
     value = gated(mixed, pltpu.roll(mixed, 64, 1))
-    first = core_ref[0] == 0
-    lane = iota(value.shape, 1)
-    begin = jnp.where(first, 0, 64)
-    value = jnp.where(first, value, pltpu.roll(value, 64, 1))
-    value = jnp.where((lane >= begin) & (lane < begin + 64), value, 0.0).astype(BF16)
-    for k in range(out_ref.shape[0]):
-        out_ref[k, :, :512] = full
-        out_ref[k, :, 512:] = value
-
-
-def make_hidden(core, parts):
+    lane = iota((32, LANES), 1)
+    put(256, jnp.where(lane < 64, value[:32], pltpu.roll(value[32:], 64, 1)))
+
+
+def make_hidden(stay, above, below):
     return pl.pallas_call(
         hidden_kernel,
-        in_specs=[smem()] + whole(1),
-        out_specs=whole(1)[0],
-        out_shape=jax.ShapeDtypeStruct((8, 64, 640), BF16),
+        in_specs=whole(3),
+        out_specs=whole(1)[0],
+        out_shape=jax.ShapeDtypeStruct((8, 288, LANES), BF16),
         compiler_params=params(16),
         cost_estimate=cost(5_000_000, 2_000_000),
         name="hidden",
-    )(core, parts)
-
-
-def down_kernel(core_ref, own_ref, other_ref, w_ref, out_ref):
-    core = core_ref[0]
-    mine = pl.ds(pl.multiple_of(core * 640, LANES), 512)
-    theirs = pl.ds(pl.multiple_of((1 - core) * 640, LANES), 512)
-    total = dot(own_ref[:, :512], w_ref[mine, :]) + dot(other_ref[:, :512], w_ref[theirs, :])
-    total = total + dot(own_ref[:, 512:] + other_ref[:, 512:], w_ref[512:640, :])
-    out_ref[...] = total.astype(BF16)
-
-
-def down(core, own, other, w_down):
-    return pl.pallas_call(
-        down_kernel,
-        in_specs=[smem()] + whole(3),
-        out_specs=whole(1)[0],
-        out_shape=jax.ShapeDtypeStruct((512, w_down.shape[1]), BF16),
-        compiler_params=params(16),
-        cost_estimate=cost(550_000_000, 3_500_000),
-        name="down",
-    )(core, own, other, w_down)
+    )(stay, above, below)
+
+
+def down_kernel(turn, core_ref, units_ref, w_ref, *rest):
+    core = core_ref[0] if turn == 0 else 1 - core_ref[0]
+    low = core == 0
+    rows = pl.ds(pl.multiple_of(core * 640, LANES), 512)
+    blocks = [units_ref[:, j * 64 : (j + 1) * 64].reshape(512, LANES) for j in range(4)]
+    total = dot(jnp.concatenate(blocks, axis=1), w_ref[:, rows], ((1,), (1,)))
+    packed = units_ref[:, 256:288].astype(F32).reshape(256, LANES)
+    turned = pltpu.roll(packed, 64, 1)
+    lane = iota(packed.shape, 1)
+    begin = jnp.where(low, 0, 64)
+    here = (lane >= begin) & (lane < begin + 64)
+    top = jnp.where(here, jnp.where(low, packed, turned), 0.0).reshape(8, 32, LANES)
+    bottom = jnp.where(here, jnp.where(low, turned, packed), 0.0).reshape(8, 32, LANES)
+    mixed = jnp.concatenate([top, bottom], axis=1).reshape(512, LANES).astype(BF16)
+    total = total + dot(mixed, w_ref[:, 512:640], ((1,), (1,)))
+    if turn == 1:
+        total = total + rest[0][...]
+    rest[-1][...] = total.astype(rest[-1].dtype)
+
+
+def down(core, units, w_down, before=None):
+    turn = 0 if before is None else 1
+    return pl.pallas_call(
+        functools.partial(down_kernel, turn),
+        in_specs=[smem()] + whole(2 + turn),
+        out_specs=whole(1)[0],
+        out_shape=jax.ShapeDtypeStruct((512, w_down.shape[0]), BF16 if turn else F32),
+        compiler_params=params(16),
+        cost_estimate=cost(280_000_000, 2_000_000),
+        name="down" + "ab"[turn],
+    )(core, units, w_down, *([before] if turn else []))
 
 
 def last_kernel(parts_ref, mid_ref, out_ref):
@@ -314,6 +420,10 @@
 
 def swap(x):
     return lax.ppermute(x, "core", [(0, 1), (1, 0)])
+
+
+def shift(x, far):
+    return lax.ppermute(x, "z", [(i, (i + far) % 8) for i in range(8)])
 
 
 def body(
@@ -332,20 +442,27 @@
 ):
     core = lax.axis_index("core").astype(jnp.int32).reshape(1)
     place = lax.axis_index(HID).astype(jnp.int32).reshape(1)
+    height = lax.axis_index("z").astype(jnp.int32).reshape(1)
     gate_other = swap(w_gate)
     up_other = swap(w_up)
 
-    context = attend(indices[:, None, :], q_latent, q_rope, latent_cache, rope_cache)
+    context = attend(indices, q_latent, q_rope, latent_cache, rope_cache)
     moved = exchange(context.reshape(32, 8, LAT), LAYER).reshape(256, LAT)
     flat = exchange(heads(core, moved, w_uv), "z").reshape(512, 512)
-    partial = project(core, flat, swap(flat), w_out)
+    other = swap(flat)
+    partial = project(core, other, w_out.T, project(core, flat, w_out.T))
     parts = exchange(partial.reshape(16, 32, -1), HID)
     mid, scaled = middle(place, parts, residual, norm_gain[None, :])
     scaled = exchange(scaled, HID).reshape(512, 512)
-    wide = widen(core, scaled, swap(scaled), w_gate, gate_other, w_up, up_other)
-    hidden = make_hidden(core, exchange(wide, "z"))
-    hidden = exchange(hidden, "z").reshape(512, 640)
-    outer = down(core, hidden, swap(hidden), w_down)
+    scaled_other = swap(scaled)
+    part = first(core, scaled, w_gate, w_up)
+    rest = (core, height, part, scaled, scaled_other, gate_other, up_other)
+    from_above = shift(widen(TO_LOWER, BF16, *rest), 7)
+    from_below = shift(widen(TO_UPPER, BF16, *rest), 1)
+    stay, lower, upper = merge(widen(TO_KEEP, F32, *rest), from_above, from_below)
+    hidden = exchange(make_hidden(stay, shift(lower, 5), shift(upper, 3)), "z")
+    other = swap(hidden)
+    outer = down(core, other, w_down.T, down(core, hidden, w_down.T))
     return last(exchange(outer.reshape(16, 32, -1), HID), mid)
 
 

time: 174 us -> 158 us (0.908)
  blocking collectives: 110 us -> 71.8 us
  waiting for transfers between devices: 19.3 us -> 37.9 us
  starting transfers between devices: 19.8 us -> 27.7 us
  local copies, waits for them, and re-layouts: 9.94 us -> 2.46 us
  Pallas kernels: 14.1 us -> 17.3 us
    all_to_all x5 -> x4, blocking collectives: 110 us -> 71.8 us  [exchange(): return lax.all_to_all(x, axes, split_axis=0, concat_axis=0, tiled=True)]
    ppermute x0 -> x4, waiting for transfers between devices: none -> 18.9 us  [shift(): return lax.ppermute(x, 'z', [(i, (i + far) % 8) for i in range(8)])]
    unnamed x21 -> x11, local copies, waits for them, and re-layouts: 9.21 us -> 2.46 us
    ppermute x0 -> x4, starting transfers between devices: none -> 4.94 us  [shift(): return lax.ppermute(x, 'z', [(i, (i + far) % 8) for i in range(8)])]
    pallas_call x5 -> x11, Pallas kernels: 12.8 us -> 16 us  [the longest x1 8.83 us: attend(): pl.pallas_call(attend_kernel, grid=(2,), in_specs=[pl.BlockSpec(idx.shape...]
    ppermute x5, starting transfers between devices: 7.47 us -> 10.4 us  [swap(): return lax.ppermute(x, 'core', [(0, 1), (1, 0)])]
  transfers between devices with their start and end apart: 7 -> 11, of which waited for: 4 -> 8; matrix products, arithmetic and copies ran while one was open for 2% -> 1% of each run, Pallas kernels for 0% -> 3%
where the time goes in v2:
time: 158 us; the launch traced here: 157 us
  blocking collectives  71.8 us (45%)
  waiting for transfers between devices  37.9 us (24%)
  starting transfers between devices  27.7 us (18%)
  Pallas kernels  17.3 us (11%)
  local copies, waits for them, and re-layouts  2.46 us (2%)
    all_to_all x4, blocking collectives, exchange(): return lax.all_to_all(x, axes, split_axis=0, concat_axis=0, tiled=True)  71.8 us
    ppermute x4, waiting for transfers between devices, shift(): return lax.ppermute(x, 'z', [(i, (i + far) % 8) for i in range(8)])  18.9 us
    all_to_all x2, waiting for transfers between devices, exchange(): return lax.all_to_all(x, axes, split_axis=0, concat_axis=0, tiled=True)  16.9 us
    all_to_all x2, starting transfers between devices, exchange(): return lax.all_to_all(x, axes, split_axis=0, concat_axis=0, tiled=True)  12.4 us
    ppermute x5, starting transfers between devices, swap(): return lax.ppermute(x, 'core', [(0, 1), (1, 0)])  10.4 us
    pallas_call x1, Pallas kernels, attend(): pl.pallas_call(attend_kernel, grid=(2,), in_specs=[pl.BlockSpec(idx.shape...  8.83 us
    ppermute x4, starting transfers between devices, shift(): return lax.ppermute(x, 'z', [(i, (i + far) % 8) for i in range(8)])  4.94 us
  transfers between devices with their start and end apart: 11, of which 8 were waited for; matrix products, arithmetic and copies ran while one was open for 1% of the time, Pallas kernels for 3%

profile of v2, /device:TPU:1, one launch (start us, length us, event | category | flops | bytes accessed | tf_op | source)
XLA Modules:
  0.0 157.3 jit_solution(11571219900368993193)
XLA Ops:
  0.0 0.0 copy-start.2
  0.0 8.8 %attend.1 = bf16[256,512]{1,0:T(8,128)(2,1)} custom-call(s32[2,2048]{1,0:T(2,128)} %idx_ref.1, bf16[2,128,512]{2,1,0:T(8,128)(2,1)} %ql_ref.1, bf16[2,64,128]{2,1,0:T(8,128)(2,1)} %qr_ref.1, bf16[2,3072,512]{2,1,0:T(8,128)(2,1)} %lat_ref.1, bf16[2,64,3072]{2,1,0:T(8,128)(2,1)} %rope_ref.1), custom_call_target="tpu_custom_call" | custom-call | flops 1800000000 | bytes 8000000 | tf_op jit(solution)/shard_map/attend/pallas_call | solution.py:92
  8.8 8.7 %all-to-all-start = ((bf16[32,8,512]{2,1,0:T(8,128)(2,1)}), bf16[32,8,512]{2,1,0:T(8,128)(2,1)S(1)}, u32[]{:S(2)}, u32[]{:S(2)}) async-start(bf16[32,8,512]{2,1,0:T(8,128)(2,1)} %bitcast.24), calls=%async_computation | async-start | bytes 524288 | tf_op jit(solution)/shard_map/all_to_all | solution.py:418
  17.6 8.3 %all-to-all-done = bf16[32,8,512]{2,1,0:T(8,128)(2,1)S(1)} async-done(((bf16[32,8,512]{2,1,0:T(8,128)(2,1)}), bf16[32,8,512]{2,1,0:T(8,128)(2,1)S(1)}, u32[]{:S(2)}, u32[]{:S(2)}) %all-to-all-start) | async-done | bytes 262176 | tf_op jit(solution)/shard_map/all_to_all | solution.py:418
  25.9 0.0 copy-done.2
  25.9 0.4 heads.1
  26.2 23.4 %all_to_all.30 = bf16[8,64,512]{2,1,0:T(8,128)(2,1)S(1)} all-to-all(bf16[8,64,512]{2,1,0:T(8,128)(2,1)S(1)} %heads.1), channel_id=1, replica_groups=mesh['z'=8,'core'=2,'y'=4,'x'=4] {'z'}, dimensions={0} | all-to-all | bytes 1048576 | tf_op jit(solution)/shard_map/all_to_all | solution.py:418
  49.7 3.0 %collective-permute-start = (bf16[512,512]{1,0:T(8,128)(2,1)S(1)}, bf16[512,512]{1,0:T(8,128)(2,1)S(1)}, u32[]{:S(2)}, u32[]{:S(2)}) collective-permute-start(bf16[512,512]{1,0:T(8,128)(2,1)S(1)} %bitcast.20), channel_id=1, source_target_pairs={{0,16},{16,0},{1,17},{17,1},{2,18},{18,2},{3,19},{19,3},{4,20},{20... | collective-permute-start | bytes 1572872 | tf_op jit(solution)/shard_map/ppermute | solution.py:422
  52.7 0.0 copy-done.1
  52.7 0.5 projecta.1.rest_0_
  53.1 1.1 collective-permute-done.heads_ref
  54.2 1.3 projectb.1
  55.5 3.6 %all-to-all-start.2 = ((bf16[16,32,448]{2,1,0:T(8,128)(2,1)}), bf16[16,32,448]{2,1,0:T(8,128)(2,1)S(1)}, u32[]{:S(2)}, u32[]{:S(2)}) async-start(bf16[16,32,448]{2,1,0:T(8,128)(2,1)} %bitcast.7), calls=%async_computation.2 | async-start | bytes 1048576 | tf_op jit(solution)/shard_map/all_to_all | solution.py:418
  59.1 0.7 collective-permute-start.2
  59.9 0.1 collective-permute-start.3
  60.0 0.0 copy-done.4
  60.0 1.2 copy.13.res_ref
  61.2 8.6 %all-to-all-done.2.parts_ref = bf16[16,32,448]{2,1,0:T(8,128)(2,1)S(1)} async-done(((bf16[16,32,448]{2,1,0:T(8,128)(2,1)}), bf16[16,32,448]{2,1,0:T(8,128)(2,1)S(1)}, u32[]{:S(2)}, u32[]{:S(2)}) %all-to-all-start.2) | async-done | bytes 458784 | tf_op jit(solution)/shard_map/all_to_all | solution.py:418
  69.8 0.3 middle.1
  70.1 13.4 %all_to_all.31 = bf16[16,32,512]{2,1,0:T(8,128)(2,1)S(1)} all-to-all(bf16[16,32,512]{2,1,0:T(8,128)(2,1)S(1)} %get-tuple-element.10), channel_id=1, replica_groups=mesh['z'=8,'core'=2,'y'=4,'x'=4] {'y','x'}, dimensions={0} | all-to-all | bytes 1048576 | tf_op jit(solution)/shard_map/all_to_all | solution.py:418
  83.5 2.3 %collective-permute-start.1 = (bf16[512,512]{1,0:T(8,128)(2,1)S(1)}, bf16[512,512]{1,0:T(8,128)(2,1)S(1)}, u32[]{:S(2)}, u32[]{:S(2)}) collective-permute-start(bf16[512,512]{1,0:T(8,128)(2,1)S(1)} %bitcast.11), channel_id=1, source_target_pairs={{0,16},{16,0},{1,17},{17,1},{2,18},{18,2},{3,19},{19,3},{4,20},{20... | collective-permute-start | bytes 1572872 | tf_op jit(solution)/shard_map/ppermute | solution.py:422
  85.9 1.2 copy-done.3
  87.1 2.2 %first.1.part_ref = f32[512,1280]{1,0:T(8,128)S(1)} custom-call(s32[1]{0:T(128)} %bitcast.core_ref, bf16[512,512]{1,0:T(8,128)(2,1)S(1)} %bitcast.12, bf16[448,1152]{1,0:T(8,128)(2,1)} %g_ref.1, bf16[448,1152]{1,0:T(8,128)(2,1)S(1)} %copy-done.3), custom_call_target="tpu_custom_call" | custom-call | flops 560000000 | bytes 5000000 | tf_op jit(solution)/shard_map/first/pallas_call | solution.py:203
  89.3 0.0 collective-permute-done.2.g_ref
  89.3 0.0 collective-permute-done.3.u_ref
  89.3 0.0 collective-permute-done.1.other_ref
  89.3 0.5 widen.4
  89.8 0.1 collective-permute-start.4
  89.9 0.5 widen.5
  90.5 0.0 copy-start
  90.5 1.5 collective-permute-start.5
  92.0 0.6 widen.3.keep_ref
  92.6 7.8 %collective-permute-done.4.above_ref = bf16[1488,128]{1,0:T(8,128)(2,1)S(1)} collective-permute-done((bf16[1488,128]{1,0:T(8,128)(2,1)S(1)}, bf16[1488,128]{1,0:T(8,128)(2,1)S(1)}, u32[]{:S(2)}, u32[]{:S(2)}) %collective-permute-start.4) | collective-permute-done | bytes 380960 | tf_op jit(solution)/shard_map/ppermute | solution.py:426
  100.4 1.8 %collective-permute-done.5.below_ref = bf16[1488,128]{1,0:T(8,128)(2,1)S(1)} collective-permute-done((bf16[1488,128]{1,0:T(8,128)(2,1)S(1)}, bf16[1488,128]{1,0:T(8,128)(2,1)S(1)}, u32[]{:S(2)}, u32[]{:S(2)}) %collective-permute-start.5) | collective-permute-done | bytes 380960 | tf_op jit(solution)/shard_map/ppermute | solution.py:426
  102.3 0.1 merge.1
  102.4 0.1 collective-permute-start.6
  102.5 3.3 %collective-permute-start.7 = (bf16[592,128]{1,0:T(8,128)(2,1)S(1)}, bf16[592,128]{1,0:T(8,128)(2,1)S(1)}, u32[]{:S(2)}, u32[]{:S(2)}) collective-permute-start(bf16[592,128]{1,0:T(8,128)(2,1)S(1)} %get-tuple-element.13), channel_id=1, source_target_pairs={{0,96},{32,128},{64,160},{96,192},{128,224},{160,0},{192,32},{224,... | collective-permute-start | bytes 454664 | tf_op jit(solution)/shard_map/ppermute | solution.py:426
  105.7 3.6 %collective-permute-done.6.above_ref = bf16[592,128]{1,0:T(8,128)(2,1)S(1)} collective-permute-done((bf16[592,128]{1,0:T(8,128)(2,1)S(1)}, bf16[592,128]{1,0:T(8,128)(2,1)S(1)}, u32[]{:S(2)}, u32[]{:S(2)}) %collective-permute-start.6) | collective-permute-done | bytes 151584 | tf_op jit(solution)/shard_map/ppermute | solution.py:426
  109.3 5.6 %collective-permute-done.7.below_ref = bf16[592,128]{1,0:T(8,128)(2,1)S(1)} collective-permute-done((bf16[592,128]{1,0:T(8,128)(2,1)S(1)}, bf16[592,128]{1,0:T(8,128)(2,1)S(1)}, u32[]{:S(2)}, u32[]{:S(2)}) %collective-permute-start.7) | collective-permute-done | bytes 151584 | tf_op jit(solution)/shard_map/ppermute | solution.py:426
  114.9 0.3 hidden.1
  115.2 20.4 %all_to_all.32.units_ref = bf16[8,288,128]{2,1,0:T(8,128)(2,1)S(1)} all-to-all(bf16[8,288,128]{2,1,0:T(8,128)(2,1)S(1)} %hidden.1), channel_id=1, replica_groups=mesh['z'=8,'core'=2,'y'=4,'x'=4] {'z'}, dimensions={0} | all-to-all | bytes 1179648 | tf_op jit(solution)/shard_map/all_to_all | solution.py:418
  135.7 4.2 %collective-permute-start.8 = (bf16[8,288,128]{2,1,0:T(8,128)(2,1)S(1)}, bf16[8,288,128]{2,1,0:T(8,128)(2,1)S(1)}, u32[]{:S(2)}, u32[]{:S(2)}) collective-permute-start(bf16[8,288,128]{2,1,0:T(8,128)(2,1)S(1)} %all_to_all.32.units_ref), channel_id=1, source_target_pairs={{0,16},{16,0},{1,17},{17,1},{2,18},{18,2},{3,19},{19,3},{4,20},{20... | collective-permute-start | bytes 1769480 | tf_op jit(solution)/shard_map/ppermute | solution.py:422
  139.9 0.0 copy-done
  139.9 0.6 downa.1.rest_0_
  140.5 1.0 collective-permute-done.8.units_ref
  141.5 0.6 downb.1
  142.1 14.5 %all_to_all.33.parts_ref = bf16[16,32,448]{2,1,0:T(8,128)(2,1)S(1)} all-to-all(bf16[16,32,448]{2,1,0:T(8,128)(2,1)S(1)} %bitcast.22), channel_id=1, replica_groups=mesh['z'=8,'core'=2,'y'=4,'x'=4] {'y','x'}, dimensions={0} | all-to-all | bytes 917504 | tf_op jit(solution)/shard_map/all_to_all | solution.py:418
  156.6 0.7 last.1
  (4 shorter events, 0.0 us)
Async XLA Ops:
  0.0 25.9 %copy-start.2 = (bf16[8,512,128]{2,1,0:T(8,128)(2,1)S(1)}, bf16[8,512,128]{2,1,0:T(8,128)(2,1)}, u32[]{:S(2)}) copy-start(bf16[8,512,128]{2,1,0:T(8,128)(2,1)} %w_ref.1) | copy-start | bytes 3145732
  0.0 52.7 %copy-start.1 = (bf16[1024,448]{0,1:T(8,128)(2,1)S(1)}, bf16[1024,448]{0,1:T(8,128)(2,1)}, u32[]{:S(2)}) copy-start(bf16[1024,448]{0,1:T(8,128)(2,1)} %param.18) | copy-start | bytes 2752516
  8.8 51.1 %copy-start.4 = (bf16[448]{0:T(512)(128)(2,1)S(1)}, bf16[448]{0:T(512)(128)(2,1)}, u32[]{:S(2)}) copy-start(bf16[448]{0:T(512)(128)(2,1)} %param.20) | copy-start | bytes 2692
  8.8 17.0 %all-to-all-start = ((bf16[32,8,512]{2,1,0:T(8,128)(2,1)}), bf16[32,8,512]{2,1,0:T(8,128)(2,1)S(1)}, u32[]{:S(2)}, u32[]{:S(2)}) async-start(bf16[32,8,512]{2,1,0:T(8,128)(2,1)} %bitcast.24), calls=%async_computation | async-start | bytes 524288 | tf_op jit(solution)/shard_map/all_to_all | solution.py:418
  49.7 4.5 %collective-permute-start = (bf16[512,512]{1,0:T(8,128)(2,1)S(1)}, bf16[512,512]{1,0:T(8,128)(2,1)S(1)}, u32[]{:S(2)}, u32[]{:S(2)}) collective-permute-start(bf16[512,512]{1,0:T(8,128)(2,1)S(1)} %bitcast.20), channel_id=1, source_target_pairs={{0,16},{16,0},{1,17},{17,1},{2,18},{18,2},{3,19},{19,3},{4,20},{20... | collective-permute-start | bytes 1572872 | tf_op jit(solution)/shard_map/ppermute | solution.py:422
  55.5 14.4 %all-to-all-start.2 = ((bf16[16,32,448]{2,1,0:T(8,128)(2,1)}), bf16[16,32,448]{2,1,0:T(8,128)(2,1)S(1)}, u32[]{:S(2)}, u32[]{:S(2)}) async-start(bf16[16,32,448]{2,1,0:T(8,128)(2,1)} %bitcast.7), calls=%async_computation.2 | async-start | bytes 1048576 | tf_op jit(solution)/shard_map/all_to_all | solution.py:418
  59.1 30.2 %collective-permute-start.2 = (bf16[448,1152]{1,0:T(8,128)(2,1)}, bf16[448,1152]{1,0:T(8,128)(2,1)S(1)}, u32[]{:S(2)}, u32[]{:S(2)}) collective-permute-start(bf16[448,1152]{1,0:T(8,128)(2,1)} %g_ref.1), channel_id=1, source_target_pairs={{0,16},{16,0},{1,17},{17,1},{2,18},{18,2},{3,19},{19,3},{4,20},{20... | collective-permute-start | bytes 3096584 | tf_op jit(solution)/shard_map/ppermute | solution.py:422
  59.9 29.4 %collective-permute-start.3 = (bf16[448,1152]{1,0:T(8,128)(2,1)}, bf16[448,1152]{1,0:T(8,128)(2,1)S(1)}, u32[]{:S(2)}, u32[]{:S(2)}) collective-permute-start(bf16[448,1152]{1,0:T(8,128)(2,1)} %u_ref.1), channel_id=1, source_target_pairs={{0,16},{16,0},{1,17},{17,1},{2,18},{18,2},{3,19},{19,3},{4,20},{20... | collective-permute-start | bytes 3096584 | tf_op jit(solution)/shard_map/ppermute | solution.py:422
  83.5 5.8 %collective-permute-start.1 = (bf16[512,512]{1,0:T(8,128)(2,1)S(1)}, bf16[512,512]{1,0:T(8,128)(2,1)S(1)}, u32[]{:S(2)}, u32[]{:S(2)}) collective-permute-start(bf16[512,512]{1,0:T(8,128)(2,1)S(1)} %bitcast.11), channel_id=1, source_target_pairs={{0,16},{16,0},{1,17},{17,1},{2,18},{18,2},{3,19},{19,3},{4,20},{20... | collective-permute-start | bytes 1572872 | tf_op jit(solution)/shard_map/ppermute | solution.py:422
  85.9 1.2 copy-start.3
  89.8 10.6 %collective-permute-start.4 = (bf16[1488,128]{1,0:T(8,128)(2,1)S(1)}, bf16[1488,128]{1,0:T(8,128)(2,1)S(1)}, u32[]{:S(2)}, u32[]{:S(2)}) collective-permute-start(bf16[1488,128]{1,0:T(8,128)(2,1)S(1)} %widen.4), channel_id=1, source_target_pairs={{0,224},{32,0},{64,32},{96,64},{128,96},{160,128},{192,160},{224,1... | collective-permute-start | bytes 1142792 | tf_op jit(solution)/shard_map/ppermute | solution.py:426
  90.5 49.4 %copy-start = (bf16[1152,448]{0,1:T(8,128)(2,1)S(1)}, bf16[1152,448]{0,1:T(8,128)(2,1)}, u32[]{:S(2)}) copy-start(bf16[1152,448]{0,1:T(8,128)(2,1)} %param.23) | copy-start | bytes 3096580
  90.5 11.8 %collective-permute-start.5 = (bf16[1488,128]{1,0:T(8,128)(2,1)S(1)}, bf16[1488,128]{1,0:T(8,128)(2,1)S(1)}, u32[]{:S(2)}, u32[]{:S(2)}) collective-permute-start(bf16[1488,128]{1,0:T(8,128)(2,1)S(1)} %widen.5), channel_id=1, source_target_pairs={{0,32},{32,64},{64,96},{96,128},{128,160},{160,192},{192,224},{224... | collective-permute-start | bytes 1142792 | tf_op jit(solution)/shard_map/ppermute | solution.py:426
  102.4 6.9 %collective-permute-start.6 = (bf16[592,128]{1,0:T(8,128)(2,1)S(1)}, bf16[592,128]{1,0:T(8,128)(2,1)S(1)}, u32[]{:S(2)}, u32[]{:S(2)}) collective-permute-start(bf16[592,128]{1,0:T(8,128)(2,1)S(1)} %get-tuple-element.12), channel_id=1, source_target_pairs={{0,160},{32,192},{64,224},{96,0},{128,32},{160,64},{192,96},{224,1... | collective-permute-start | bytes 454664 | tf_op jit(solution)/shard_map/ppermute | solution.py:426
  102.5 12.5 %collective-permute-start.7 = (bf16[592,128]{1,0:T(8,128)(2,1)S(1)}, bf16[592,128]{1,0:T(8,128)(2,1)S(1)}, u32[]{:S(2)}, u32[]{:S(2)}) collective-permute-start(bf16[592,128]{1,0:T(8,128)(2,1)S(1)} %get-tuple-element.13), channel_id=1, source_target_pairs={{0,96},{32,128},{64,160},{96,192},{128,224},{160,0},{192,32},{224,... | collective-permute-start | bytes 454664 | tf_op jit(solution)/shard_map/ppermute | solution.py:426
  135.7 5.9 %collective-permute-start.8 = (bf16[8,288,128]{2,1,0:T(8,128)(2,1)S(1)}, bf16[8,288,128]{2,1,0:T(8,128)(2,1)S(1)}, u32[]{:S(2)}, u32[]{:S(2)}) collective-permute-start(bf16[8,288,128]{2,1,0:T(8,128)(2,1)S(1)} %all_to_all.32.units_ref), channel_id=1, source_target_pairs={{0,16},{16,0},{1,17},{17,1},{2,18},{18,2},{3,19},{19,3},{4,20},{20... | collective-permute-start | bytes 1769480 | tf_op jit(solution)/shard_map/ppermute | solution.py:422

commit v3 on v2

--- a/solution.py
+++ b/solution.py
@@ -20,6 +20,7 @@
 HID = ("y", "x")
 LAYER = ("core", "y", "x")
 LANES = 128
+FAR = (0, 1, 7, 2, 6, 3, 5, 4)
 EXP2_SCALE = math.log2(math.e) / math.sqrt(VDIM + ROPE)
 
 
@@ -50,33 +51,32 @@
 def attend_kernel(idx_ref, ql_ref, qr_ref, lat_ref, rope_ref, out_ref, scores, both):
     seq = pl.program_id(0)
     idx = idx_ref[pl.ds(seq, 1), :]
-    groups = CTX // LANES
     high = (iota((32, idx.shape[1]), 0) == lax.shift_right_logical(idx, 7)).astype(F32).astype(BF16)
     low = (iota((LANES, idx.shape[1]), 0) == (idx & 127)).astype(F32).astype(BF16)
-    count = dot(high, low, ((1,), (1,)))
-    bias = jnp.where(count > 0.5, 0.0, -1e30)
+    bias = jnp.where(dot(low, high, ((1,), (1,))) > 0.5, 0.0, -1e30)
 
     q_lat = ql_ref[0]
     q_rope = qr_ref[0]
-    step = 512
-    top = jnp.full((HEADS, LANES), -3e38, F32)
+    step = 1024
+    top = jnp.full((8, HEADS), -3e38, F32)
     for at in range(0, CTX, step):
-        part = dot(q_lat, lat_ref[0, at : at + step, :], ((1,), (1,)))
-        part = part + dot(q_rope, rope_ref[0, :, at : at + step], ((0,), (0,)))
+        part = dot(lat_ref[0, at : at + step, :], q_lat, ((1,), (1,)))
+        part = part + dot(rope_ref[0, :, at : at + step], q_rope, ((0,), (0,)))
         for j in range(step // LANES):
             g = at // LANES + j
-            piece = part[:, j * LANES : (j + 1) * LANES] + bias[g : g + 1, :]
-            scores[:, g * LANES : (g + 1) * LANES] = piece
-            top = jnp.maximum(top, piece)
-    peak = jnp.max(top, axis=1, keepdims=True)
-    total = jnp.zeros((HEADS, LANES), F32)
+            piece = part[j * LANES : (j + 1) * LANES] + bias[:, g : g + 1]
+            scores[g * LANES : (g + 1) * LANES, :] = piece
+            top = jnp.maximum(top, jnp.max(piece.reshape(16, 8, HEADS), axis=0))
+    peak = jnp.max(top, axis=0, keepdims=True)
+    total = jnp.zeros((8, HEADS), F32)
     acc = jnp.zeros((HEADS, LAT), F32)
     for at in range(0, CTX, step):
-        e = jnp.exp2((scores[:, at : at + step] - peak) * EXP2_SCALE)
-        for j in range(step // LANES):
-            total = total + e[:, j * LANES : (j + 1) * LANES]
-        acc = acc + dot(e.astype(BF16), lat_ref[0, at : at + step, :])
-    norm = jnp.sum(total, axis=1, keepdims=True)
+        e = jnp.exp2((scores[at : at + step, :] - peak) * EXP2_SCALE)
+        total = total + jnp.sum(e.reshape(step // 8, 8, HEADS), axis=0)
+        acc = acc + dot(e.astype(BF16), lat_ref[0, at : at + step, :], ((0,), (0,)))
+    norm = jnp.sum(total, axis=0, keepdims=True)
+    same = iota((HEADS, HEADS), 0) == iota((HEADS, HEADS), 1)
+    norm = jnp.sum(jnp.where(same, norm, 0.0), axis=1, keepdims=True)
     both[pl.ds(pl.multiple_of(seq * HEADS, HEADS), HEADS), :] = (acc / norm).astype(BF16)
 
     @pl.when(seq == 1)
@@ -101,7 +101,7 @@
         ],
         out_specs=pl.BlockSpec((256, LAT), lambda s: (0, 0)),
         out_shape=jax.ShapeDtypeStruct((256, LAT), BF16),
-        scratch_shapes=[pltpu.VMEM((HEADS, CTX), F32), pltpu.VMEM((256, LAT), BF16)],
+        scratch_shapes=[pltpu.VMEM((CTX, HEADS), F32), pltpu.VMEM((256, LAT), BF16)],
         compiler_params=params(58),
         cost_estimate=cost(1_800_000_000, 8_000_000),
         name="attend",
@@ -116,8 +116,7 @@
     sorted_rows = dot(pick, x_ref[...]).astype(BF16)
     for i in range(4):
         part = dot(sorted_rows[i * 64 : (i + 1) * 64], w_ref[core * 4 + i]).astype(BF16)
-        for k in range(8):
-            out_ref[k, :, i * VDIM : (i + 1) * VDIM] = part
+        out_ref[:, i * VDIM : (i + 1) * VDIM] = part
 
 
 def heads(core, x, w_uv):
@@ -125,33 +124,59 @@
         heads_kernel,
         in_specs=[smem()] + whole(2),
         out_specs=whole(1)[0],
-        out_shape=jax.ShapeDtypeStruct((8, 64, 512), BF16),
+        out_shape=jax.ShapeDtypeStruct((64, 512), BF16),
         compiler_params=params(16),
         cost_estimate=cost(100_000_000, 2_000_000),
         name="heads",
     )(core, x, w_uv)
 
 
-def project_kernel(turn, core_ref, heads_ref, w_ref, *rest):
+def pack_kernel(*refs):
+    rows = refs[0].shape[0]
+    for k, ref in enumerate(refs[:-1]):
+        refs[-1][k * rows : (k + 1) * rows] = ref[...]
+
+
+def pack(blocks):
+    rows, columns = blocks[0].shape
+    return pl.pallas_call(
+        pack_kernel,
+        in_specs=whole(8),
+        out_specs=whole(1)[0],
+        out_shape=jax.ShapeDtypeStruct((8 * rows, columns), BF16),
+        compiler_params=params(16),
+        cost_estimate=cost(0, 1_000_000),
+        name="pack",
+    )(*blocks)
+
+
+def place_chunks(out_ref, z, value):
+    for k, far in enumerate(FAR):
+        at = pl.multiple_of(lax.rem(z + far, 8) * 64, 64)
+        out_ref[pl.ds(at, 64), :] = value[k * 64 : (k + 1) * 64].astype(out_ref.dtype)
+
+
+def project_kernel(turn, core_ref, z_ref, heads_ref, w_ref, *rest):
     half = core_ref[0] if turn == 0 else 1 - core_ref[0]
     rows = pl.ds(pl.multiple_of(half * 512, 512), 512)
     total = dot(heads_ref[...], w_ref[:, rows], ((1,), (1,)))
     if turn == 1:
-        total = total + rest[0][...]
-    rest[-1][...] = total.astype(rest[-1].dtype)
-
-
-def project(core, own, w_out, before=None):
+        place_chunks(rest[1], z_ref[0], total + rest[0][...])
+    else:
+        rest[0][...] = total
+
+
+def project(core, z, own, w_out, before=None):
     turn = 0 if before is None else 1
     return pl.pallas_call(
         functools.partial(project_kernel, turn),
-        in_specs=[smem()] + whole(2 + turn),
+        in_specs=[smem(), smem()] + whole(2 + turn),
         out_specs=whole(1)[0],
         out_shape=jax.ShapeDtypeStruct((512, w_out.shape[0]), BF16 if turn else F32),
         compiler_params=params(16),
         cost_estimate=cost(240_000_000, 2_000_000),
         name="project" + "ab"[turn],
-    )(core, own, w_out, *([before] if turn else []))
+    )(core, z, own, w_out, *([before] if turn else []))
 
 
 def middle_kernel(place_ref, parts_ref, res_ref, gain_ref, mid_ref, out_ref):
@@ -337,9 +362,7 @@
     rstd = lax.rsqrt(squares / D + 1e-06)
 
     def put(at, value):
-        value = value.astype(BF16)
-        for k in range(out_ref.shape[0]):
-            out_ref[k, at : at + value.shape[0]] = value
+        out_ref[at : at + value.shape[0]] = value.astype(BF16)
 
     for j in range(4):
         gate = total(j * chunk, chunk) * rstd
@@ -355,14 +378,14 @@
         hidden_kernel,
         in_specs=whole(3),
         out_specs=whole(1)[0],
-        out_shape=jax.ShapeDtypeStruct((8, 288, LANES), BF16),
+        out_shape=jax.ShapeDtypeStruct((288, LANES), BF16),
         compiler_params=params(16),
         cost_estimate=cost(5_000_000, 2_000_000),
         name="hidden",
     )(stay, above, below)
 
 
-def down_kernel(turn, core_ref, units_ref, w_ref, *rest):
+def down_kernel(turn, core_ref, z_ref, units_ref, w_ref, *rest):
     core = core_ref[0] if turn == 0 else 1 - core_ref[0]
     low = core == 0
     rows = pl.ds(pl.multiple_of(core * 640, LANES), 512)
@@ -378,21 +401,22 @@
     mixed = jnp.concatenate([top, bottom], axis=1).reshape(512, LANES).astype(BF16)
     total = total + dot(mixed, w_ref[:, 512:640], ((1,), (1,)))
     if turn == 1:
-        total = total + rest[0][...]
-    rest[-1][...] = total.astype(rest[-1].dtype)
-
-
-def down(core, units, w_down, before=None):
+        place_chunks(rest[1], z_ref[0], total + rest[0][...])
+    else:
+        rest[0][...] = total
+
+
+def down(core, z, units, w_down, before=None):
     turn = 0 if before is None else 1
     return pl.pallas_call(
         functools.partial(down_kernel, turn),
-        in_specs=[smem()] + whole(2 + turn),
+        in_specs=[smem(), smem()] + whole(2 + turn),
         out_specs=whole(1)[0],
         out_shape=jax.ShapeDtypeStruct((512, w_down.shape[0]), BF16 if turn else F32),
         compiler_params=params(16),
         cost_estimate=cost(280_000_000, 2_000_000),
         name="down" + "ab"[turn],
-    )(core, units, w_down, *([before] if turn else []))
+    )(core, z, units, w_down, *([before] if turn else []))
 
 
 def last_kernel(parts_ref, mid_ref, out_ref):
@@ -424,6 +448,16 @@
 
 def shift(x, far):
     return lax.ppermute(x, "z", [(i, (i + far) % 8) for i in range(8)])
+
+
+def gather(x):
+    one_above, one_below = shift(x, 7), shift(x, 1)
+    two_above, two_below = shift(x, 6), shift(x, 2)
+    three_above, three_below = shift(two_above, 7), shift(two_below, 1)
+    opposite = shift(two_above, 6)
+    return pack(
+        [x, one_above, one_below, two_above, two_below, three_above, three_below, opposite]
+    )
 
 
 def body(
@@ -448,9 +482,10 @@
 
     context = attend(indices, q_latent, q_rope, latent_cache, rope_cache)
     moved = exchange(context.reshape(32, 8, LAT), LAYER).reshape(256, LAT)
-    flat = exchange(heads(core, moved, w_uv), "z").reshape(512, 512)
+    flat = gather(heads(core, moved, w_uv))
     other = swap(flat)
-    partial = project(core, other, w_out.T, project(core, flat, w_out.T))
+    part = project(core, height, flat, w_out.T)
+    partial = project(core, height, other, w_out.T, part)
     parts = exchange(partial.reshape(16, 32, -1), HID)
     mid, scaled = middle(place, parts, residual, norm_gain[None, :])
     scaled = exchange(scaled, HID).reshape(512, 512)
@@ -460,9 +495,10 @@
     from_above = shift(widen(TO_LOWER, BF16, *rest), 7)
     from_below = shift(widen(TO_UPPER, BF16, *rest), 1)
     stay, lower, upper = merge(widen(TO_KEEP, F32, *rest), from_above, from_below)
-    hidden = exchange(make_hidden(stay, shift(lower, 5), shift(upper, 3)), "z")
-    other = swap(hidden)
-    outer = down(core, other, w_down.T, down(core, hidden, w_down.T))
+    hidden = gather(make_hidden(stay, shift(lower, 5), shift(upper, 3)))
+    other = swap(hidden).reshape(8, 288, LANES)
+    part = down(core, height, hidden.reshape(8, 288, LANES), w_down.T)
+    outer = down(core, height, other, w_down.T, part)
     return last(exchange(outer.reshape(16, 32, -1), HID), mid)
 
 

time: 158 us -> 146 us (0.924)
  blocking collectives: 71.8 us -> 26.8 us
  starting transfers between devices: 27.7 us -> 53 us
  waiting for transfers between devices: 37.9 us -> 47.3 us
  Pallas kernels: 17.3 us -> 14.8 us
    all_to_all x4 -> x2, blocking collectives: 71.8 us -> 26.8 us  [exchange(): return lax.all_to_all(x, axes, split_axis=0, concat_axis=0, tiled=True)]
    ppermute x4 -> x18, starting transfers between devices: 4.94 us -> 29.3 us  [shift(): return lax.ppermute(x, 'z', [(i, (i + far) % 8) for i in range(8)])]
    ppermute x4 -> x18, waiting for transfers between devices: 18.9 us -> 28.3 us  [shift(): return lax.ppermute(x, 'z', [(i, (i + far) % 8) for i in range(8)])]
    unnamed x11 -> x13, local copies, waits for them, and re-layouts: 2.46 us -> 3.68 us
  transfers between devices with their start and end apart: 11 -> 25, of which waited for: 8 -> 13; matrix products, arithmetic and copies ran while one was open for 1% -> 1% of each run, Pallas kernels for 3% -> 2%
where the time goes in v3:
time: 146 us
  starting transfers between devices  53 us (36%)
  waiting for transfers between devices  47.3 us (32%)
  blocking collectives  26.8 us (18%)
  Pallas kernels  14.8 us (10%)
  local copies, waits for them, and re-layouts  3.68 us (3%)
    ppermute x18, starting transfers between devices, shift(): return lax.ppermute(x, 'z', [(i, (i + far) % 8) for i in range(8)])  29.3 us
    ppermute x18, waiting for transfers between devices, shift(): return lax.ppermute(x, 'z', [(i, (i + far) % 8) for i in range(8)])  28.3 us
    all_to_all x2, blocking collectives, exchange(): return lax.all_to_all(x, axes, split_axis=0, concat_axis=0, tiled=True)  26.8 us
    all_to_all x2, waiting for transfers between devices, exchange(): return lax.all_to_all(x, axes, split_axis=0, concat_axis=0, tiled=True)  16.9 us
    all_to_all x2, starting transfers between devices, exchange(): return lax.all_to_all(x, axes, split_axis=0, concat_axis=0, tiled=True)  12.3 us
    ppermute x5, starting transfers between devices, swap(): return lax.ppermute(x, 'core', [(0, 1), (1, 0)])  11.4 us
    pallas_call x1, Pallas kernels, attend(): pl.pallas_call(attend_kernel, grid=(2,), in_specs=[pl.BlockSpec(idx.shape...  7.43 us
    unnamed x13, local copies, waits for them, and re-layouts  3.68 us
  transfers between devices with their start and end apart: 25, of which 13 were waited for; matrix products, arithmetic and copies ran while one was open for 1% of the time, Pallas kernels for 2%

profile of v3, /device:TPU:1, one launch (start us, length us, event | category | flops | bytes accessed | tf_op | source)
XLA Modules:
  0.0 145.8 jit_solution(9705386705532341961)
XLA Ops:
  0.0 7.4 %attend.1 = bf16[256,512]{1,0:T(8,128)(2,1)} custom-call(s32[2,2048]{1,0:T(2,128)} %idx_ref.1, bf16[2,128,512]{2,1,0:T(8,128)(2,1)} %ql_ref.1, bf16[2,64,128]{2,1,0:T(8,128)(2,1)} %qr_ref.1, bf16[2,3072,512]{2,1,0:T(8,128)(2,1)} %lat_ref.1, bf16[2,64,3072]{2,1,0:T(8,128)(2,1)} %rope_ref.1), custom_call_target="tpu_custom_call" | custom-call | flops 1800000000 | bytes 8000000 | tf_op jit(solution)/shard_map/attend/pallas_call | solution.py:92
  7.4 8.7 %all-to-all-start = ((bf16[32,8,512]{2,1,0:T(8,128)(2,1)}), bf16[32,8,512]{2,1,0:T(8,128)(2,1)S(1)}, u32[]{:S(2)}, u32[]{:S(2)}) async-start(bf16[32,8,512]{2,1,0:T(8,128)(2,1)} %bitcast.25), calls=%async_computation | async-start | bytes 524288 | tf_op jit(solution)/shard_map/all_to_all | solution.py:442
  16.2 8.3 %all-to-all-done = bf16[32,8,512]{2,1,0:T(8,128)(2,1)S(1)} async-done(((bf16[32,8,512]{2,1,0:T(8,128)(2,1)}), bf16[32,8,512]{2,1,0:T(8,128)(2,1)S(1)}, u32[]{:S(2)}, u32[]{:S(2)}) %all-to-all-start) | async-done | bytes 262176 | tf_op jit(solution)/shard_map/all_to_all | solution.py:442
  24.8 3.1 %collective-permute-start.3 = (bf16[64,512]{1,0:T(8,128)(2,1)S(1)}, bf16[64,512]{1,0:T(8,128)(2,1)S(1)}, u32[]{:S(2)}, u32[]{:S(2)}) collective-permute-start(bf16[64,512]{1,0:T(8,128)(2,1)S(1)} %heads.1.refs_0_), channel_id=1, source_target_pairs={{0,64},{32,96},{64,128},{96,160},{128,192},{160,224},{192,0},{224,... | collective-permute-start | bytes 196616 | tf_op jit(solution)/shard_map/ppermute | solution.py:450
  27.9 3.1 %collective-permute-start.2 = (bf16[64,512]{1,0:T(8,128)(2,1)S(1)}, bf16[64,512]{1,0:T(8,128)(2,1)S(1)}, u32[]{:S(2)}, u32[]{:S(2)}) collective-permute-start(bf16[64,512]{1,0:T(8,128)(2,1)S(1)} %heads.1.refs_0_), channel_id=1, source_target_pairs={{0,192},{32,224},{64,0},{96,32},{128,64},{160,96},{192,128},{224,1... | collective-permute-start | bytes 196616 | tf_op jit(solution)/shard_map/ppermute | solution.py:450
  31.0 0.7 collective-permute-start.1
  31.8 1.9 %collective-permute-start = (bf16[64,512]{1,0:T(8,128)(2,1)S(1)}, bf16[64,512]{1,0:T(8,128)(2,1)S(1)}, u32[]{:S(2)}, u32[]{:S(2)}) collective-permute-start(bf16[64,512]{1,0:T(8,128)(2,1)S(1)} %heads.1.refs_0_), channel_id=1, source_target_pairs={{0,224},{32,0},{64,32},{96,64},{128,96},{160,128},{192,160},{224,1... | collective-permute-start | bytes 196616 | tf_op jit(solution)/shard_map/ppermute | solution.py:450
  33.7 0.7 collective-permute-start.5
  34.7 2.0 %collective-permute-start.6 = (bf16[64,512]{1,0:T(8,128)(2,1)S(1)}, bf16[64,512]{1,0:T(8,128)(2,1)S(1)}, u32[]{:S(2)}, u32[]{:S(2)}) collective-permute-start(bf16[64,512]{1,0:T(8,128)(2,1)S(1)} %collective-permute-done.2.refs_3_), channel_id=1, source_target_pairs={{0,192},{32,224},{64,0},{96,32},{128,64},{160,96},{192,128},{224,1... | collective-permute-start | bytes 196616 | tf_op jit(solution)/shard_map/ppermute | solution.py:450
  36.7 0.7 collective-permute-start.4
  37.4 0.6 collective-permute-done.5.refs_6_
  38.0 2.7 %collective-permute-done.6.refs_7_ = bf16[64,512]{1,0:T(8,128)(2,1)S(1)} collective-permute-done((bf16[64,512]{1,0:T(8,128)(2,1)S(1)}, bf16[64,512]{1,0:T(8,128)(2,1)S(1)}, u32[]{:S(2)}, u32[]{:S(2)}) %collective-permute-start.6) | collective-permute-done | bytes 65568 | tf_op jit(solution)/shard_map/ppermute | solution.py:450
  40.8 3.4 %collective-permute-start.7 = (bf16[512,512]{1,0:T(8,128)(2,1)S(1)}, bf16[512,512]{1,0:T(8,128)(2,1)S(1)}, u32[]{:S(2)}, u32[]{:S(2)}) collective-permute-start(bf16[512,512]{1,0:T(8,128)(2,1)S(1)} %pack.2.heads_ref), channel_id=1, source_target_pairs={{0,16},{16,0},{1,17},{17,1},{2,18},{18,2},{3,19},{19,3},{4,20},{20... | collective-permute-start | bytes 1572872 | tf_op jit(solution)/shard_map/ppermute | solution.py:446
  44.6 1.1 collective-permute-done.7.heads_ref
  45.7 1.3 projectb.1
  46.9 3.6 %all-to-all-start.1 = ((bf16[16,32,448]{2,1,0:T(8,128)(2,1)}), bf16[16,32,448]{2,1,0:T(8,128)(2,1)S(1)}, u32[]{:S(2)}, u32[]{:S(2)}) async-start(bf16[16,32,448]{2,1,0:T(8,128)(2,1)} %bitcast.6), calls=%async_computation.1 | async-start | bytes 1048576 | tf_op jit(solution)/shard_map/all_to_all | solution.py:442
  50.5 0.7 collective-permute-start.9
  51.4 1.2 copy.13.res_ref
  52.6 8.6 %all-to-all-done.1.parts_ref = bf16[16,32,448]{2,1,0:T(8,128)(2,1)S(1)} async-done(((bf16[16,32,448]{2,1,0:T(8,128)(2,1)}), bf16[16,32,448]{2,1,0:T(8,128)(2,1)S(1)}, u32[]{:S(2)}, u32[]{:S(2)}) %all-to-all-start.1) | async-done | bytes 458784 | tf_op jit(solution)/shard_map/all_to_all | solution.py:442
  61.5 13.4 %all_to_all.20 = bf16[16,32,512]{2,1,0:T(8,128)(2,1)S(1)} all-to-all(bf16[16,32,512]{2,1,0:T(8,128)(2,1)S(1)} %get-tuple-element.10), channel_id=1, replica_groups=mesh['z'=8,'core'=2,'y'=4,'x'=4] {'y','x'}, dimensions={0} | all-to-all | bytes 1048576 | tf_op jit(solution)/shard_map/all_to_all | solution.py:442
  74.9 2.3 %collective-permute-start.8 = (bf16[512,512]{1,0:T(8,128)(2,1)S(1)}, bf16[512,512]{1,0:T(8,128)(2,1)S(1)}, u32[]{:S(2)}, u32[]{:S(2)}) collective-permute-start(bf16[512,512]{1,0:T(8,128)(2,1)S(1)} %bitcast.12), channel_id=1, source_target_pairs={{0,16},{16,0},{1,17},{17,1},{2,18},{18,2},{3,19},{19,3},{4,20},{20... | collective-permute-start | bytes 1572872 | tf_op jit(solution)/shard_map/ppermute | solution.py:446
  77.3 1.2 copy-done.3
  78.5 1.2 copy-done.4
  79.7 1.0 first.1.part_ref
  80.7 0.5 widen.4
  81.3 2.4 %collective-permute-start.11 = (bf16[1488,128]{1,0:T(8,128)(2,1)S(1)}, bf16[1488,128]{1,0:T(8,128)(2,1)S(1)}, u32[]{:S(2)}, u32[]{:S(2)}) collective-permute-start(bf16[1488,128]{1,0:T(8,128)(2,1)S(1)} %widen.4), channel_id=1, source_target_pairs={{0,224},{32,0},{64,32},{96,64},{128,96},{160,128},{192,160},{224,1... | collective-permute-start | bytes 1142792 | tf_op jit(solution)/shard_map/ppermute | solution.py:450
  83.6 0.5 widen.5
  84.3 0.6 widen.3.keep_ref
  84.9 7.1 %collective-permute-done.11.above_ref = bf16[1488,128]{1,0:T(8,128)(2,1)S(1)} collective-permute-done((bf16[1488,128]{1,0:T(8,128)(2,1)S(1)}, bf16[1488,128]{1,0:T(8,128)(2,1)S(1)}, u32[]{:S(2)}, u32[]{:S(2)}) %collective-permute-start.11) | collective-permute-done | bytes 380960 | tf_op jit(solution)/shard_map/ppermute | solution.py:450
  91.9 3.7 %collective-permute-done.12.below_ref = bf16[1488,128]{1,0:T(8,128)(2,1)S(1)} collective-permute-done((bf16[1488,128]{1,0:T(8,128)(2,1)S(1)}, bf16[1488,128]{1,0:T(8,128)(2,1)S(1)}, u32[]{:S(2)}, u32[]{:S(2)}) %collective-permute-start.12) | collective-permute-done | bytes 380960 | tf_op jit(solution)/shard_map/ppermute | solution.py:450
  95.8 1.9 %collective-permute-start.13 = (bf16[592,128]{1,0:T(8,128)(2,1)S(1)}, bf16[592,128]{1,0:T(8,128)(2,1)S(1)}, u32[]{:S(2)}, u32[]{:S(2)}) collective-permute-start(bf16[592,128]{1,0:T(8,128)(2,1)S(1)} %get-tuple-element.12), channel_id=1, source_target_pairs={{0,160},{32,192},{64,224},{96,0},{128,32},{160,64},{192,96},{224,1... | collective-permute-start | bytes 454664 | tf_op jit(solution)/shard_map/ppermute | solution.py:450
  97.7 1.5 %collective-permute-start.14 = (bf16[592,128]{1,0:T(8,128)(2,1)S(1)}, bf16[592,128]{1,0:T(8,128)(2,1)S(1)}, u32[]{:S(2)}, u32[]{:S(2)}) collective-permute-start(bf16[592,128]{1,0:T(8,128)(2,1)S(1)} %get-tuple-element.13), channel_id=1, source_target_pairs={{0,96},{32,128},{64,160},{96,192},{128,224},{160,0},{192,32},{224,... | collective-permute-start | bytes 454664 | tf_op jit(solution)/shard_map/ppermute | solution.py:450
  99.1 10.5 %collective-permute-done.13.above_ref = bf16[592,128]{1,0:T(8,128)(2,1)S(1)} collective-permute-done((bf16[592,128]{1,0:T(8,128)(2,1)S(1)}, bf16[592,128]{1,0:T(8,128)(2,1)S(1)}, u32[]{:S(2)}, u32[]{:S(2)}) %collective-permute-start.13) | collective-permute-done | bytes 151584 | tf_op jit(solution)/shard_map/ppermute | solution.py:450
  109.9 1.2 collective-permute-start.18
  111.1 2.4 %collective-permute-start.17 = (bf16[288,128]{1,0:T(8,128)(2,1)S(1)}, bf16[288,128]{1,0:T(8,128)(2,1)S(1)}, u32[]{:S(2)}, u32[]{:S(2)}) collective-permute-start(bf16[288,128]{1,0:T(8,128)(2,1)S(1)} %hidden.1.refs_0_), channel_id=1, source_target_pairs={{0,192},{32,224},{64,0},{96,32},{128,64},{160,96},{192,128},{224,1... | collective-permute-start | bytes 221192 | tf_op jit(solution)/shard_map/ppermute | solution.py:450
  113.5 1.7 %collective-permute-start.16 = (bf16[288,128]{1,0:T(8,128)(2,1)S(1)}, bf16[288,128]{1,0:T(8,128)(2,1)S(1)}, u32[]{:S(2)}, u32[]{:S(2)}) collective-permute-start(bf16[288,128]{1,0:T(8,128)(2,1)S(1)} %hidden.1.refs_0_), channel_id=1, source_target_pairs={{0,32},{32,64},{64,96},{96,128},{128,160},{160,192},{192,224},{224... | collective-permute-start | bytes 221192 | tf_op jit(solution)/shard_map/ppermute | solution.py:450
  115.3 1.1 collective-permute-start.15
  116.4 1.4 collective-permute-start.20
  117.7 2.6 %collective-permute-start.21 = (bf16[288,128]{1,0:T(8,128)(2,1)S(1)}, bf16[288,128]{1,0:T(8,128)(2,1)S(1)}, u32[]{:S(2)}, u32[]{:S(2)}) collective-permute-start(bf16[288,128]{1,0:T(8,128)(2,1)S(1)} %collective-permute-done.17.refs_3_), channel_id=1, source_target_pairs={{0,192},{32,224},{64,0},{96,32},{128,64},{160,96},{192,128},{224,1... | collective-permute-start | bytes 221192 | tf_op jit(solution)/shard_map/ppermute | solution.py:450
  120.3 0.8 collective-permute-start.19
  121.2 1.6 %collective-permute-done.21.refs_7_ = bf16[288,128]{1,0:T(8,128)(2,1)S(1)} collective-permute-done((bf16[288,128]{1,0:T(8,128)(2,1)S(1)}, bf16[288,128]{1,0:T(8,128)(2,1)S(1)}, u32[]{:S(2)}, u32[]{:S(2)}) %collective-permute-start.21) | collective-permute-done | bytes 73760 | tf_op jit(solution)/shard_map/ppermute | solution.py:450
  122.8 1.7 %collective-permute-done.19.refs_5_ = bf16[288,128]{1,0:T(8,128)(2,1)S(1)} collective-permute-done((bf16[288,128]{1,0:T(8,128)(2,1)S(1)}, bf16[288,128]{1,0:T(8,128)(2,1)S(1)}, u32[]{:S(2)}, u32[]{:S(2)}) %collective-permute-start.19) | collective-permute-done | bytes 73760 | tf_op jit(solution)/shard_map/ppermute | solution.py:450
  124.5 4.9 %collective-permute-start.22 = (bf16[2304,128]{1,0:T(8,128)(2,1)S(1)}, bf16[2304,128]{1,0:T(8,128)(2,1)S(1)}, u32[]{:S(2)}, u32[]{:S(2)}) collective-permute-start(bf16[2304,128]{1,0:T(8,128)(2,1)S(1)} %pack.3), channel_id=1, source_target_pairs={{0,16},{16,0},{1,17},{17,1},{2,18},{18,2},{3,19},{19,3},{4,20},{20... | collective-permute-start | bytes 1769480 | tf_op jit(solution)/shard_map/ppermute | solution.py:446
  129.4 0.6 downa.1.rest_0_
  130.0 1.0 collective-permute-done.22
  131.0 0.7 downb.1
  131.7 13.4 %all_to_all.21.parts_ref = bf16[16,32,448]{2,1,0:T(8,128)(2,1)S(1)} all-to-all(bf16[16,32,448]{2,1,0:T(8,128)(2,1)S(1)} %bitcast.22), channel_id=1, replica_groups=mesh['z'=8,'core'=2,'y'=4,'x'=4] {'y','x'}, dimensions={0} | all-to-all | bytes 917504 | tf_op jit(solution)/shard_map/all_to_all | solution.py:442
  145.1 0.7 last.1
  (34 shorter events, 2.2 us)
Async XLA Ops:
  0.0 24.5 %copy-start.2 = (bf16[8,512,128]{2,1,0:T(8,128)(2,1)S(1)}, bf16[8,512,128]{2,1,0:T(8,128)(2,1)}, u32[]{:S(2)}) copy-start(bf16[8,512,128]{2,1,0:T(8,128)(2,1)} %w_ref.1) | copy-start | bytes 3145732
  0.0 44.1 %copy-start.1 = (bf16[1024,448]{0,1:T(8,128)(2,1)S(1)}, bf16[1024,448]{0,1:T(8,128)(2,1)}, u32[]{:S(2)}) copy-start(bf16[1024,448]{0,1:T(8,128)(2,1)} %param.18) | copy-start | bytes 2752516
  7.4 43.9 %copy-start.5 = (bf16[448]{0:T(512)(128)(2,1)S(1)}, bf16[448]{0:T(512)(128)(2,1)}, u32[]{:S(2)}) copy-start(bf16[448]{0:T(512)(128)(2,1)} %param.20) | copy-start | bytes 2692
  7.4 17.0 %all-to-all-start = ((bf16[32,8,512]{2,1,0:T(8,128)(2,1)}), bf16[32,8,512]{2,1,0:T(8,128)(2,1)S(1)}, u32[]{:S(2)}, u32[]{:S(2)}) async-start(bf16[32,8,512]{2,1,0:T(8,128)(2,1)} %bitcast.25), calls=%async_computation | async-start | bytes 524288 | tf_op jit(solution)/shard_map/all_to_all | solution.py:442
  24.8 8.9 %collective-permute-start.3 = (bf16[64,512]{1,0:T(8,128)(2,1)S(1)}, bf16[64,512]{1,0:T(8,128)(2,1)S(1)}, u32[]{:S(2)}, u32[]{:S(2)}) collective-permute-start(bf16[64,512]{1,0:T(8,128)(2,1)S(1)} %heads.1.refs_0_), channel_id=1, source_target_pairs={{0,64},{32,96},{64,128},{96,160},{128,192},{160,224},{192,0},{224,... | collective-permute-start | bytes 196616 | tf_op jit(solution)/shard_map/ppermute | solution.py:450
  27.9 6.8 %collective-permute-start.2 = (bf16[64,512]{1,0:T(8,128)(2,1)S(1)}, bf16[64,512]{1,0:T(8,128)(2,1)S(1)}, u32[]{:S(2)}, u32[]{:S(2)}) collective-permute-start(bf16[64,512]{1,0:T(8,128)(2,1)S(1)} %heads.1.refs_0_), channel_id=1, source_target_pairs={{0,192},{32,224},{64,0},{96,32},{128,64},{160,96},{192,128},{224,1... | collective-permute-start | bytes 196616 | tf_op jit(solution)/shard_map/ppermute | solution.py:450
  31.0 6.4 %collective-permute-start.1 = (bf16[64,512]{1,0:T(8,128)(2,1)S(1)}, bf16[64,512]{1,0:T(8,128)(2,1)S(1)}, u32[]{:S(2)}, u32[]{:S(2)}) collective-permute-start(bf16[64,512]{1,0:T(8,128)(2,1)S(1)} %heads.1.refs_0_), channel_id=1, source_target_pairs={{0,32},{32,64},{64,96},{96,128},{128,160},{160,192},{192,224},{224... | collective-permute-start | bytes 196616 | tf_op jit(solution)/shard_map/ppermute | solution.py:450
  31.8 5.7 %collective-permute-start = (bf16[64,512]{1,0:T(8,128)(2,1)S(1)}, bf16[64,512]{1,0:T(8,128)(2,1)S(1)}, u32[]{:S(2)}, u32[]{:S(2)}) collective-permute-start(bf16[64,512]{1,0:T(8,128)(2,1)S(1)} %heads.1.refs_0_), channel_id=1, source_target_pairs={{0,224},{32,0},{64,32},{96,64},{128,96},{160,128},{192,160},{224,1... | collective-permute-start | bytes 196616 | tf_op jit(solution)/shard_map/ppermute | solution.py:450
  33.7 4.3 %collective-permute-start.5 = (bf16[64,512]{1,0:T(8,128)(2,1)S(1)}, bf16[64,512]{1,0:T(8,128)(2,1)S(1)}, u32[]{:S(2)}, u32[]{:S(2)}) collective-permute-start(bf16[64,512]{1,0:T(8,128)(2,1)S(1)} %collective-permute-done.3.refs_4_), channel_id=1, source_target_pairs={{0,32},{32,64},{64,96},{96,128},{128,160},{160,192},{192,224},{224... | collective-permute-start | bytes 196616 | tf_op jit(solution)/shard_map/ppermute | solution.py:450
  34.7 6.0 %collective-permute-start.6 = (bf16[64,512]{1,0:T(8,128)(2,1)S(1)}, bf16[64,512]{1,0:T(8,128)(2,1)S(1)}, u32[]{:S(2)}, u32[]{:S(2)}) collective-permute-start(bf16[64,512]{1,0:T(8,128)(2,1)S(1)} %collective-permute-done.2.refs_3_), channel_id=1, source_target_pairs={{0,192},{32,224},{64,0},{96,32},{128,64},{160,96},{192,128},{224,1... | collective-permute-start | bytes 196616 | tf_op jit(solution)/shard_map/ppermute | solution.py:450
  36.7 4.0 %collective-permute-start.4 = (bf16[64,512]{1,0:T(8,128)(2,1)S(1)}, bf16[64,512]{1,0:T(8,128)(2,1)S(1)}, u32[]{:S(2)}, u32[]{:S(2)}) collective-permute-start(bf16[64,512]{1,0:T(8,128)(2,1)S(1)} %collective-permute-done.2.refs_3_), channel_id=1, source_target_pairs={{0,224},{32,0},{64,32},{96,64},{128,96},{160,128},{192,160},{224,1... | collective-permute-start | bytes 196616 | tf_op jit(solution)/shard_map/ppermute | solution.py:450
  40.8 4.9 %collective-permute-start.7 = (bf16[512,512]{1,0:T(8,128)(2,1)S(1)}, bf16[512,512]{1,0:T(8,128)(2,1)S(1)}, u32[]{:S(2)}, u32[]{:S(2)}) collective-permute-start(bf16[512,512]{1,0:T(8,128)(2,1)S(1)} %pack.2.heads_ref), channel_id=1, source_target_pairs={{0,16},{16,0},{1,17},{17,1},{2,18},{18,2},{3,19},{19,3},{4,20},{20... | collective-permute-start | bytes 1572872 | tf_op jit(solution)/shard_map/ppermute | solution.py:446
  46.9 14.3 %all-to-all-start.1 = ((bf16[16,32,448]{2,1,0:T(8,128)(2,1)}), bf16[16,32,448]{2,1,0:T(8,128)(2,1)S(1)}, u32[]{:S(2)}, u32[]{:S(2)}) async-start(bf16[16,32,448]{2,1,0:T(8,128)(2,1)} %bitcast.6), calls=%async_computation.1 | async-start | bytes 1048576 | tf_op jit(solution)/shard_map/all_to_all | solution.py:442
  50.5 30.2 %collective-permute-start.9 = (bf16[448,1152]{1,0:T(8,128)(2,1)}, bf16[448,1152]{1,0:T(8,128)(2,1)S(1)}, u32[]{:S(2)}, u32[]{:S(2)}) collective-permute-start(bf16[448,1152]{1,0:T(8,128)(2,1)} %g_ref.1), channel_id=1, source_target_pairs={{0,16},{16,0},{1,17},{17,1},{2,18},{18,2},{3,19},{19,3},{4,20},{20... | collective-permute-start | bytes 3096584 | tf_op jit(solution)/shard_map/ppermute | solution.py:446
  51.3 29.4 %collective-permute-start.10 = (bf16[448,1152]{1,0:T(8,128)(2,1)}, bf16[448,1152]{1,0:T(8,128)(2,1)S(1)}, u32[]{:S(2)}, u32[]{:S(2)}) collective-permute-start(bf16[448,1152]{1,0:T(8,128)(2,1)} %u_ref.1), channel_id=1, source_target_pairs={{0,16},{16,0},{1,17},{17,1},{2,18},{18,2},{3,19},{19,3},{4,20},{20... | collective-permute-start | bytes 3096584 | tf_op jit(solution)/shard_map/ppermute | solution.py:446
  74.9 5.8 %collective-permute-start.8 = (bf16[512,512]{1,0:T(8,128)(2,1)S(1)}, bf16[512,512]{1,0:T(8,128)(2,1)S(1)}, u32[]{:S(2)}, u32[]{:S(2)}) collective-permute-start(bf16[512,512]{1,0:T(8,128)(2,1)S(1)} %bitcast.12), channel_id=1, source_target_pairs={{0,16},{16,0},{1,17},{17,1},{2,18},{18,2},{3,19},{19,3},{4,20},{20... | collective-permute-start | bytes 1572872 | tf_op jit(solution)/shard_map/ppermute | solution.py:446
  77.3 1.2 copy-start.3
  78.5 1.2 copy-start.4
  81.3 10.7 %collective-permute-start.11 = (bf16[1488,128]{1,0:T(8,128)(2,1)S(1)}, bf16[1488,128]{1,0:T(8,128)(2,1)S(1)}, u32[]{:S(2)}, u32[]{:S(2)}) collective-permute-start(bf16[1488,128]{1,0:T(8,128)(2,1)S(1)} %widen.4), channel_id=1, source_target_pairs={{0,224},{32,0},{64,32},{96,64},{128,96},{160,128},{192,160},{224,1... | collective-permute-start | bytes 1142792 | tf_op jit(solution)/shard_map/ppermute | solution.py:450
  84.2 45.2 %copy-start = (bf16[1152,448]{0,1:T(8,128)(2,1)S(1)}, bf16[1152,448]{0,1:T(8,128)(2,1)}, u32[]{:S(2)}) copy-start(bf16[1152,448]{0,1:T(8,128)(2,1)} %param.23) | copy-start | bytes 3096580
  84.2 11.5 %collective-permute-start.12 = (bf16[1488,128]{1,0:T(8,128)(2,1)S(1)}, bf16[1488,128]{1,0:T(8,128)(2,1)S(1)}, u32[]{:S(2)}, u32[]{:S(2)}) collective-permute-start(bf16[1488,128]{1,0:T(8,128)(2,1)S(1)} %widen.5), channel_id=1, source_target_pairs={{0,32},{32,64},{64,96},{96,128},{128,160},{160,192},{192,224},{224... | collective-permute-start | bytes 1142792 | tf_op jit(solution)/shard_map/ppermute | solution.py:450
  95.8 13.9 %collective-permute-start.13 = (bf16[592,128]{1,0:T(8,128)(2,1)S(1)}, bf16[592,128]{1,0:T(8,128)(2,1)S(1)}, u32[]{:S(2)}, u32[]{:S(2)}) collective-permute-start(bf16[592,128]{1,0:T(8,128)(2,1)S(1)} %get-tuple-element.12), channel_id=1, source_target_pairs={{0,160},{32,192},{64,224},{96,0},{128,32},{160,64},{192,96},{224,1... | collective-permute-start | bytes 454664 | tf_op jit(solution)/shard_map/ppermute | solution.py:450
  97.7 12.0 %collective-permute-start.14 = (bf16[592,128]{1,0:T(8,128)(2,1)S(1)}, bf16[592,128]{1,0:T(8,128)(2,1)S(1)}, u32[]{:S(2)}, u32[]{:S(2)}) collective-permute-start(bf16[592,128]{1,0:T(8,128)(2,1)S(1)} %get-tuple-element.13), channel_id=1, source_target_pairs={{0,96},{32,128},{64,160},{96,192},{128,224},{160,0},{192,32},{224,... | collective-permute-start | bytes 454664 | tf_op jit(solution)/shard_map/ppermute | solution.py:450
  109.9 6.4 %collective-permute-start.18 = (bf16[288,128]{1,0:T(8,128)(2,1)S(1)}, bf16[288,128]{1,0:T(8,128)(2,1)S(1)}, u32[]{:S(2)}, u32[]{:S(2)}) collective-permute-start(bf16[288,128]{1,0:T(8,128)(2,1)S(1)} %hidden.1.refs_0_), channel_id=1, source_target_pairs={{0,64},{32,96},{64,128},{96,160},{128,192},{160,224},{192,0},{224,... | collective-permute-start | bytes 221192 | tf_op jit(solution)/shard_map/ppermute | solution.py:450
  111.1 6.6 %collective-permute-start.17 = (bf16[288,128]{1,0:T(8,128)(2,1)S(1)}, bf16[288,128]{1,0:T(8,128)(2,1)S(1)}, u32[]{:S(2)}, u32[]{:S(2)}) collective-permute-start(bf16[288,128]{1,0:T(8,128)(2,1)S(1)} %hidden.1.refs_0_), channel_id=1, source_target_pairs={{0,192},{32,224},{64,0},{96,32},{128,64},{160,96},{192,128},{224,1... | collective-permute-start | bytes 221192 | tf_op jit(solution)/shard_map/ppermute | solution.py:450
  113.5 7.6 %collective-permute-start.16 = (bf16[288,128]{1,0:T(8,128)(2,1)S(1)}, bf16[288,128]{1,0:T(8,128)(2,1)S(1)}, u32[]{:S(2)}, u32[]{:S(2)}) collective-permute-start(bf16[288,128]{1,0:T(8,128)(2,1)S(1)} %hidden.1.refs_0_), channel_id=1, source_target_pairs={{0,32},{32,64},{64,96},{96,128},{128,160},{160,192},{192,224},{224... | collective-permute-start | bytes 221192 | tf_op jit(solution)/shard_map/ppermute | solution.py:450
  115.3 5.8 %collective-permute-start.15 = (bf16[288,128]{1,0:T(8,128)(2,1)S(1)}, bf16[288,128]{1,0:T(8,128)(2,1)S(1)}, u32[]{:S(2)}, u32[]{:S(2)}) collective-permute-start(bf16[288,128]{1,0:T(8,128)(2,1)S(1)} %hidden.1.refs_0_), channel_id=1, source_target_pairs={{0,224},{32,0},{64,32},{96,64},{128,96},{160,128},{192,160},{224,1... | collective-permute-start | bytes 221192 | tf_op jit(solution)/shard_map/ppermute | solution.py:450
  116.4 4.8 %collective-permute-start.20 = (bf16[288,128]{1,0:T(8,128)(2,1)S(1)}, bf16[288,128]{1,0:T(8,128)(2,1)S(1)}, u32[]{:S(2)}, u32[]{:S(2)}) collective-permute-start(bf16[288,128]{1,0:T(8,128)(2,1)S(1)} %collective-permute-done.18.refs_4_), channel_id=1, source_target_pairs={{0,32},{32,64},{64,96},{96,128},{128,160},{160,192},{192,224},{224... | collective-permute-start | bytes 221192 | tf_op jit(solution)/shard_map/ppermute | solution.py:450
  117.7 5.0 %collective-permute-start.21 = (bf16[288,128]{1,0:T(8,128)(2,1)S(1)}, bf16[288,128]{1,0:T(8,128)(2,1)S(1)}, u32[]{:S(2)}, u32[]{:S(2)}) collective-permute-start(bf16[288,128]{1,0:T(8,128)(2,1)S(1)} %collective-permute-done.17.refs_3_), channel_id=1, source_target_pairs={{0,192},{32,224},{64,0},{96,32},{128,64},{160,96},{192,128},{224,1... | collective-permute-start | bytes 221192 | tf_op jit(solution)/shard_map/ppermute | solution.py:450
  120.3 4.2 %collective-permute-start.19 = (bf16[288,128]{1,0:T(8,128)(2,1)S(1)}, bf16[288,128]{1,0:T(8,128)(2,1)S(1)}, u32[]{:S(2)}, u32[]{:S(2)}) collective-permute-start(bf16[288,128]{1,0:T(8,128)(2,1)S(1)} %collective-permute-done.17.refs_3_), channel_id=1, source_target_pairs={{0,224},{32,0},{64,32},{96,64},{128,96},{160,128},{192,160},{224,1... | collective-permute-start | bytes 221192 | tf_op jit(solution)/shard_map/ppermute | solution.py:450
  124.5 6.5 %collective-permute-start.22 = (bf16[2304,128]{1,0:T(8,128)(2,1)S(1)}, bf16[2304,128]{1,0:T(8,128)(2,1)S(1)}, u32[]{:S(2)}, u32[]{:S(2)}) collective-permute-start(bf16[2304,128]{1,0:T(8,128)(2,1)S(1)} %pack.3), channel_id=1, source_target_pairs={{0,16},{16,0},{1,17},{17,1},{2,18},{18,2},{3,19},{19,3},{4,20},{20... | collective-permute-start | bytes 1769480 | tf_op jit(solution)/shard_map/ppermute | solution.py:446

commit v4 on v3

--- a/solution.py
+++ b/solution.py
@@ -209,7 +209,7 @@
             jax.ShapeDtypeStruct((16, rows, 512), BF16),
         ],
         compiler_params=params(16),
-        cost_estimate=cost(1_000_000, 1_500_000),
+        cost_estimate=cost(2_500_000_000, 1_500_000),
         name="middle",
     )(place, parts, residual, gain)
 
@@ -236,15 +236,23 @@
     )(core, own, gate, upper)
 
 
-def widen_kernel(takes, core_ref, z_ref, part_ref, own_ref, other_ref, g_ref, u_ref, out_ref):
+def widen_kernel(lists, core_ref, z_ref, part_ref, own_ref, other_ref, g_ref, u_ref, *outs):
     deep = g_ref.shape[0]
     low = core_ref[0] == 0
     full = pl.ds(pl.multiple_of(core_ref[0] * 640, LANES), 512)
-    wide = out_ref.dtype == F32
+    wide = outs[0].dtype == F32
+    places = []
+    source = 0
+    for out_ref, takes in zip(outs, lists):
+        at = 0
+        for far, begin, rows in takes:
+            places.append((out_ref, at, source, far, begin, rows))
+            at += 9 * rows + 16
+            source += rows
 
     def rows_of(ref, columns):
         pieces = []
-        for far, begin, rows in takes:
+        for _, _, _, far, begin, rows in places:
             at = lax.rem(z_ref[0] + far, 8) * 64 + begin
             pieces.append(ref[pl.ds(pl.multiple_of(at, 32), rows), columns])
         return jnp.concatenate(pieces, axis=0)
@@ -252,16 +260,13 @@
     other = rows_of(other_ref, slice(0, deep))
 
     def put(block, value):
-        value = value.astype(out_ref.dtype)
-        at = source = 0
-        for _, _, rows in takes:
+        value = value.astype(outs[0].dtype)
+        for out_ref, at, source, _, _, rows in places:
             for j in range(value.shape[1] // LANES):
                 begin = at + (block + j) * rows
                 out_ref[begin : begin + rows] = value[
                     source : source + rows, j * LANES : (j + 1) * LANES
                 ]
-            at += 9 * rows + 16
-            source += rows
 
     put(0, rows_of(part_ref, slice(0, 512)) + dot(other, g_ref[:, full]))
     put(4, rows_of(part_ref, slice(512, 1024)) + dot(other, u_ref[:, full]))
@@ -275,14 +280,11 @@
     extra = slice(deep, 512)
     squares = jnp.sum(rows_of(own_ref, extra).astype(F32), axis=1, keepdims=True)
     squares = squares + jnp.sum(rows_of(other_ref, extra).astype(F32), axis=1, keepdims=True)
-    at = source = 0
-    for _, first_row, rows in takes:
+    for out_ref, at, source, _, first_row, rows in places:
         same = iota((rows, LANES), 0) + first_row == iota((rows, LANES), 1)
         line = jnp.where(same, squares[source : source + rows], 0.0)
         line = jnp.sum(line, axis=0, keepdims=True)
         out_ref[at + 9 * rows : at + 9 * rows + 16] = tile_of(line, wide).astype(out_ref.dtype)
-        at += 9 * rows + 16
-        source += rows
 
 
 def tile_of(line, wide):
@@ -291,13 +293,15 @@
     return jnp.where(row == 0, high, jnp.where(row == 1, line - high, 0.0))
 
 
-def widen(takes, kind, core, z, part, own, other, gate, upper):
-    rows = sum(9 * n + 16 for _, _, n in takes)
-    return pl.pallas_call(
-        functools.partial(widen_kernel, takes),
+def widen(lists, kind, core, z, part, own, other, gate, upper):
+    shapes = [
+        jax.ShapeDtypeStruct((sum(9 * n + 16 for _, _, n in takes), LANES), kind) for takes in lists
+    ]
+    return pl.pallas_call(
+        functools.partial(widen_kernel, lists),
         in_specs=[smem(), smem()] + whole(5),
-        out_specs=whole(1)[0],
-        out_shape=jax.ShapeDtypeStruct((rows, LANES), kind),
+        out_specs=whole(len(lists)),
+        out_shape=shapes,
         compiler_params=params(16),
         cost_estimate=cost(200_000_000, 6_000_000),
         name="widen",
@@ -305,22 +309,24 @@
 
 
 BLOCK = 592
-TO_LOWER = ((7, 0, 64), (2, 0, 64), (4, 0, 32))
-TO_UPPER = ((1, 0, 64), (6, 0, 64), (4, 32, 32))
-TO_KEEP = ((0, 0, 64), (5, 0, 64), (3, 0, 64))
-
-
-def merge_kernel(keep_ref, above_ref, below_ref, stay_ref, down_ref, up_ref):
+TO_LOWER = ((7, 0, 64), (5, 0, 64))
+TO_UPPER = ((1, 0, 64), (3, 0, 64))
+TWO_LOWER = ((4, 0, 32),)
+TWO_UPPER = ((4, 32, 32),)
+TO_KEEP = ((0, 0, 64), (6, 0, 64), (2, 0, 64))
+
+
+def merge_kernel(keep_ref, above_ref, below_ref, far_above_ref, far_below_ref, stay_ref, down_ref, up_ref):
     def block(ref, k):
         return ref[k * BLOCK : (k + 1) * BLOCK].astype(F32)
 
     stay_ref[...] = block(keep_ref, 0) + block(above_ref, 0) + block(below_ref, 0)
     for out_ref, k, full_ref, half_ref, shift in (
-        (down_ref, 1, below_ref, above_ref, 0),
-        (up_ref, 2, above_ref, below_ref, 32),
+        (down_ref, 1, above_ref, far_above_ref, 0),
+        (up_ref, 2, below_ref, far_below_ref, 32),
     ):
         total = block(keep_ref, k) + block(full_ref, 1)
-        half = half_ref[2 * BLOCK :].astype(F32)
+        half = half_ref[...].astype(F32)
         for j in range(9):
             at = j * 64
             out_ref[at + 32 - shift : at + 64 - shift] = total[
@@ -332,17 +338,17 @@
         out_ref[576:592] = tile_of(line, False).astype(BF16)
 
 
-def merge(keep, above, below):
+def merge(*parts):
     shapes = [jax.ShapeDtypeStruct((BLOCK, LANES), kind) for kind in (F32, BF16, BF16)]
     return pl.pallas_call(
         merge_kernel,
-        in_specs=whole(3),
+        in_specs=whole(5),
         out_specs=whole(3),
         out_shape=shapes,
         compiler_params=params(16),
         cost_estimate=cost(5_000_000, 3_000_000),
         name="merge",
-    )(keep, above, below)
+    )(*parts)
 
 
 def gated(gate, upper):
@@ -492,10 +498,11 @@
     scaled_other = swap(scaled)
     part = first(core, scaled, w_gate, w_up)
     rest = (core, height, part, scaled, scaled_other, gate_other, up_other)
-    from_above = shift(widen(TO_LOWER, BF16, *rest), 7)
-    from_below = shift(widen(TO_UPPER, BF16, *rest), 1)
-    stay, lower, upper = merge(widen(TO_KEEP, F32, *rest), from_above, from_below)
-    hidden = gather(make_hidden(stay, shift(lower, 5), shift(upper, 3)))
+    two_lower, two_upper, lower, upper = widen((TWO_LOWER, TWO_UPPER, TO_LOWER, TO_UPPER), BF16, *rest)
+    arrived = (shift(lower, 7), shift(upper, 1), shift(two_lower, 6), shift(two_upper, 2))
+    (keep,) = widen((TO_KEEP,), F32, *rest)
+    stay, lower, upper = merge(keep, *arrived)
+    hidden = gather(make_hidden(stay, shift(lower, 6), shift(upper, 2)))
     other = swap(hidden).reshape(8, 288, LANES)
     part = down(core, height, hidden.reshape(8, 288, LANES), w_down.T)
     outer = down(core, height, other, w_down.T, part)

time: 146 us -> 143 us (0.979)
  waiting for transfers between devices: 47.3 us -> 42.2 us
  starting transfers between devices: 53 us -> 54.9 us
    ppermute x18 -> x20, waiting for transfers between devices: 28.3 us -> 22.9 us  [shift(): return lax.ppermute(x, 'z', [(i, (i + far) % 8) for i in range(8)])]
    ppermute x18 -> x20, starting transfers between devices: 29.3 us -> 31.4 us  [shift(): return lax.ppermute(x, 'z', [(i, (i + far) % 8) for i in range(8)])]
    unnamed x13 -> x15, local copies, waits for them, and re-layouts: 3.68 us -> 3.18 us
  transfers between devices with their start and end apart: 25 -> 27, of which waited for: 13 -> 14; matrix products, arithmetic and copies ran while one was open for 1% -> 1% of each run, Pallas kernels for 2% -> 3%
where the time goes in v4:
time: 143 us
  starting transfers between devices  54.9 us (38%)
  waiting for transfers between devices  42.2 us (30%)
  blocking collectives  26.7 us (19%)
  Pallas kernels  15.6 us (11%)
  local copies, waits for them, and re-layouts  3.18 us (2%)
    ppermute x20, starting transfers between devices, shift(): return lax.ppermute(x, 'z', [(i, (i + far) % 8) for i in range(8)])  31.4 us
    all_to_all x2, blocking collectives, exchange(): return lax.all_to_all(x, axes, split_axis=0, concat_axis=0, tiled=True)  26.7 us
    ppermute x20, waiting for transfers between devices, shift(): return lax.ppermute(x, 'z', [(i, (i + far) % 8) for i in range(8)])  22.9 us
    all_to_all x2, waiting for transfers between devices, exchange(): return lax.all_to_all(x, axes, split_axis=0, concat_axis=0, tiled=True)  16.6 us
    all_to_all x2, starting transfers between devices, exchange(): return lax.all_to_all(x, axes, split_axis=0, concat_axis=0, tiled=True)  13 us
    ppermute x5, starting transfers between devices, swap(): return lax.ppermute(x, 'core', [(0, 1), (1, 0)])  10.4 us
    pallas_call x1, Pallas kernels, attend(): pl.pallas_call(attend_kernel, grid=(2,), in_specs=[pl.BlockSpec(idx.shape...  7.44 us
    unnamed x15, local copies, waits for them, and re-layouts  3.18 us
  transfers between devices with their start and end apart: 27, of which 14 were waited for; matrix products, arithmetic and copies ran while one was open for 1% of the time, Pallas kernels for 3%

profile of v4, /device:TPU:1, one launch (start us, length us, event | category | flops | bytes accessed | tf_op | source)
XLA Modules:
  0.0 142.6 jit_solution(11459692089129176975)
XLA Ops:
  0.0 7.4 %attend.1 = bf16[256,512]{1,0:T(8,128)(2,1)} custom-call(s32[2,2048]{1,0:T(2,128)} %idx_ref.1, bf16[2,128,512]{2,1,0:T(8,128)(2,1)} %ql_ref.1, bf16[2,64,128]{2,1,0:T(8,128)(2,1)} %qr_ref.1, bf16[2,3072,512]{2,1,0:T(8,128)(2,1)} %lat_ref.1, bf16[2,64,3072]{2,1,0:T(8,128)(2,1)} %rope_ref.1), custom_call_target="tpu_custom_call" | custom-call | flops 1800000000 | bytes 8000000 | tf_op jit(solution)/shard_map/attend/pallas_call | solution.py:92
  7.4 8.7 %all-to-all-start = ((bf16[32,8,512]{2,1,0:T(8,128)(2,1)}), bf16[32,8,512]{2,1,0:T(8,128)(2,1)S(1)}, u32[]{:S(2)}, u32[]{:S(2)}) async-start(bf16[32,8,512]{2,1,0:T(8,128)(2,1)} %bitcast.24), calls=%async_computation | async-start | bytes 524288 | tf_op jit(solution)/shard_map/all_to_all | solution.py:448
  16.2 8.3 %all-to-all-done = bf16[32,8,512]{2,1,0:T(8,128)(2,1)S(1)} async-done(((bf16[32,8,512]{2,1,0:T(8,128)(2,1)}), bf16[32,8,512]{2,1,0:T(8,128)(2,1)S(1)}, u32[]{:S(2)}, u32[]{:S(2)}) %all-to-all-start) | async-done | bytes 262176 | tf_op jit(solution)/shard_map/all_to_all | solution.py:448
  24.9 3.1 %collective-permute-start.3 = (bf16[64,512]{1,0:T(8,128)(2,1)S(1)}, bf16[64,512]{1,0:T(8,128)(2,1)S(1)}, u32[]{:S(2)}, u32[]{:S(2)}) collective-permute-start(bf16[64,512]{1,0:T(8,128)(2,1)S(1)} %heads.1.refs_0_), channel_id=1, source_target_pairs={{0,64},{32,96},{64,128},{96,160},{128,192},{160,224},{192,0},{224,... | collective-permute-start | bytes 196616 | tf_op jit(solution)/shard_map/ppermute | solution.py:456
  27.9 3.1 %collective-permute-start.2 = (bf16[64,512]{1,0:T(8,128)(2,1)S(1)}, bf16[64,512]{1,0:T(8,128)(2,1)S(1)}, u32[]{:S(2)}, u32[]{:S(2)}) collective-permute-start(bf16[64,512]{1,0:T(8,128)(2,1)S(1)} %heads.1.refs_0_), channel_id=1, source_target_pairs={{0,192},{32,224},{64,0},{96,32},{128,64},{160,96},{192,128},{224,1... | collective-permute-start | bytes 196616 | tf_op jit(solution)/shard_map/ppermute | solution.py:456
  31.1 0.7 collective-permute-start.1
  31.8 1.9 %collective-permute-start = (bf16[64,512]{1,0:T(8,128)(2,1)S(1)}, bf16[64,512]{1,0:T(8,128)(2,1)S(1)}, u32[]{:S(2)}, u32[]{:S(2)}) collective-permute-start(bf16[64,512]{1,0:T(8,128)(2,1)S(1)} %heads.1.refs_0_), channel_id=1, source_target_pairs={{0,224},{32,0},{64,32},{96,64},{128,96},{160,128},{192,160},{224,1... | collective-permute-start | bytes 196616 | tf_op jit(solution)/shard_map/ppermute | solution.py:456
  33.7 0.7 collective-permute-start.5
  34.7 2.0 %collective-permute-start.6 = (bf16[64,512]{1,0:T(8,128)(2,1)S(1)}, bf16[64,512]{1,0:T(8,128)(2,1)S(1)}, u32[]{:S(2)}, u32[]{:S(2)}) collective-permute-start(bf16[64,512]{1,0:T(8,128)(2,1)S(1)} %collective-permute-done.2.refs_3_), channel_id=1, source_target_pairs={{0,192},{32,224},{64,0},{96,32},{128,64},{160,96},{192,128},{224,1... | collective-permute-start | bytes 196616 | tf_op jit(solution)/shard_map/ppermute | solution.py:456
  36.8 0.7 collective-permute-start.4
  37.4 0.6 collective-permute-done.5.refs_6_
  38.1 2.7 %collective-permute-done.6.refs_7_ = bf16[64,512]{1,0:T(8,128)(2,1)S(1)} collective-permute-done((bf16[64,512]{1,0:T(8,128)(2,1)S(1)}, bf16[64,512]{1,0:T(8,128)(2,1)S(1)}, u32[]{:S(2)}, u32[]{:S(2)}) %collective-permute-start.6) | collective-permute-done | bytes 65568 | tf_op jit(solution)/shard_map/ppermute | solution.py:456
  40.8 3.4 %collective-permute-start.7 = (bf16[512,512]{1,0:T(8,128)(2,1)S(1)}, bf16[512,512]{1,0:T(8,128)(2,1)S(1)}, u32[]{:S(2)}, u32[]{:S(2)}) collective-permute-start(bf16[512,512]{1,0:T(8,128)(2,1)S(1)} %pack.2.heads_ref), channel_id=1, source_target_pairs={{0,16},{16,0},{1,17},{17,1},{2,18},{18,2},{3,19},{19,3},{4,20},{20... | collective-permute-start | bytes 1572872 | tf_op jit(solution)/shard_map/ppermute | solution.py:452
  44.6 1.1 collective-permute-done.7.heads_ref
  45.7 1.3 projectb.1
  46.9 4.2 %all-to-all-start.1 = ((bf16[16,32,448]{2,1,0:T(8,128)(2,1)}), bf16[16,32,448]{2,1,0:T(8,128)(2,1)}, u32[]{:S(2)}, u32[]{:S(2)}) async-start(bf16[16,32,448]{2,1,0:T(8,128)(2,1)} %bitcast.6), calls=%async_computation.1 | async-start | bytes 1048576 | tf_op jit(solution)/shard_map/all_to_all | solution.py:448
  51.8 2.0 %copy.13.res_ref = bf16[512,448]{1,0:T(8,128)(2,1)} copy(bf16[512,448]{0,1:T(8,128)(2,1)} %param.19) | data formatting | bytes 917504 | tf_op args[7]
  53.8 8.4 %all-to-all-done.1.parts_ref = bf16[16,32,448]{2,1,0:T(8,128)(2,1)} async-done(((bf16[16,32,448]{2,1,0:T(8,128)(2,1)}), bf16[16,32,448]{2,1,0:T(8,128)(2,1)}, u32[]{:S(2)}, u32[]{:S(2)}) %all-to-all-start.1) | async-done | bytes 458784 | tf_op jit(solution)/shard_map/all_to_all | solution.py:448
  62.2 1.1 copy-done.5
  63.3 1.3 middle.1
  64.6 13.3 %all_to_all.20 = bf16[16,32,512]{2,1,0:T(8,128)(2,1)S(1)} all-to-all(bf16[16,32,512]{2,1,0:T(8,128)(2,1)S(1)} %get-tuple-element.14), channel_id=1, replica_groups=mesh['z'=8,'core'=2,'y'=4,'x'=4] {'y','x'}, dimensions={0} | all-to-all | bytes 1048576 | tf_op jit(solution)/shard_map/all_to_all | solution.py:448
  78.0 2.2 %collective-permute-start.8 = (bf16[512,512]{1,0:T(8,128)(2,1)S(1)}, bf16[512,512]{1,0:T(8,128)(2,1)S(1)}, u32[]{:S(2)}, u32[]{:S(2)}) collective-permute-start(bf16[512,512]{1,0:T(8,128)(2,1)S(1)} %bitcast.12), channel_id=1, source_target_pairs={{0,16},{16,0},{1,17},{17,1},{2,18},{18,2},{3,19},{19,3},{4,20},{20... | collective-permute-start | bytes 1572872 | tf_op jit(solution)/shard_map/ppermute | solution.py:452
  80.2 1.0 first.1.part_ref
  81.2 0.5 collective-permute-done.8.other_ref
  81.7 0.8 widen.3
  82.5 2.5 %collective-permute-start.11 = (bf16[1184,128]{1,0:T(8,128)(2,1)S(1)}, bf16[1184,128]{1,0:T(8,128)(2,1)S(1)}, u32[]{:S(2)}, u32[]{:S(2)}) collective-permute-start(bf16[1184,128]{1,0:T(8,128)(2,1)S(1)} %get-tuple-element.15), channel_id=1, source_target_pairs={{0,224},{32,0},{64,32},{96,64},{128,96},{160,128},{192,160},{224,1... | collective-permute-start | bytes 909320 | tf_op jit(solution)/shard_map/ppermute | solution.py:456
  85.0 2.0 %collective-permute-start.13 = (bf16[304,128]{1,0:T(8,128)(2,1)S(1)}, bf16[304,128]{1,0:T(8,128)(2,1)S(1)}, u32[]{:S(2)}, u32[]{:S(2)}) collective-permute-start(bf16[304,128]{1,0:T(8,128)(2,1)S(1)} %get-tuple-element.17), channel_id=1, source_target_pairs={{0,192},{32,224},{64,0},{96,32},{128,64},{160,96},{192,128},{224,1... | collective-permute-start | bytes 233480 | tf_op jit(solution)/shard_map/ppermute | solution.py:456
  87.3 0.6 widen.2.keep_ref
  87.9 6.6 %collective-permute-done.13.far_above_ref = bf16[304,128]{1,0:T(8,128)(2,1)S(1)} collective-permute-done((bf16[304,128]{1,0:T(8,128)(2,1)S(1)}, bf16[304,128]{1,0:T(8,128)(2,1)S(1)}, u32[]{:S(2)}, u32[]{:S(2)}) %collective-permute-start.13) | collective-permute-done | bytes 77856 | tf_op jit(solution)/shard_map/ppermute | solution.py:456
  94.5 1.6 %collective-permute-done.14.far_below_ref = bf16[304,128]{1,0:T(8,128)(2,1)S(1)} collective-permute-done((bf16[304,128]{1,0:T(8,128)(2,1)S(1)}, bf16[304,128]{1,0:T(8,128)(2,1)S(1)}, u32[]{:S(2)}, u32[]{:S(2)}) %collective-permute-start.14) | collective-permute-done | bytes 77856 | tf_op jit(solution)/shard_map/ppermute | solution.py:456
  96.3 2.8 %collective-permute-start.15 = (bf16[592,128]{1,0:T(8,128)(2,1)S(1)}, bf16[592,128]{1,0:T(8,128)(2,1)S(1)}, u32[]{:S(2)}, u32[]{:S(2)}) collective-permute-start(bf16[592,128]{1,0:T(8,128)(2,1)S(1)} %get-tuple-element.20), channel_id=1, source_target_pairs={{0,192},{32,224},{64,0},{96,32},{128,64},{160,96},{192,128},{224,1... | collective-permute-start | bytes 454664 | tf_op jit(solution)/shard_map/ppermute | solution.py:456
  99.0 0.6 collective-permute-start.16
  99.6 4.7 %collective-permute-done.15.above_ref = bf16[592,128]{1,0:T(8,128)(2,1)S(1)} collective-permute-done((bf16[592,128]{1,0:T(8,128)(2,1)S(1)}, bf16[592,128]{1,0:T(8,128)(2,1)S(1)}, u32[]{:S(2)}, u32[]{:S(2)}) %collective-permute-start.15) | collective-permute-done | bytes 151584 | tf_op jit(solution)/shard_map/ppermute | solution.py:456
  104.3 1.0 collective-permute-done.16.below_ref
  105.6 4.3 %collective-permute-start.20 = (bf16[288,128]{1,0:T(8,128)(2,1)S(1)}, bf16[288,128]{1,0:T(8,128)(2,1)S(1)}, u32[]{:S(2)}, u32[]{:S(2)}) collective-permute-start(bf16[288,128]{1,0:T(8,128)(2,1)S(1)} %hidden.1.refs_0_), channel_id=1, source_target_pairs={{0,64},{32,96},{64,128},{96,160},{128,192},{160,224},{192,0},{224,... | collective-permute-start | bytes 221192 | tf_op jit(solution)/shard_map/ppermute | solution.py:456
  109.8 1.7 %collective-permute-start.18 = (bf16[288,128]{1,0:T(8,128)(2,1)S(1)}, bf16[288,128]{1,0:T(8,128)(2,1)S(1)}, u32[]{:S(2)}, u32[]{:S(2)}) collective-permute-start(bf16[288,128]{1,0:T(8,128)(2,1)S(1)} %hidden.1.refs_0_), channel_id=1, source_target_pairs={{0,32},{32,64},{64,96},{96,128},{128,160},{160,192},{192,224},{224... | collective-permute-start | bytes 221192 | tf_op jit(solution)/shard_map/ppermute | solution.py:456
  111.5 1.0 collective-permute-start.17
  112.5 1.5 %collective-permute-start.22 = (bf16[288,128]{1,0:T(8,128)(2,1)S(1)}, bf16[288,128]{1,0:T(8,128)(2,1)S(1)}, u32[]{:S(2)}, u32[]{:S(2)}) collective-permute-start(bf16[288,128]{1,0:T(8,128)(2,1)S(1)} %collective-permute-done.20.refs_4_), channel_id=1, source_target_pairs={{0,32},{32,64},{64,96},{96,128},{128,160},{160,192},{192,224},{224... | collective-permute-start | bytes 221192 | tf_op jit(solution)/shard_map/ppermute | solution.py:456
  114.0 1.5 %collective-permute-done.19.refs_3_ = bf16[288,128]{1,0:T(8,128)(2,1)S(1)} collective-permute-done((bf16[288,128]{1,0:T(8,128)(2,1)S(1)}, bf16[288,128]{1,0:T(8,128)(2,1)S(1)}, u32[]{:S(2)}, u32[]{:S(2)}) %collective-permute-start.19) | collective-permute-done | bytes 73760 | tf_op jit(solution)/shard_map/ppermute | solution.py:456
  115.5 1.1 collective-permute-start.23
  116.6 1.5 %collective-permute-start.21 = (bf16[288,128]{1,0:T(8,128)(2,1)S(1)}, bf16[288,128]{1,0:T(8,128)(2,1)S(1)}, u32[]{:S(2)}, u32[]{:S(2)}) collective-permute-start(bf16[288,128]{1,0:T(8,128)(2,1)S(1)} %collective-permute-done.19.refs_3_), channel_id=1, source_target_pairs={{0,224},{32,0},{64,32},{96,64},{128,96},{160,128},{192,160},{224,1... | collective-permute-start | bytes 221192 | tf_op jit(solution)/shard_map/ppermute | solution.py:456
  118.1 3.9 %collective-permute-done.23.refs_7_ = bf16[288,128]{1,0:T(8,128)(2,1)S(1)} collective-permute-done((bf16[288,128]{1,0:T(8,128)(2,1)S(1)}, bf16[288,128]{1,0:T(8,128)(2,1)S(1)}, u32[]{:S(2)}, u32[]{:S(2)}) %collective-permute-start.23) | collective-permute-done | bytes 73760 | tf_op jit(solution)/shard_map/ppermute | solution.py:456
  122.0 4.3 %collective-permute-start.24 = (bf16[2304,128]{1,0:T(8,128)(2,1)S(1)}, bf16[2304,128]{1,0:T(8,128)(2,1)S(1)}, u32[]{:S(2)}, u32[]{:S(2)}) collective-permute-start(bf16[2304,128]{1,0:T(8,128)(2,1)S(1)} %pack.3), channel_id=1, source_target_pairs={{0,16},{16,0},{1,17},{17,1},{2,18},{18,2},{3,19},{19,3},{4,20},{20... | collective-permute-start | bytes 1769480 | tf_op jit(solution)/shard_map/ppermute | solution.py:452
  126.3 0.6 downa.1.rest_0_
  126.9 1.0 collective-permute-done.24
  127.9 0.7 downb.1
  128.6 13.4 %all_to_all.21.parts_ref = bf16[16,32,448]{2,1,0:T(8,128)(2,1)S(1)} all-to-all(bf16[16,32,448]{2,1,0:T(8,128)(2,1)S(1)} %bitcast.21), channel_id=1, replica_groups=mesh['z'=8,'core'=2,'y'=4,'x'=4] {'y','x'}, dimensions={0} | all-to-all | bytes 917504 | tf_op jit(solution)/shard_map/all_to_all | solution.py:448
  141.9 0.7 last.1
  (39 shorter events, 2.7 us)
Async XLA Ops:
  0.0 24.5 %copy-start.2 = (bf16[8,512,128]{2,1,0:T(8,128)(2,1)S(1)}, bf16[8,512,128]{2,1,0:T(8,128)(2,1)}, u32[]{:S(2)}) copy-start(bf16[8,512,128]{2,1,0:T(8,128)(2,1)} %w_ref.1) | copy-start | bytes 3145732
  0.0 44.1 %copy-start.1 = (bf16[1024,448]{0,1:T(8,128)(2,1)S(1)}, bf16[1024,448]{0,1:T(8,128)(2,1)}, u32[]{:S(2)}) copy-start(bf16[1024,448]{0,1:T(8,128)(2,1)} %param.18) | copy-start | bytes 2752516
  7.4 43.8 %copy-start.3 = (bf16[448,1152]{1,0:T(8,128)(2,1)S(1)}, bf16[448,1152]{1,0:T(8,128)(2,1)}, u32[]{:S(2)}) copy-start(bf16[448,1152]{1,0:T(8,128)(2,1)} %g_ref.1) | copy-start | bytes 3096580
  7.4 44.4 %copy-start.6 = (bf16[448]{0:T(512)(128)(2,1)S(1)}, bf16[448]{0:T(512)(128)(2,1)}, u32[]{:S(2)}) copy-start(bf16[448]{0:T(512)(128)(2,1)} %param.20) | copy-start | bytes 2692
  7.4 17.0 %all-to-all-start = ((bf16[32,8,512]{2,1,0:T(8,128)(2,1)}), bf16[32,8,512]{2,1,0:T(8,128)(2,1)S(1)}, u32[]{:S(2)}, u32[]{:S(2)}) async-start(bf16[32,8,512]{2,1,0:T(8,128)(2,1)} %bitcast.24), calls=%async_computation | async-start | bytes 524288 | tf_op jit(solution)/shard_map/all_to_all | solution.py:448
  24.9 8.9 %collective-permute-start.3 = (bf16[64,512]{1,0:T(8,128)(2,1)S(1)}, bf16[64,512]{1,0:T(8,128)(2,1)S(1)}, u32[]{:S(2)}, u32[]{:S(2)}) collective-permute-start(bf16[64,512]{1,0:T(8,128)(2,1)S(1)} %heads.1.refs_0_), channel_id=1, source_target_pairs={{0,64},{32,96},{64,128},{96,160},{128,192},{160,224},{192,0},{224,... | collective-permute-start | bytes 196616 | tf_op jit(solution)/shard_map/ppermute | solution.py:456
  27.9 6.8 %collective-permute-start.2 = (bf16[64,512]{1,0:T(8,128)(2,1)S(1)}, bf16[64,512]{1,0:T(8,128)(2,1)S(1)}, u32[]{:S(2)}, u32[]{:S(2)}) collective-permute-start(bf16[64,512]{1,0:T(8,128)(2,1)S(1)} %heads.1.refs_0_), channel_id=1, source_target_pairs={{0,192},{32,224},{64,0},{96,32},{128,64},{160,96},{192,128},{224,1... | collective-permute-start | bytes 196616 | tf_op jit(solution)/shard_map/ppermute | solution.py:456
  31.1 6.4 %collective-permute-start.1 = (bf16[64,512]{1,0:T(8,128)(2,1)S(1)}, bf16[64,512]{1,0:T(8,128)(2,1)S(1)}, u32[]{:S(2)}, u32[]{:S(2)}) collective-permute-start(bf16[64,512]{1,0:T(8,128)(2,1)S(1)} %heads.1.refs_0_), channel_id=1, source_target_pairs={{0,32},{32,64},{64,96},{96,128},{128,160},{160,192},{192,224},{224... | collective-permute-start | bytes 196616 | tf_op jit(solution)/shard_map/ppermute | solution.py:456
  31.8 5.7 %collective-permute-start = (bf16[64,512]{1,0:T(8,128)(2,1)S(1)}, bf16[64,512]{1,0:T(8,128)(2,1)S(1)}, u32[]{:S(2)}, u32[]{:S(2)}) collective-permute-start(bf16[64,512]{1,0:T(8,128)(2,1)S(1)} %heads.1.refs_0_), channel_id=1, source_target_pairs={{0,224},{32,0},{64,32},{96,64},{128,96},{160,128},{192,160},{224,1... | collective-permute-start | bytes 196616 | tf_op jit(solution)/shard_map/ppermute | solution.py:456
  33.7 4.3 %collective-permute-start.5 = (bf16[64,512]{1,0:T(8,128)(2,1)S(1)}, bf16[64,512]{1,0:T(8,128)(2,1)S(1)}, u32[]{:S(2)}, u32[]{:S(2)}) collective-permute-start(bf16[64,512]{1,0:T(8,128)(2,1)S(1)} %collective-permute-done.3.refs_4_), channel_id=1, source_target_pairs={{0,32},{32,64},{64,96},{96,128},{128,160},{160,192},{192,224},{224... | collective-permute-start | bytes 196616 | tf_op jit(solution)/shard_map/ppermute | solution.py:456
  34.7 6.0 %collective-permute-start.6 = (bf16[64,512]{1,0:T(8,128)(2,1)S(1)}, bf16[64,512]{1,0:T(8,128)(2,1)S(1)}, u32[]{:S(2)}, u32[]{:S(2)}) collective-permute-start(bf16[64,512]{1,0:T(8,128)(2,1)S(1)} %collective-permute-done.2.refs_3_), channel_id=1, source_target_pairs={{0,192},{32,224},{64,0},{96,32},{128,64},{160,96},{192,128},{224,1... | collective-permute-start | bytes 196616 | tf_op jit(solution)/shard_map/ppermute | solution.py:456
  36.8 4.0 %collective-permute-start.4 = (bf16[64,512]{1,0:T(8,128)(2,1)S(1)}, bf16[64,512]{1,0:T(8,128)(2,1)S(1)}, u32[]{:S(2)}, u32[]{:S(2)}) collective-permute-start(bf16[64,512]{1,0:T(8,128)(2,1)S(1)} %collective-permute-done.2.refs_3_), channel_id=1, source_target_pairs={{0,224},{32,0},{64,32},{96,64},{128,96},{160,128},{192,160},{224,1... | collective-permute-start | bytes 196616 | tf_op jit(solution)/shard_map/ppermute | solution.py:456
  40.8 4.9 %collective-permute-start.7 = (bf16[512,512]{1,0:T(8,128)(2,1)S(1)}, bf16[512,512]{1,0:T(8,128)(2,1)S(1)}, u32[]{:S(2)}, u32[]{:S(2)}) collective-permute-start(bf16[512,512]{1,0:T(8,128)(2,1)S(1)} %pack.2.heads_ref), channel_id=1, source_target_pairs={{0,16},{16,0},{1,17},{17,1},{2,18},{18,2},{3,19},{19,3},{4,20},{20... | collective-permute-start | bytes 1572872 | tf_op jit(solution)/shard_map/ppermute | solution.py:452
  46.9 15.3 %all-to-all-start.1 = ((bf16[16,32,448]{2,1,0:T(8,128)(2,1)}), bf16[16,32,448]{2,1,0:T(8,128)(2,1)}, u32[]{:S(2)}, u32[]{:S(2)}) async-start(bf16[16,32,448]{2,1,0:T(8,128)(2,1)} %bitcast.6), calls=%async_computation.1 | async-start | bytes 1048576 | tf_op jit(solution)/shard_map/all_to_all | solution.py:448
  51.2 29.9 %collective-permute-start.9 = (bf16[448,1152]{1,0:T(8,128)(2,1)S(1)}, bf16[448,1152]{1,0:T(8,128)(2,1)S(1)}, u32[]{:S(2)}, u32[]{:S(2)}) collective-permute-start(bf16[448,1152]{1,0:T(8,128)(2,1)S(1)} %copy-done.3), channel_id=1, source_target_pairs={{0,16},{16,0},{1,17},{17,1},{2,18},{18,2},{3,19},{19,3},{4,20},{20... | collective-permute-start | bytes 3096584 | tf_op jit(solution)/shard_map/ppermute | solution.py:452
  51.7 29.5 %collective-permute-start.10 = (bf16[448,1152]{1,0:T(8,128)(2,1)}, bf16[448,1152]{1,0:T(8,128)(2,1)S(1)}, u32[]{:S(2)}, u32[]{:S(2)}) collective-permute-start(bf16[448,1152]{1,0:T(8,128)(2,1)} %u_ref.1), channel_id=1, source_target_pairs={{0,16},{16,0},{1,17},{17,1},{2,18},{18,2},{3,19},{19,3},{4,20},{20... | collective-permute-start | bytes 3096584 | tf_op jit(solution)/shard_map/ppermute | solution.py:452
  62.2 18.0 %copy-start.4 = (bf16[448,1152]{1,0:T(8,128)(2,1)S(1)}, bf16[448,1152]{1,0:T(8,128)(2,1)}, u32[]{:S(2)}) copy-start(bf16[448,1152]{1,0:T(8,128)(2,1)} %u_ref.1) | copy-start | bytes 3096580
  62.2 1.1 copy-start.5
  78.0 3.7 %collective-permute-start.8 = (bf16[512,512]{1,0:T(8,128)(2,1)S(1)}, bf16[512,512]{1,0:T(8,128)(2,1)S(1)}, u32[]{:S(2)}, u32[]{:S(2)}) collective-permute-start(bf16[512,512]{1,0:T(8,128)(2,1)S(1)} %bitcast.12), channel_id=1, source_target_pairs={{0,16},{16,0},{1,17},{17,1},{2,18},{18,2},{3,19},{19,3},{4,20},{20... | collective-permute-start | bytes 1572872 | tf_op jit(solution)/shard_map/ppermute | solution.py:452
  82.5 43.8 %copy-start = (bf16[1152,448]{0,1:T(8,128)(2,1)S(1)}, bf16[1152,448]{0,1:T(8,128)(2,1)}, u32[]{:S(2)}) copy-start(bf16[1152,448]{0,1:T(8,128)(2,1)} %param.23) | copy-start | bytes 3096580
  82.5 13.6 %collective-permute-start.11 = (bf16[1184,128]{1,0:T(8,128)(2,1)S(1)}, bf16[1184,128]{1,0:T(8,128)(2,1)S(1)}, u32[]{:S(2)}, u32[]{:S(2)}) collective-permute-start(bf16[1184,128]{1,0:T(8,128)(2,1)S(1)} %get-tuple-element.15), channel_id=1, source_target_pairs={{0,224},{32,0},{64,32},{96,64},{128,96},{160,128},{192,160},{224,1... | collective-permute-start | bytes 909320 | tf_op jit(solution)/shard_map/ppermute | solution.py:456
  85.0 11.1 %collective-permute-start.12 = (bf16[1184,128]{1,0:T(8,128)(2,1)S(1)}, bf16[1184,128]{1,0:T(8,128)(2,1)S(1)}, u32[]{:S(2)}, u32[]{:S(2)}) collective-permute-start(bf16[1184,128]{1,0:T(8,128)(2,1)S(1)} %get-tuple-element.16), channel_id=1, source_target_pairs={{0,32},{32,64},{64,96},{96,128},{128,160},{160,192},{192,224},{224... | collective-permute-start | bytes 909320 | tf_op jit(solution)/shard_map/ppermute | solution.py:456
  85.0 9.5 %collective-permute-start.13 = (bf16[304,128]{1,0:T(8,128)(2,1)S(1)}, bf16[304,128]{1,0:T(8,128)(2,1)S(1)}, u32[]{:S(2)}, u32[]{:S(2)}) collective-permute-start(bf16[304,128]{1,0:T(8,128)(2,1)S(1)} %get-tuple-element.17), channel_id=1, source_target_pairs={{0,192},{32,224},{64,0},{96,32},{128,64},{160,96},{192,128},{224,1... | collective-permute-start | bytes 233480 | tf_op jit(solution)/shard_map/ppermute | solution.py:456
  86.9 9.2 %collective-permute-start.14 = (bf16[304,128]{1,0:T(8,128)(2,1)S(1)}, bf16[304,128]{1,0:T(8,128)(2,1)S(1)}, u32[]{:S(2)}, u32[]{:S(2)}) collective-permute-start(bf16[304,128]{1,0:T(8,128)(2,1)S(1)} %get-tuple-element.18), channel_id=1, source_target_pairs={{0,64},{32,96},{64,128},{96,160},{128,192},{160,224},{192,0},{224,... | collective-permute-start | bytes 233480 | tf_op jit(solution)/shard_map/ppermute | solution.py:456
  96.3 8.0 %collective-permute-start.15 = (bf16[592,128]{1,0:T(8,128)(2,1)S(1)}, bf16[592,128]{1,0:T(8,128)(2,1)S(1)}, u32[]{:S(2)}, u32[]{:S(2)}) collective-permute-start(bf16[592,128]{1,0:T(8,128)(2,1)S(1)} %get-tuple-element.20), channel_id=1, source_target_pairs={{0,192},{32,224},{64,0},{96,32},{128,64},{160,96},{192,128},{224,1... | collective-permute-start | bytes 454664 | tf_op jit(solution)/shard_map/ppermute | solution.py:456
  99.0 6.3 %collective-permute-start.16 = (bf16[592,128]{1,0:T(8,128)(2,1)S(1)}, bf16[592,128]{1,0:T(8,128)(2,1)S(1)}, u32[]{:S(2)}, u32[]{:S(2)}) collective-permute-start(bf16[592,128]{1,0:T(8,128)(2,1)S(1)} %get-tuple-element.21), channel_id=1, source_target_pairs={{0,64},{32,96},{64,128},{96,160},{128,192},{160,224},{192,0},{224,... | collective-permute-start | bytes 454664 | tf_op jit(solution)/shard_map/ppermute | solution.py:456
  105.6 7.0 %collective-permute-start.20 = (bf16[288,128]{1,0:T(8,128)(2,1)S(1)}, bf16[288,128]{1,0:T(8,128)(2,1)S(1)}, u32[]{:S(2)}, u32[]{:S(2)}) collective-permute-start(bf16[288,128]{1,0:T(8,128)(2,1)S(1)} %hidden.1.refs_0_), channel_id=1, source_target_pairs={{0,64},{32,96},{64,128},{96,160},{128,192},{160,224},{192,0},{224,... | collective-permute-start | bytes 221192 | tf_op jit(solution)/shard_map/ppermute | solution.py:456
  109.8 5.6 %collective-permute-start.19 = (bf16[288,128]{1,0:T(8,128)(2,1)S(1)}, bf16[288,128]{1,0:T(8,128)(2,1)S(1)}, u32[]{:S(2)}, u32[]{:S(2)}) collective-permute-start(bf16[288,128]{1,0:T(8,128)(2,1)S(1)} %hidden.1.refs_0_), channel_id=1, source_target_pairs={{0,192},{32,224},{64,0},{96,32},{128,64},{160,96},{192,128},{224,1... | collective-permute-start | bytes 221192 | tf_op jit(solution)/shard_map/ppermute | solution.py:456
  109.8 8.2 %collective-permute-start.18 = (bf16[288,128]{1,0:T(8,128)(2,1)S(1)}, bf16[288,128]{1,0:T(8,128)(2,1)S(1)}, u32[]{:S(2)}, u32[]{:S(2)}) collective-permute-start(bf16[288,128]{1,0:T(8,128)(2,1)S(1)} %hidden.1.refs_0_), channel_id=1, source_target_pairs={{0,32},{32,64},{64,96},{96,128},{128,160},{160,192},{192,224},{224... | collective-permute-start | bytes 221192 | tf_op jit(solution)/shard_map/ppermute | solution.py:456
  111.5 6.5 %collective-permute-start.17 = (bf16[288,128]{1,0:T(8,128)(2,1)S(1)}, bf16[288,128]{1,0:T(8,128)(2,1)S(1)}, u32[]{:S(2)}, u32[]{:S(2)}) collective-permute-start(bf16[288,128]{1,0:T(8,128)(2,1)S(1)} %hidden.1.refs_0_), channel_id=1, source_target_pairs={{0,224},{32,0},{64,32},{96,64},{128,96},{160,128},{192,160},{224,1... | collective-permute-start | bytes 221192 | tf_op jit(solution)/shard_map/ppermute | solution.py:456
  112.5 5.5 %collective-permute-start.22 = (bf16[288,128]{1,0:T(8,128)(2,1)S(1)}, bf16[288,128]{1,0:T(8,128)(2,1)S(1)}, u32[]{:S(2)}, u32[]{:S(2)}) collective-permute-start(bf16[288,128]{1,0:T(8,128)(2,1)S(1)} %collective-permute-done.20.refs_4_), channel_id=1, source_target_pairs={{0,32},{32,64},{64,96},{96,128},{128,160},{160,192},{192,224},{224... | collective-permute-start | bytes 221192 | tf_op jit(solution)/shard_map/ppermute | solution.py:456
  115.5 6.5 %collective-permute-start.23 = (bf16[288,128]{1,0:T(8,128)(2,1)S(1)}, bf16[288,128]{1,0:T(8,128)(2,1)S(1)}, u32[]{:S(2)}, u32[]{:S(2)}) collective-permute-start(bf16[288,128]{1,0:T(8,128)(2,1)S(1)} %collective-permute-done.19.refs_3_), channel_id=1, source_target_pairs={{0,192},{32,224},{64,0},{96,32},{128,64},{160,96},{192,128},{224,1... | collective-permute-start | bytes 221192 | tf_op jit(solution)/shard_map/ppermute | solution.py:456
  116.6 5.4 %collective-permute-start.21 = (bf16[288,128]{1,0:T(8,128)(2,1)S(1)}, bf16[288,128]{1,0:T(8,128)(2,1)S(1)}, u32[]{:S(2)}, u32[]{:S(2)}) collective-permute-start(bf16[288,128]{1,0:T(8,128)(2,1)S(1)} %collective-permute-done.19.refs_3_), channel_id=1, source_target_pairs={{0,224},{32,0},{64,32},{96,64},{128,96},{160,128},{192,160},{224,1... | collective-permute-start | bytes 221192 | tf_op jit(solution)/shard_map/ppermute | solution.py:456
  122.0 5.9 %collective-permute-start.24 = (bf16[2304,128]{1,0:T(8,128)(2,1)S(1)}, bf16[2304,128]{1,0:T(8,128)(2,1)S(1)}, u32[]{:S(2)}, u32[]{:S(2)}) collective-permute-start(bf16[2304,128]{1,0:T(8,128)(2,1)S(1)} %pack.3), channel_id=1, source_target_pairs={{0,16},{16,0},{1,17},{17,1},{2,18},{18,2},{3,19},{19,3},{4,20},{20... | collective-permute-start | bytes 1769480 | tf_op jit(solution)/shard_map/ppermute | solution.py:452

commit v5 on v4

--- a/solution.py
+++ b/solution.py
@@ -157,35 +157,62 @@
 
 
 def project_kernel(turn, core_ref, z_ref, heads_ref, w_ref, *rest):
+    if turn == 0:
+        place_ref, res_hbm, out_ref, mine_ref, res_ref, sem = rest
+        count = mine_ref.shape[0]
+        group = LANES // count
+        lanes = pl.multiple_of(place_ref[0] // group * LANES, LANES)
+        copy = pltpu.make_async_copy(res_hbm.at[:, pl.ds(lanes, LANES)], res_ref, sem)
+        copy.start()
     half = core_ref[0] if turn == 0 else 1 - core_ref[0]
     rows = pl.ds(pl.multiple_of(half * 512, 512), 512)
     total = dot(heads_ref[...], w_ref[:, rows], ((1,), (1,)))
     if turn == 1:
         place_chunks(rest[1], z_ref[0], total + rest[0][...])
     else:
-        rest[0][...] = total
-
-
-def project(core, z, own, w_out, before=None):
-    turn = 0 if before is None else 1
-    return pl.pallas_call(
-        functools.partial(project_kernel, turn),
-        in_specs=[smem(), smem()] + whole(2 + turn),
-        out_specs=whole(1)[0],
-        out_shape=jax.ShapeDtypeStruct((512, w_out.shape[0]), BF16 if turn else F32),
+        out_ref[...] = total
+        copy.wait()
+        begin = lax.rem(place_ref[0], group) * count
+        shape = (count, LANES)
+        pick = (iota(shape, 1) == iota(shape, 0) + begin).astype(F32).astype(BF16)
+        mine_ref[...] = dot(pick, res_ref[...], ((1,), (1,))).astype(BF16)
+
+
+def project_first(core, z, own, w_out, place, residual):
+    cols = w_out.shape[0]
+    return pl.pallas_call(
+        functools.partial(project_kernel, 0),
+        in_specs=[smem(), smem()] + whole(2) + [smem(), pl.BlockSpec(memory_space=pltpu.HBM)],
+        out_specs=whole(2),
+        out_shape=[
+            jax.ShapeDtypeStruct((512, cols), F32),
+            jax.ShapeDtypeStruct((32, cols), BF16),
+        ],
+        scratch_shapes=[pltpu.VMEM((cols, LANES), BF16), pltpu.SemaphoreType.DMA],
         compiler_params=params(16),
         cost_estimate=cost(240_000_000, 2_000_000),
-        name="project" + "ab"[turn],
-    )(core, z, own, w_out, *([before] if turn else []))
-
-
-def middle_kernel(place_ref, parts_ref, res_ref, gain_ref, mid_ref, out_ref):
+        name="projecta",
+    )(core, z, own, w_out, place, residual)
+
+
+def project(core, z, other, w_out, before):
+    return pl.pallas_call(
+        functools.partial(project_kernel, 1),
+        in_specs=[smem(), smem()] + whole(3),
+        out_specs=whole(1)[0],
+        out_shape=jax.ShapeDtypeStruct((512, w_out.shape[0]), BF16),
+        compiler_params=params(16),
+        cost_estimate=cost(240_000_000, 2_000_000),
+        name="projectb",
+    )(core, z, other, w_out, before)
+
+
+def middle_kernel(parts_ref, res_ref, gain_ref, mid_ref, out_ref):
     rows, cols = mid_ref.shape
     total = parts_ref[0].astype(F32)
     for k in range(1, parts_ref.shape[0]):
         total = total + parts_ref[k].astype(F32)
-    res = res_ref[pl.ds(pl.multiple_of(place_ref[0] * rows, rows), rows), :]
-    mid = (res.astype(F32) + total).astype(BF16)
+    mid = (res_ref[...].astype(F32) + total).astype(BF16)
     mid_ref[...] = mid
     wide = mid.astype(F32)
     squares = jnp.sum(wide * wide, axis=1, keepdims=True)
@@ -198,11 +225,11 @@
         out_ref[k, :, cols:] = extra
 
 
-def middle(place, parts, residual, gain):
+def middle(parts, residual, gain):
     rows, cols = parts.shape[1:]
     return pl.pallas_call(
         middle_kernel,
-        in_specs=[smem()] + whole(3),
+        in_specs=whole(3),
         out_specs=whole(2),
         out_shape=[
             jax.ShapeDtypeStruct((rows, cols), BF16),
@@ -211,7 +238,7 @@
         compiler_params=params(16),
         cost_estimate=cost(2_500_000_000, 1_500_000),
         name="middle",
-    )(place, parts, residual, gain)
+    )(parts, residual, gain)
 
 
 def first_kernel(core_ref, own_ref, g_ref, u_ref, out_ref):
@@ -311,44 +338,37 @@
 BLOCK = 592
 TO_LOWER = ((7, 0, 64), (5, 0, 64))
 TO_UPPER = ((1, 0, 64), (3, 0, 64))
-TWO_LOWER = ((4, 0, 32),)
-TWO_UPPER = ((4, 32, 32),)
+TO_OPPOSITE = ((4, 0, 64),)
 TO_KEEP = ((0, 0, 64), (6, 0, 64), (2, 0, 64))
 
 
-def merge_kernel(keep_ref, above_ref, below_ref, far_above_ref, far_below_ref, stay_ref, down_ref, up_ref):
+def merge_kernel(core_ref, keep_ref, above_ref, below_ref, far_ref, stay_ref, down_ref, up_ref):
     def block(ref, k):
         return ref[k * BLOCK : (k + 1) * BLOCK].astype(F32)
 
     stay_ref[...] = block(keep_ref, 0) + block(above_ref, 0) + block(below_ref, 0)
-    for out_ref, k, full_ref, half_ref, shift in (
-        (down_ref, 1, above_ref, far_above_ref, 0),
-        (up_ref, 2, below_ref, far_below_ref, 32),
+    far = far_ref[...].astype(F32)
+    for out_ref, k, near_ref, goes in (
+        (down_ref, 1, above_ref, core_ref[0] == 1),
+        (up_ref, 2, below_ref, core_ref[0] == 0),
     ):
-        total = block(keep_ref, k) + block(full_ref, 1)
-        half = half_ref[...].astype(F32)
-        for j in range(9):
-            at = j * 64
-            out_ref[at + 32 - shift : at + 64 - shift] = total[
-                at + 32 - shift : at + 64 - shift
-            ].astype(BF16)
-            value = total[at + shift : at + shift + 32] + half[j * 32 : (j + 1) * 32]
-            out_ref[at + shift : at + shift + 32] = value.astype(BF16)
-        line = jnp.sum(total[576:592] + half[288:304], axis=0, keepdims=True)
-        out_ref[576:592] = tile_of(line, False).astype(BF16)
-
-
-def merge(*parts):
+        total = block(keep_ref, k) + block(near_ref, 1) + jnp.where(goes, far, 0.0)
+        out_ref[:576] = total[:576].astype(BF16)
+        line = jnp.sum(total[576:], axis=0, keepdims=True)
+        out_ref[576:] = tile_of(line, False).astype(BF16)
+
+
+def merge(core, *parts):
     shapes = [jax.ShapeDtypeStruct((BLOCK, LANES), kind) for kind in (F32, BF16, BF16)]
     return pl.pallas_call(
         merge_kernel,
-        in_specs=whole(5),
+        in_specs=[smem()] + whole(4),
         out_specs=whole(3),
         out_shape=shapes,
         compiler_params=params(16),
         cost_estimate=cost(5_000_000, 3_000_000),
         name="merge",
-    )(*parts)
+    )(core, *parts)
 
 
 def gated(gate, upper):
@@ -456,6 +476,11 @@
     return lax.ppermute(x, "z", [(i, (i + far) % 8) for i in range(8)])
 
 
+def part_ways(x):
+    pairs = [(2 * z + c, 2 * ((z + (2, 6)[c]) % 8) + c) for z in range(8) for c in range(2)]
+    return lax.ppermute(x, ("z", "core"), pairs)
+
+
 def gather(x):
     one_above, one_below = shift(x, 7), shift(x, 1)
     two_above, two_below = shift(x, 6), shift(x, 2)
@@ -490,18 +515,18 @@
     moved = exchange(context.reshape(32, 8, LAT), LAYER).reshape(256, LAT)
     flat = gather(heads(core, moved, w_uv))
     other = swap(flat)
-    part = project(core, height, flat, w_out.T)
+    part, mine = project_first(core, height, flat, w_out.T, place, residual.T)
     partial = project(core, height, other, w_out.T, part)
     parts = exchange(partial.reshape(16, 32, -1), HID)
-    mid, scaled = middle(place, parts, residual, norm_gain[None, :])
+    mid, scaled = middle(parts, mine, norm_gain[None, :])
     scaled = exchange(scaled, HID).reshape(512, 512)
     scaled_other = swap(scaled)
     part = first(core, scaled, w_gate, w_up)
     rest = (core, height, part, scaled, scaled_other, gate_other, up_other)
-    two_lower, two_upper, lower, upper = widen((TWO_LOWER, TWO_UPPER, TO_LOWER, TO_UPPER), BF16, *rest)
-    arrived = (shift(lower, 7), shift(upper, 1), shift(two_lower, 6), shift(two_upper, 2))
+    opposite, lower, upper = widen((TO_OPPOSITE, TO_LOWER, TO_UPPER), BF16, *rest)
+    arrived = (shift(lower, 7), shift(upper, 1), part_ways(opposite))
     (keep,) = widen((TO_KEEP,), F32, *rest)
-    stay, lower, upper = merge(keep, *arrived)
+    stay, lower, upper = merge(core, keep, *arrived)
     hidden = gather(make_hidden(stay, shift(lower, 6), shift(upper, 2)))
     other = swap(hidden).reshape(8, 288, LANES)
     part = down(core, height, hidden.reshape(8, 288, LANES), w_down.T)

time: 143 us -> 142 us (level)
  waiting for transfers between devices: 42.2 us -> 44.7 us
  local copies, waits for them, and re-layouts: 3.18 us -> 1.05 us
  starting transfers between devices: 54.9 us -> 53.2 us
    ppermute x0 -> x1, waiting for transfers between devices: none -> 8.43 us  [part_ways(): return lax.ppermute(x, ('z', 'core'), pairs)]
    ppermute x20 -> x18, waiting for transfers between devices: 22.9 us -> 15.8 us  [shift(): return lax.ppermute(x, 'z', [(i, (i + far) % 8) for i in range(8)])]
    ppermute x20 -> x18, starting transfers between devices: 31.4 us -> 27.7 us  [shift(): return lax.ppermute(x, 'z', [(i, (i + far) % 8) for i in range(8)])]
    all_to_all x2, waiting for transfers between devices: 16.6 us -> 18.9 us  [exchange(): return lax.all_to_all(x, axes, split_axis=0, concat_axis=0, tiled=True)]
    unnamed x15 -> x14, local copies, waits for them, and re-layouts: 3.18 us -> 1.04 us
    ppermute x0 -> x1, starting transfers between devices: none -> 1.94 us  [part_ways(): return lax.ppermute(x, ('z', 'core'), pairs)]
  transfers between devices with their start and end apart: 27 -> 26, of which waited for: 14 -> 13; matrix products, arithmetic and copies ran while one was open for 1% -> 0% of each run, Pallas kernels for 3% -> 3%
where the time goes in v5:
time: 142 us
  starting transfers between devices  53.2 us (37%)
  waiting for transfers between devices  44.7 us (31%)
  blocking collectives  26.9 us (19%)
  Pallas kernels  15.9 us (11%)
    ppermute x18, starting transfers between devices, shift(): return lax.ppermute(x, 'z', [(i, (i + far) % 8) for i in range(8)])  27.7 us
    all_to_all x2, blocking collectives, exchange(): return lax.all_to_all(x, axes, split_axis=0, concat_axis=0, tiled=True)  26.9 us
    all_to_all x2, waiting for transfers between devices, exchange(): return lax.all_to_all(x, axes, split_axis=0, concat_axis=0, tiled=True)  18.9 us
    ppermute x18, waiting for transfers between devices, shift(): return lax.ppermute(x, 'z', [(i, (i + far) % 8) for i in range(8)])  15.8 us
    all_to_all x2, starting transfers between devices, exchange(): return lax.all_to_all(x, axes, split_axis=0, concat_axis=0, tiled=True)  13 us
    ppermute x5, starting transfers between devices, swap(): return lax.ppermute(x, 'core', [(0, 1), (1, 0)])  10.6 us
    ppermute x1, waiting for transfers between devices, part_ways(): return lax.ppermute(x, ('z', 'core'), pairs)  8.43 us
    pallas_call x1, Pallas kernels, attend(): pl.pallas_call(attend_kernel, grid=(2,), in_specs=[pl.BlockSpec(idx.shape...  7.44 us
  transfers between devices with their start and end apart: 26, of which 13 were waited for; matrix products, arithmetic and copies ran while one was open for 0% of the time, Pallas kernels for 3%

profile of v5, /device:TPU:1, one launch (start us, length us, event | category | flops | bytes accessed | tf_op | source)
XLA Modules:
  0.0 141.9 jit_solution(10857750796433503149)
XLA Ops:
  0.0 7.4 %attend.1 = bf16[256,512]{1,0:T(8,128)(2,1)} custom-call(s32[2,2048]{1,0:T(2,128)} %idx_ref.1, bf16[2,128,512]{2,1,0:T(8,128)(2,1)} %ql_ref.1, bf16[2,64,128]{2,1,0:T(8,128)(2,1)} %qr_ref.1, bf16[2,3072,512]{2,1,0:T(8,128)(2,1)} %lat_ref.1, bf16[2,64,3072]{2,1,0:T(8,128)(2,1)} %rope_ref.1), custom_call_target="tpu_custom_call" | custom-call | flops 1800000000 | bytes 8000000 | tf_op jit(solution)/shard_map/attend/pallas_call | solution.py:92
  7.4 8.7 %all-to-all-start = ((bf16[32,8,512]{2,1,0:T(8,128)(2,1)}), bf16[32,8,512]{2,1,0:T(8,128)(2,1)S(1)}, u32[]{:S(2)}, u32[]{:S(2)}) async-start(bf16[32,8,512]{2,1,0:T(8,128)(2,1)} %bitcast.26), calls=%async_computation | async-start | bytes 524288 | tf_op jit(solution)/shard_map/all_to_all | solution.py:468
  16.2 8.3 %all-to-all-done = bf16[32,8,512]{2,1,0:T(8,128)(2,1)S(1)} async-done(((bf16[32,8,512]{2,1,0:T(8,128)(2,1)}), bf16[32,8,512]{2,1,0:T(8,128)(2,1)S(1)}, u32[]{:S(2)}, u32[]{:S(2)}) %all-to-all-start) | async-done | bytes 262176 | tf_op jit(solution)/shard_map/all_to_all | solution.py:468
  24.5 0.4 heads.1.refs_0_
  24.9 3.1 %collective-permute-start.3 = (bf16[64,512]{1,0:T(8,128)(2,1)S(1)}, bf16[64,512]{1,0:T(8,128)(2,1)S(1)}, u32[]{:S(2)}, u32[]{:S(2)}) collective-permute-start(bf16[64,512]{1,0:T(8,128)(2,1)S(1)} %heads.1.refs_0_), channel_id=1, source_target_pairs={{0,64},{32,96},{64,128},{96,160},{128,192},{160,224},{192,0},{224,... | collective-permute-start | bytes 196616 | tf_op jit(solution)/shard_map/ppermute | solution.py:476
  27.9 3.1 %collective-permute-start.2 = (bf16[64,512]{1,0:T(8,128)(2,1)S(1)}, bf16[64,512]{1,0:T(8,128)(2,1)S(1)}, u32[]{:S(2)}, u32[]{:S(2)}) collective-permute-start(bf16[64,512]{1,0:T(8,128)(2,1)S(1)} %heads.1.refs_0_), channel_id=1, source_target_pairs={{0,192},{32,224},{64,0},{96,32},{128,64},{160,96},{192,128},{224,1... | collective-permute-start | bytes 196616 | tf_op jit(solution)/shard_map/ppermute | solution.py:476
  31.1 0.7 collective-permute-start.1
  31.8 1.9 %collective-permute-start = (bf16[64,512]{1,0:T(8,128)(2,1)S(1)}, bf16[64,512]{1,0:T(8,128)(2,1)S(1)}, u32[]{:S(2)}, u32[]{:S(2)}) collective-permute-start(bf16[64,512]{1,0:T(8,128)(2,1)S(1)} %heads.1.refs_0_), channel_id=1, source_target_pairs={{0,224},{32,0},{64,32},{96,64},{128,96},{160,128},{192,160},{224,1... | collective-permute-start | bytes 196616 | tf_op jit(solution)/shard_map/ppermute | solution.py:476
  33.7 0.7 collective-permute-start.5
  34.4 0.3 collective-permute-done.2.refs_3_
  34.7 2.0 %collective-permute-start.6 = (bf16[64,512]{1,0:T(8,128)(2,1)S(1)}, bf16[64,512]{1,0:T(8,128)(2,1)S(1)}, u32[]{:S(2)}, u32[]{:S(2)}) collective-permute-start(bf16[64,512]{1,0:T(8,128)(2,1)S(1)} %collective-permute-done.2.refs_3_), channel_id=1, source_target_pairs={{0,192},{32,224},{64,0},{96,32},{128,64},{160,96},{192,128},{224,1... | collective-permute-start | bytes 196616 | tf_op jit(solution)/shard_map/ppermute | solution.py:476
  36.8 0.7 collective-permute-start.4
  37.4 0.6 collective-permute-done.5.refs_6_
  38.1 2.7 %collective-permute-done.6.refs_7_ = bf16[64,512]{1,0:T(8,128)(2,1)S(1)} collective-permute-done((bf16[64,512]{1,0:T(8,128)(2,1)S(1)}, bf16[64,512]{1,0:T(8,128)(2,1)S(1)}, u32[]{:S(2)}, u32[]{:S(2)}) %collective-permute-start.6) | collective-permute-done | bytes 65568 | tf_op jit(solution)/shard_map/ppermute | solution.py:476
  40.8 3.4 %collective-permute-start.7 = (bf16[512,512]{1,0:T(8,128)(2,1)S(1)}, bf16[512,512]{1,0:T(8,128)(2,1)S(1)}, u32[]{:S(2)}, u32[]{:S(2)}) collective-permute-start(bf16[512,512]{1,0:T(8,128)(2,1)S(1)} %pack.2.heads_ref), channel_id=1, source_target_pairs={{0,16},{16,0},{1,17},{17,1},{2,18},{18,2},{3,19},{19,3},{4,20},{20... | collective-permute-start | bytes 1572872 | tf_op jit(solution)/shard_map/ppermute | solution.py:472
  44.2 1.0 copy-done.5
  45.2 0.7 projecta.1
  45.9 1.3 projectb.1
  47.1 4.2 %all-to-all-start.1 = ((bf16[16,32,448]{2,1,0:T(8,128)(2,1)}), bf16[16,32,448]{2,1,0:T(8,128)(2,1)}, u32[]{:S(2)}, u32[]{:S(2)}) async-start(bf16[16,32,448]{2,1,0:T(8,128)(2,1)} %bitcast.7), calls=%async_computation.1 | async-start | bytes 1048576 | tf_op jit(solution)/shard_map/all_to_all | solution.py:468
  51.7 0.3 collective-permute-start.10
  52.0 10.6 %all-to-all-done.1.parts_ref = bf16[16,32,448]{2,1,0:T(8,128)(2,1)} async-done(((bf16[16,32,448]{2,1,0:T(8,128)(2,1)}), bf16[16,32,448]{2,1,0:T(8,128)(2,1)}, u32[]{:S(2)}, u32[]{:S(2)}) %all-to-all-start.1) | async-done | bytes 458784 | tf_op jit(solution)/shard_map/all_to_all | solution.py:468
  62.6 1.4 middle.1
  64.0 13.5 %all_to_all.20 = bf16[16,32,512]{2,1,0:T(8,128)(2,1)S(1)} all-to-all(bf16[16,32,512]{2,1,0:T(8,128)(2,1)S(1)} %get-tuple-element.17), channel_id=1, replica_groups=mesh['z'=8,'core'=2,'y'=4,'x'=4] {'y','x'}, dimensions={0} | all-to-all | bytes 1048576 | tf_op jit(solution)/shard_map/all_to_all | solution.py:468
  77.4 2.1 %collective-permute-start.8 = (bf16[512,512]{1,0:T(8,128)(2,1)S(1)}, bf16[512,512]{1,0:T(8,128)(2,1)S(1)}, u32[]{:S(2)}, u32[]{:S(2)}) collective-permute-start(bf16[512,512]{1,0:T(8,128)(2,1)S(1)} %bitcast.13), channel_id=1, source_target_pairs={{0,16},{16,0},{1,17},{17,1},{2,18},{18,2},{3,19},{19,3},{4,20},{20... | collective-permute-start | bytes 1572872 | tf_op jit(solution)/shard_map/ppermute | solution.py:472
  79.5 1.0 first.1.part_ref
  80.5 0.5 collective-permute-done.8.other_ref
  81.0 0.8 widen.3
  81.8 2.5 %collective-permute-start.11 = (bf16[1184,128]{1,0:T(8,128)(2,1)S(1)}, bf16[1184,128]{1,0:T(8,128)(2,1)S(1)}, u32[]{:S(2)}, u32[]{:S(2)}) collective-permute-start(bf16[1184,128]{1,0:T(8,128)(2,1)S(1)} %get-tuple-element.18), channel_id=1, source_target_pairs={{0,224},{32,0},{64,32},{96,64},{128,96},{160,128},{192,160},{224,1... | collective-permute-start | bytes 909320 | tf_op jit(solution)/shard_map/ppermute | solution.py:476
  84.3 1.9 %collective-permute-start.13 = (bf16[592,128]{1,0:T(8,128)(2,1)S(1)}, bf16[592,128]{1,0:T(8,128)(2,1)S(1)}, u32[]{:S(2)}, u32[]{:S(2)}) collective-permute-start(bf16[592,128]{1,0:T(8,128)(2,1)S(1)} %get-tuple-element.20), channel_id=1, source_target_pairs={{0,64},{16,208},{32,96},{48,240},{64,128},{80,16},{96,160},{112,48... | collective-permute-start | bytes 454664 | tf_op jit(solution)/shard_map/ppermute | solution.py:481
  86.3 0.6 widen.2.keep_ref
  86.9 8.4 %collective-permute-done.13.far_ref = bf16[592,128]{1,0:T(8,128)(2,1)S(1)} collective-permute-done((bf16[592,128]{1,0:T(8,128)(2,1)S(1)}, bf16[592,128]{1,0:T(8,128)(2,1)S(1)}, u32[]{:S(2)}, u32[]{:S(2)}) %collective-permute-start.13) | collective-permute-done | bytes 151584 | tf_op jit(solution)/shard_map/ppermute | solution.py:481
  95.5 3.4 %collective-permute-start.14 = (bf16[592,128]{1,0:T(8,128)(2,1)S(1)}, bf16[592,128]{1,0:T(8,128)(2,1)S(1)}, u32[]{:S(2)}, u32[]{:S(2)}) collective-permute-start(bf16[592,128]{1,0:T(8,128)(2,1)S(1)} %get-tuple-element.22), channel_id=1, source_target_pairs={{0,192},{32,224},{64,0},{96,32},{128,64},{160,96},{192,128},{224,1... | collective-permute-start | bytes 454664 | tf_op jit(solution)/shard_map/ppermute | solution.py:476
  98.9 0.6 collective-permute-start.15
  99.4 4.1 %collective-permute-done.14.above_ref = bf16[592,128]{1,0:T(8,128)(2,1)S(1)} collective-permute-done((bf16[592,128]{1,0:T(8,128)(2,1)S(1)}, bf16[592,128]{1,0:T(8,128)(2,1)S(1)}, u32[]{:S(2)}, u32[]{:S(2)}) %collective-permute-start.14) | collective-permute-done | bytes 151584 | tf_op jit(solution)/shard_map/ppermute | solution.py:476
  103.6 3.1 %collective-permute-done.15.below_ref = bf16[592,128]{1,0:T(8,128)(2,1)S(1)} collective-permute-done((bf16[592,128]{1,0:T(8,128)(2,1)S(1)}, bf16[592,128]{1,0:T(8,128)(2,1)S(1)}, u32[]{:S(2)}, u32[]{:S(2)}) %collective-permute-start.15) | collective-permute-done | bytes 151584 | tf_op jit(solution)/shard_map/ppermute | solution.py:476
  106.9 0.8 collective-permute-start.19
  107.7 2.8 %collective-permute-start.18 = (bf16[288,128]{1,0:T(8,128)(2,1)S(1)}, bf16[288,128]{1,0:T(8,128)(2,1)S(1)}, u32[]{:S(2)}, u32[]{:S(2)}) collective-permute-start(bf16[288,128]{1,0:T(8,128)(2,1)S(1)} %hidden.1.refs_0_), channel_id=1, source_target_pairs={{0,192},{32,224},{64,0},{96,32},{128,64},{160,96},{192,128},{224,1... | collective-permute-start | bytes 221192 | tf_op jit(solution)/shard_map/ppermute | solution.py:476
  110.5 2.7 %collective-permute-start.16 = (bf16[288,128]{1,0:T(8,128)(2,1)S(1)}, bf16[288,128]{1,0:T(8,128)(2,1)S(1)}, u32[]{:S(2)}, u32[]{:S(2)}) collective-permute-start(bf16[288,128]{1,0:T(8,128)(2,1)S(1)} %hidden.1.refs_0_), channel_id=1, source_target_pairs={{0,224},{32,0},{64,32},{96,64},{128,96},{160,128},{192,160},{224,1... | collective-permute-start | bytes 221192 | tf_op jit(solution)/shard_map/ppermute | solution.py:476
  113.2 2.7 %collective-permute-start.22 = (bf16[288,128]{1,0:T(8,128)(2,1)S(1)}, bf16[288,128]{1,0:T(8,128)(2,1)S(1)}, u32[]{:S(2)}, u32[]{:S(2)}) collective-permute-start(bf16[288,128]{1,0:T(8,128)(2,1)S(1)} %collective-permute-done.18.refs_3_), channel_id=1, source_target_pairs={{0,192},{32,224},{64,0},{96,32},{128,64},{160,96},{192,128},{224,1... | collective-permute-start | bytes 221192 | tf_op jit(solution)/shard_map/ppermute | solution.py:476
  115.9 1.8 %collective-permute-done.21.refs_6_ = bf16[288,128]{1,0:T(8,128)(2,1)S(1)} collective-permute-done((bf16[288,128]{1,0:T(8,128)(2,1)S(1)}, bf16[288,128]{1,0:T(8,128)(2,1)S(1)}, u32[]{:S(2)}, u32[]{:S(2)}) %collective-permute-start.21) | collective-permute-done | bytes 73760 | tf_op jit(solution)/shard_map/ppermute | solution.py:476
  117.8 1.7 %collective-permute-done.22.refs_7_ = bf16[288,128]{1,0:T(8,128)(2,1)S(1)} collective-permute-done((bf16[288,128]{1,0:T(8,128)(2,1)S(1)}, bf16[288,128]{1,0:T(8,128)(2,1)S(1)}, u32[]{:S(2)}, u32[]{:S(2)}) %collective-permute-start.22) | collective-permute-done | bytes 73760 | tf_op jit(solution)/shard_map/ppermute | solution.py:476
  119.4 1.4 %collective-permute-done.20.refs_5_ = bf16[288,128]{1,0:T(8,128)(2,1)S(1)} collective-permute-done((bf16[288,128]{1,0:T(8,128)(2,1)S(1)}, bf16[288,128]{1,0:T(8,128)(2,1)S(1)}, u32[]{:S(2)}, u32[]{:S(2)}) %collective-permute-start.20) | collective-permute-done | bytes 73760 | tf_op jit(solution)/shard_map/ppermute | solution.py:476
  120.9 4.6 %collective-permute-start.23 = (bf16[2304,128]{1,0:T(8,128)(2,1)S(1)}, bf16[2304,128]{1,0:T(8,128)(2,1)S(1)}, u32[]{:S(2)}, u32[]{:S(2)}) collective-permute-start(bf16[2304,128]{1,0:T(8,128)(2,1)S(1)} %pack.3), channel_id=1, source_target_pairs={{0,16},{16,0},{1,17},{17,1},{2,18},{18,2},{3,19},{19,3},{4,20},{20... | collective-permute-start | bytes 1769480 | tf_op jit(solution)/shard_map/ppermute | solution.py:472
  125.5 0.6 downa.1.rest_0_
  126.1 1.0 collective-permute-done.23
  127.1 0.7 downb.1
  127.8 13.4 %all_to_all.21.parts_ref = bf16[16,32,448]{2,1,0:T(8,128)(2,1)S(1)} all-to-all(bf16[16,32,448]{2,1,0:T(8,128)(2,1)S(1)} %bitcast.22), channel_id=1, replica_groups=mesh['z'=8,'core'=2,'y'=4,'x'=4] {'y','x'}, dimensions={0} | all-to-all | bytes 917504 | tf_op jit(solution)/shard_map/all_to_all | solution.py:468
  141.2 0.7 last.1
  (36 shorter events, 0.9 us)
Async XLA Ops:
  0.0 24.5 %copy-start.2 = (bf16[8,512,128]{2,1,0:T(8,128)(2,1)S(1)}, bf16[8,512,128]{2,1,0:T(8,128)(2,1)}, u32[]{:S(2)}) copy-start(bf16[8,512,128]{2,1,0:T(8,128)(2,1)} %w_ref.1) | copy-start | bytes 3145732
  0.0 44.1 %copy-start.1 = (bf16[1024,448]{0,1:T(8,128)(2,1)S(1)}, bf16[1024,448]{0,1:T(8,128)(2,1)}, u32[]{:S(2)}) copy-start(bf16[1024,448]{0,1:T(8,128)(2,1)} %param.18) | copy-start | bytes 2752516
  7.4 43.9 %copy-start.3 = (bf16[448,1152]{1,0:T(8,128)(2,1)S(1)}, bf16[448,1152]{1,0:T(8,128)(2,1)}, u32[]{:S(2)}) copy-start(bf16[448,1152]{1,0:T(8,128)(2,1)} %g_ref.1) | copy-start | bytes 3096580
  7.4 44.5 %copy-start.6 = (bf16[448]{0:T(512)(128)(2,1)S(1)}, bf16[448]{0:T(512)(128)(2,1)}, u32[]{:S(2)}) copy-start(bf16[448]{0:T(512)(128)(2,1)} %param.20) | copy-start | bytes 2692
  7.4 17.0 %all-to-all-start = ((bf16[32,8,512]{2,1,0:T(8,128)(2,1)}), bf16[32,8,512]{2,1,0:T(8,128)(2,1)S(1)}, u32[]{:S(2)}, u32[]{:S(2)}) async-start(bf16[32,8,512]{2,1,0:T(8,128)(2,1)} %bitcast.26), calls=%async_computation | async-start | bytes 524288 | tf_op jit(solution)/shard_map/all_to_all | solution.py:468
  24.9 8.9 %collective-permute-start.3 = (bf16[64,512]{1,0:T(8,128)(2,1)S(1)}, bf16[64,512]{1,0:T(8,128)(2,1)S(1)}, u32[]{:S(2)}, u32[]{:S(2)}) collective-permute-start(bf16[64,512]{1,0:T(8,128)(2,1)S(1)} %heads.1.refs_0_), channel_id=1, source_target_pairs={{0,64},{32,96},{64,128},{96,160},{128,192},{160,224},{192,0},{224,... | collective-permute-start | bytes 196616 | tf_op jit(solution)/shard_map/ppermute | solution.py:476
  27.9 6.8 %collective-permute-start.2 = (bf16[64,512]{1,0:T(8,128)(2,1)S(1)}, bf16[64,512]{1,0:T(8,128)(2,1)S(1)}, u32[]{:S(2)}, u32[]{:S(2)}) collective-permute-start(bf16[64,512]{1,0:T(8,128)(2,1)S(1)} %heads.1.refs_0_), channel_id=1, source_target_pairs={{0,192},{32,224},{64,0},{96,32},{128,64},{160,96},{192,128},{224,1... | collective-permute-start | bytes 196616 | tf_op jit(solution)/shard_map/ppermute | solution.py:476
  31.1 6.4 %collective-permute-start.1 = (bf16[64,512]{1,0:T(8,128)(2,1)S(1)}, bf16[64,512]{1,0:T(8,128)(2,1)S(1)}, u32[]{:S(2)}, u32[]{:S(2)}) collective-permute-start(bf16[64,512]{1,0:T(8,128)(2,1)S(1)} %heads.1.refs_0_), channel_id=1, source_target_pairs={{0,32},{32,64},{64,96},{96,128},{128,160},{160,192},{192,224},{224... | collective-permute-start | bytes 196616 | tf_op jit(solution)/shard_map/ppermute | solution.py:476
  31.8 5.7 %collective-permute-start = (bf16[64,512]{1,0:T(8,128)(2,1)S(1)}, bf16[64,512]{1,0:T(8,128)(2,1)S(1)}, u32[]{:S(2)}, u32[]{:S(2)}) collective-permute-start(bf16[64,512]{1,0:T(8,128)(2,1)S(1)} %heads.1.refs_0_), channel_id=1, source_target_pairs={{0,224},{32,0},{64,32},{96,64},{128,96},{160,128},{192,160},{224,1... | collective-permute-start | bytes 196616 | tf_op jit(solution)/shard_map/ppermute | solution.py:476
  33.7 4.3 %collective-permute-start.5 = (bf16[64,512]{1,0:T(8,128)(2,1)S(1)}, bf16[64,512]{1,0:T(8,128)(2,1)S(1)}, u32[]{:S(2)}, u32[]{:S(2)}) collective-permute-start(bf16[64,512]{1,0:T(8,128)(2,1)S(1)} %collective-permute-done.3.refs_4_), channel_id=1, source_target_pairs={{0,32},{32,64},{64,96},{96,128},{128,160},{160,192},{192,224},{224... | collective-permute-start | bytes 196616 | tf_op jit(solution)/shard_map/ppermute | solution.py:476
  34.7 6.0 %collective-permute-start.6 = (bf16[64,512]{1,0:T(8,128)(2,1)S(1)}, bf16[64,512]{1,0:T(8,128)(2,1)S(1)}, u32[]{:S(2)}, u32[]{:S(2)}) collective-permute-start(bf16[64,512]{1,0:T(8,128)(2,1)S(1)} %collective-permute-done.2.refs_3_), channel_id=1, source_target_pairs={{0,192},{32,224},{64,0},{96,32},{128,64},{160,96},{192,128},{224,1... | collective-permute-start | bytes 196616 | tf_op jit(solution)/shard_map/ppermute | solution.py:476
  36.8 4.0 %collective-permute-start.4 = (bf16[64,512]{1,0:T(8,128)(2,1)S(1)}, bf16[64,512]{1,0:T(8,128)(2,1)S(1)}, u32[]{:S(2)}, u32[]{:S(2)}) collective-permute-start(bf16[64,512]{1,0:T(8,128)(2,1)S(1)} %collective-permute-done.2.refs_3_), channel_id=1, source_target_pairs={{0,224},{32,0},{64,32},{96,64},{128,96},{160,128},{192,160},{224,1... | collective-permute-start | bytes 196616 | tf_op jit(solution)/shard_map/ppermute | solution.py:476
  40.8 5.1 %collective-permute-start.7 = (bf16[512,512]{1,0:T(8,128)(2,1)S(1)}, bf16[512,512]{1,0:T(8,128)(2,1)S(1)}, u32[]{:S(2)}, u32[]{:S(2)}) collective-permute-start(bf16[512,512]{1,0:T(8,128)(2,1)S(1)} %pack.2.heads_ref), channel_id=1, source_target_pairs={{0,16},{16,0},{1,17},{17,1},{2,18},{18,2},{3,19},{19,3},{4,20},{20... | collective-permute-start | bytes 1572872 | tf_op jit(solution)/shard_map/ppermute | solution.py:472
  44.2 1.0 copy-start.5
  47.1 15.4 %all-to-all-start.1 = ((bf16[16,32,448]{2,1,0:T(8,128)(2,1)}), bf16[16,32,448]{2,1,0:T(8,128)(2,1)}, u32[]{:S(2)}, u32[]{:S(2)}) async-start(bf16[16,32,448]{2,1,0:T(8,128)(2,1)} %bitcast.7), calls=%async_computation.1 | async-start | bytes 1048576 | tf_op jit(solution)/shard_map/all_to_all | solution.py:468
  51.4 29.1 %collective-permute-start.9 = (bf16[448,1152]{1,0:T(8,128)(2,1)S(1)}, bf16[448,1152]{1,0:T(8,128)(2,1)S(1)}, u32[]{:S(2)}, u32[]{:S(2)}) collective-permute-start(bf16[448,1152]{1,0:T(8,128)(2,1)S(1)} %copy-done.3), channel_id=1, source_target_pairs={{0,16},{16,0},{1,17},{17,1},{2,18},{18,2},{3,19},{19,3},{4,20},{20... | collective-permute-start | bytes 3096584 | tf_op jit(solution)/shard_map/ppermute | solution.py:472
  51.7 28.8 %collective-permute-start.10 = (bf16[448,1152]{1,0:T(8,128)(2,1)}, bf16[448,1152]{1,0:T(8,128)(2,1)S(1)}, u32[]{:S(2)}, u32[]{:S(2)}) collective-permute-start(bf16[448,1152]{1,0:T(8,128)(2,1)} %u_ref.1), channel_id=1, source_target_pairs={{0,16},{16,0},{1,17},{17,1},{2,18},{18,2},{3,19},{19,3},{4,20},{20... | collective-permute-start | bytes 3096584 | tf_op jit(solution)/shard_map/ppermute | solution.py:472
  62.6 16.9 %copy-start.4 = (bf16[448,1152]{1,0:T(8,128)(2,1)S(1)}, bf16[448,1152]{1,0:T(8,128)(2,1)}, u32[]{:S(2)}) copy-start(bf16[448,1152]{1,0:T(8,128)(2,1)} %u_ref.1) | copy-start | bytes 3096580
  77.4 3.6 %collective-permute-start.8 = (bf16[512,512]{1,0:T(8,128)(2,1)S(1)}, bf16[512,512]{1,0:T(8,128)(2,1)S(1)}, u32[]{:S(2)}, u32[]{:S(2)}) collective-permute-start(bf16[512,512]{1,0:T(8,128)(2,1)S(1)} %bitcast.13), channel_id=1, source_target_pairs={{0,16},{16,0},{1,17},{17,1},{2,18},{18,2},{3,19},{19,3},{4,20},{20... | collective-permute-start | bytes 1572872 | tf_op jit(solution)/shard_map/ppermute | solution.py:472
  81.8 43.6 %copy-start = (bf16[1152,448]{0,1:T(8,128)(2,1)S(1)}, bf16[1152,448]{0,1:T(8,128)(2,1)}, u32[]{:S(2)}) copy-start(bf16[1152,448]{0,1:T(8,128)(2,1)} %param.23) | copy-start | bytes 3096580
  81.8 13.5 %collective-permute-start.11 = (bf16[1184,128]{1,0:T(8,128)(2,1)S(1)}, bf16[1184,128]{1,0:T(8,128)(2,1)S(1)}, u32[]{:S(2)}, u32[]{:S(2)}) collective-permute-start(bf16[1184,128]{1,0:T(8,128)(2,1)S(1)} %get-tuple-element.18), channel_id=1, source_target_pairs={{0,224},{32,0},{64,32},{96,64},{128,96},{160,128},{192,160},{224,1... | collective-permute-start | bytes 909320 | tf_op jit(solution)/shard_map/ppermute | solution.py:476
  84.3 11.0 %collective-permute-start.12 = (bf16[1184,128]{1,0:T(8,128)(2,1)S(1)}, bf16[1184,128]{1,0:T(8,128)(2,1)S(1)}, u32[]{:S(2)}, u32[]{:S(2)}) collective-permute-start(bf16[1184,128]{1,0:T(8,128)(2,1)S(1)} %get-tuple-element.19), channel_id=1, source_target_pairs={{0,32},{32,64},{64,96},{96,128},{128,160},{160,192},{192,224},{224... | collective-permute-start | bytes 909320 | tf_op jit(solution)/shard_map/ppermute | solution.py:476
  84.3 11.0 %collective-permute-start.13 = (bf16[592,128]{1,0:T(8,128)(2,1)S(1)}, bf16[592,128]{1,0:T(8,128)(2,1)S(1)}, u32[]{:S(2)}, u32[]{:S(2)}) collective-permute-start(bf16[592,128]{1,0:T(8,128)(2,1)S(1)} %get-tuple-element.20), channel_id=1, source_target_pairs={{0,64},{16,208},{32,96},{48,240},{64,128},{80,16},{96,160},{112,48... | collective-permute-start | bytes 454664 | tf_op jit(solution)/shard_map/ppermute | solution.py:481
  95.5 8.1 %collective-permute-start.14 = (bf16[592,128]{1,0:T(8,128)(2,1)S(1)}, bf16[592,128]{1,0:T(8,128)(2,1)S(1)}, u32[]{:S(2)}, u32[]{:S(2)}) collective-permute-start(bf16[592,128]{1,0:T(8,128)(2,1)S(1)} %get-tuple-element.22), channel_id=1, source_target_pairs={{0,192},{32,224},{64,0},{96,32},{128,64},{160,96},{192,128},{224,1... | collective-permute-start | bytes 454664 | tf_op jit(solution)/shard_map/ppermute | solution.py:476
  98.9 7.8 %collective-permute-start.15 = (bf16[592,128]{1,0:T(8,128)(2,1)S(1)}, bf16[592,128]{1,0:T(8,128)(2,1)S(1)}, u32[]{:S(2)}, u32[]{:S(2)}) collective-permute-start(bf16[592,128]{1,0:T(8,128)(2,1)S(1)} %get-tuple-element.23), channel_id=1, source_target_pairs={{0,64},{32,96},{64,128},{96,160},{128,192},{160,224},{192,0},{224,... | collective-permute-start | bytes 454664 | tf_op jit(solution)/shard_map/ppermute | solution.py:476
  106.9 6.3 %collective-permute-start.19 = (bf16[288,128]{1,0:T(8,128)(2,1)S(1)}, bf16[288,128]{1,0:T(8,128)(2,1)S(1)}, u32[]{:S(2)}, u32[]{:S(2)}) collective-permute-start(bf16[288,128]{1,0:T(8,128)(2,1)S(1)} %hidden.1.refs_0_), channel_id=1, source_target_pairs={{0,64},{32,96},{64,128},{96,160},{128,192},{160,224},{192,0},{224,... | collective-permute-start | bytes 221192 | tf_op jit(solution)/shard_map/ppermute | solution.py:476
  107.7 5.5 %collective-permute-start.18 = (bf16[288,128]{1,0:T(8,128)(2,1)S(1)}, bf16[288,128]{1,0:T(8,128)(2,1)S(1)}, u32[]{:S(2)}, u32[]{:S(2)}) collective-permute-start(bf16[288,128]{1,0:T(8,128)(2,1)S(1)} %hidden.1.refs_0_), channel_id=1, source_target_pairs={{0,192},{32,224},{64,0},{96,32},{128,64},{160,96},{192,128},{224,1... | collective-permute-start | bytes 221192 | tf_op jit(solution)/shard_map/ppermute | solution.py:476
  110.5 5.4 %collective-permute-start.17 = (bf16[288,128]{1,0:T(8,128)(2,1)S(1)}, bf16[288,128]{1,0:T(8,128)(2,1)S(1)}, u32[]{:S(2)}, u32[]{:S(2)}) collective-permute-start(bf16[288,128]{1,0:T(8,128)(2,1)S(1)} %hidden.1.refs_0_), channel_id=1, source_target_pairs={{0,32},{32,64},{64,96},{96,128},{128,160},{160,192},{192,224},{224... | collective-permute-start | bytes 221192 | tf_op jit(solution)/shard_map/ppermute | solution.py:476
  110.5 5.4 %collective-permute-start.16 = (bf16[288,128]{1,0:T(8,128)(2,1)S(1)}, bf16[288,128]{1,0:T(8,128)(2,1)S(1)}, u32[]{:S(2)}, u32[]{:S(2)}) collective-permute-start(bf16[288,128]{1,0:T(8,128)(2,1)S(1)} %hidden.1.refs_0_), channel_id=1, source_target_pairs={{0,224},{32,0},{64,32},{96,64},{128,96},{160,128},{192,160},{224,1... | collective-permute-start | bytes 221192 | tf_op jit(solution)/shard_map/ppermute | solution.py:476
  113.2 4.5 %collective-permute-start.21 = (bf16[288,128]{1,0:T(8,128)(2,1)S(1)}, bf16[288,128]{1,0:T(8,128)(2,1)S(1)}, u32[]{:S(2)}, u32[]{:S(2)}) collective-permute-start(bf16[288,128]{1,0:T(8,128)(2,1)S(1)} %collective-permute-done.19.refs_4_), channel_id=1, source_target_pairs={{0,32},{32,64},{64,96},{96,128},{128,160},{160,192},{192,224},{224... | collective-permute-start | bytes 221192 | tf_op jit(solution)/shard_map/ppermute | solution.py:476
  113.2 6.2 %collective-permute-start.22 = (bf16[288,128]{1,0:T(8,128)(2,1)S(1)}, bf16[288,128]{1,0:T(8,128)(2,1)S(1)}, u32[]{:S(2)}, u32[]{:S(2)}) collective-permute-start(bf16[288,128]{1,0:T(8,128)(2,1)S(1)} %collective-permute-done.18.refs_3_), channel_id=1, source_target_pairs={{0,192},{32,224},{64,0},{96,32},{128,64},{160,96},{192,128},{224,1... | collective-permute-start | bytes 221192 | tf_op jit(solution)/shard_map/ppermute | solution.py:476
  115.9 5.0 %collective-permute-start.20 = (bf16[288,128]{1,0:T(8,128)(2,1)S(1)}, bf16[288,128]{1,0:T(8,128)(2,1)S(1)}, u32[]{:S(2)}, u32[]{:S(2)}) collective-permute-start(bf16[288,128]{1,0:T(8,128)(2,1)S(1)} %collective-permute-done.18.refs_3_), channel_id=1, source_target_pairs={{0,224},{32,0},{64,32},{96,64},{128,96},{160,128},{192,160},{224,1... | collective-permute-start | bytes 221192 | tf_op jit(solution)/shard_map/ppermute | solution.py:476
  120.9 6.2 %collective-permute-start.23 = (bf16[2304,128]{1,0:T(8,128)(2,1)S(1)}, bf16[2304,128]{1,0:T(8,128)(2,1)S(1)}, u32[]{:S(2)}, u32[]{:S(2)}) collective-permute-start(bf16[2304,128]{1,0:T(8,128)(2,1)S(1)} %pack.3), channel_id=1, source_target_pairs={{0,16},{16,0},{1,17},{17,1},{2,18},{18,2},{3,19},{19,3},{4,20},{20... | collective-permute-start | bytes 1769480 | tf_op jit(solution)/shard_map/ppermute | solution.py:472

commit v6 on v5

--- a/solution.py
+++ b/solution.py
@@ -485,7 +485,7 @@
     one_above, one_below = shift(x, 7), shift(x, 1)
     two_above, two_below = shift(x, 6), shift(x, 2)
     three_above, three_below = shift(two_above, 7), shift(two_below, 1)
-    opposite = shift(two_above, 6)
+    opposite = part_ways(jnp.where(lax.axis_index("core") == 0, two_below, two_above))
     return pack(
         [x, one_above, one_below, two_above, two_below, three_above, three_below, opposite]
     )

time: 142 us -> 141 us (level)
  starting transfers between devices: 53.2 us -> 49.4 us
  waiting for transfers between devices: 44.7 us -> 46.7 us
    ppermute x1 -> x3, waiting for transfers between devices: 8.43 us -> 15.4 us  [part_ways(): return lax.ppermute(x, ('z', 'core'), pairs)]
    ppermute x18 -> x16, starting transfers between devices: 27.7 us -> 21.1 us  [shift(): return lax.ppermute(x, 'z', [(i, (i + far) % 8) for i in range(8)])]
    ppermute x18 -> x16, waiting for transfers between devices: 15.8 us -> 10.9 us  [shift(): return lax.ppermute(x, 'z', [(i, (i + far) % 8) for i in range(8)])]
    ppermute x1 -> x3, starting transfers between devices: 1.94 us -> 5.11 us  [part_ways(): return lax.ppermute(x, ('z', 'core'), pairs)]
  transfers between devices with their start and end apart: 26 -> 26, of which waited for: 13 -> 14; matrix products, arithmetic and copies ran while one was open for 0% -> 0% of each run, Pallas kernels for 3% -> 3%
where the time goes in v6:
time: 141 us; the launch traced here: 140 us
  starting transfers between devices  49.4 us (35%)
  waiting for transfers between devices  46.7 us (33%)
  blocking collectives  26.9 us (19%)
  Pallas kernels  15.9 us (11%)
    all_to_all x2, blocking collectives, exchange(): return lax.all_to_all(x, axes, split_axis=0, concat_axis=0, tiled=True)  26.9 us
    ppermute x16, starting transfers between devices, shift(): return lax.ppermute(x, 'z', [(i, (i + far) % 8) for i in range(8)])  21.1 us
    all_to_all x2, waiting for transfers between devices, exchange(): return lax.all_to_all(x, axes, split_axis=0, concat_axis=0, tiled=True)  18.9 us
    ppermute x3, waiting for transfers between devices, part_ways(): return lax.ppermute(x, ('z', 'core'), pairs)  15.4 us
    all_to_all x2, starting transfers between devices, exchange(): return lax.all_to_all(x, axes, split_axis=0, concat_axis=0, tiled=True)  13 us
    ppermute x16, waiting for transfers between devices, shift(): return lax.ppermute(x, 'z', [(i, (i + far) % 8) for i in range(8)])  10.9 us
    ppermute x5, starting transfers between devices, swap(): return lax.ppermute(x, 'core', [(0, 1), (1, 0)])  10.3 us
    pallas_call x1, Pallas kernels, attend(): pl.pallas_call(attend_kernel, grid=(2,), in_specs=[pl.BlockSpec(idx.shape...  7.44 us
  transfers between devices with their start and end apart: 26, of which 14 were waited for; matrix products, arithmetic and copies ran while one was open for 0% of the time, Pallas kernels for 3%

profile of v6, /device:TPU:1, one launch (start us, length us, event | category | flops | bytes accessed | tf_op | source)
XLA Modules:
  0.0 140.2 jit_solution(18178684092731978487)
XLA Ops:
  0.0 7.4 %attend.1 = bf16[256,512]{1,0:T(8,128)(2,1)} custom-call(s32[2,2048]{1,0:T(2,128)} %idx_ref.1, bf16[2,128,512]{2,1,0:T(8,128)(2,1)} %ql_ref.1, bf16[2,64,128]{2,1,0:T(8,128)(2,1)} %qr_ref.1, bf16[2,3072,512]{2,1,0:T(8,128)(2,1)} %lat_ref.1, bf16[2,64,3072]{2,1,0:T(8,128)(2,1)} %rope_ref.1), custom_call_target="tpu_custom_call" | custom-call | flops 1800000000 | bytes 8000000 | tf_op jit(solution)/shard_map/attend/pallas_call | solution.py:92
  7.4 8.7 %all-to-all-start = ((bf16[32,8,512]{2,1,0:T(8,128)(2,1)}), bf16[32,8,512]{2,1,0:T(8,128)(2,1)S(1)}, u32[]{:S(2)}, u32[]{:S(2)}) async-start(bf16[32,8,512]{2,1,0:T(8,128)(2,1)} %bitcast.26), calls=%async_computation | async-start | bytes 524288 | tf_op jit(solution)/shard_map/all_to_all | solution.py:468
  16.2 8.3 %all-to-all-done = bf16[32,8,512]{2,1,0:T(8,128)(2,1)S(1)} async-done(((bf16[32,8,512]{2,1,0:T(8,128)(2,1)}), bf16[32,8,512]{2,1,0:T(8,128)(2,1)S(1)}, u32[]{:S(2)}, u32[]{:S(2)}) %all-to-all-start) | async-done | bytes 262176 | tf_op jit(solution)/shard_map/all_to_all | solution.py:468
  24.5 0.4 heads.1.refs_0_
  24.9 3.1 %collective-permute-start.3 = (bf16[64,512]{1,0:T(8,128)(2,1)S(1)}, bf16[64,512]{1,0:T(8,128)(2,1)S(1)}, u32[]{:S(2)}, u32[]{:S(2)}) collective-permute-start(bf16[64,512]{1,0:T(8,128)(2,1)S(1)} %heads.1.refs_0_), channel_id=1, source_target_pairs={{0,64},{32,96},{64,128},{96,160},{128,192},{160,224},{192,0},{224,... | collective-permute-start | bytes 196616 | tf_op jit(solution)/shard_map/ppermute | solution.py:476
  27.9 3.1 %collective-permute-start.2 = (bf16[64,512]{1,0:T(8,128)(2,1)S(1)}, bf16[64,512]{1,0:T(8,128)(2,1)S(1)}, u32[]{:S(2)}, u32[]{:S(2)}) collective-permute-start(bf16[64,512]{1,0:T(8,128)(2,1)S(1)} %heads.1.refs_0_), channel_id=1, source_target_pairs={{0,192},{32,224},{64,0},{96,32},{128,64},{160,96},{192,128},{224,1... | collective-permute-start | bytes 196616 | tf_op jit(solution)/shard_map/ppermute | solution.py:476
  31.1 0.7 collective-permute-start.1
  31.8 1.9 %collective-permute-start = (bf16[64,512]{1,0:T(8,128)(2,1)S(1)}, bf16[64,512]{1,0:T(8,128)(2,1)S(1)}, u32[]{:S(2)}, u32[]{:S(2)}) collective-permute-start(bf16[64,512]{1,0:T(8,128)(2,1)S(1)} %heads.1.refs_0_), channel_id=1, source_target_pairs={{0,224},{32,0},{64,32},{96,64},{128,96},{160,128},{192,160},{224,1... | collective-permute-start | bytes 196616 | tf_op jit(solution)/shard_map/ppermute | solution.py:476
  33.7 0.7 collective-permute-start.5
  34.8 2.1 %collective-permute-start.6 = (bf16[64,512]{1,0:T(8,128)(2,1)S(1)}, bf16[64,512]{1,0:T(8,128)(2,1)S(1)}, u32[]{:S(2)}, u32[]{:S(2)}) collective-permute-start(bf16[64,512]{1,0:T(8,128)(2,1)S(1)} %broadcast_select_fusion.1), channel_id=1, source_target_pairs={{0,64},{16,208},{32,96},{48,240},{64,128},{80,16},{96,160},{112,48... | collective-permute-start | bytes 196616 | tf_op jit(solution)/shard_map/ppermute | solution.py:481
  36.9 0.7 collective-permute-start.4
  37.5 0.5 collective-permute-done.5.refs_6_
  38.1 2.7 %collective-permute-done.6.refs_7_ = bf16[64,512]{1,0:T(8,128)(2,1)S(1)} collective-permute-done((bf16[64,512]{1,0:T(8,128)(2,1)S(1)}, bf16[64,512]{1,0:T(8,128)(2,1)S(1)}, u32[]{:S(2)}, u32[]{:S(2)}) %collective-permute-start.6) | collective-permute-done | bytes 65568 | tf_op jit(solution)/shard_map/ppermute | solution.py:481
  40.8 4.0 %collective-permute-start.7 = (bf16[512,512]{1,0:T(8,128)(2,1)S(1)}, bf16[512,512]{1,0:T(8,128)(2,1)S(1)}, u32[]{:S(2)}, u32[]{:S(2)}) collective-permute-start(bf16[512,512]{1,0:T(8,128)(2,1)S(1)} %pack.2.heads_ref), channel_id=1, source_target_pairs={{0,16},{16,0},{1,17},{17,1},{2,18},{18,2},{3,19},{19,3},{4,20},{20... | collective-permute-start | bytes 1572872 | tf_op jit(solution)/shard_map/ppermute | solution.py:472
  44.8 1.0 copy-done.5
  45.8 0.7 projecta.1
  46.5 1.3 projectb.1
  47.7 4.2 %all-to-all-start.1 = ((bf16[16,32,448]{2,1,0:T(8,128)(2,1)}), bf16[16,32,448]{2,1,0:T(8,128)(2,1)}, u32[]{:S(2)}, u32[]{:S(2)}) async-start(bf16[16,32,448]{2,1,0:T(8,128)(2,1)} %bitcast.7), calls=%async_computation.1 | async-start | bytes 1048576 | tf_op jit(solution)/shard_map/all_to_all | solution.py:468
  52.6 10.6 %all-to-all-done.1.parts_ref = bf16[16,32,448]{2,1,0:T(8,128)(2,1)} async-done(((bf16[16,32,448]{2,1,0:T(8,128)(2,1)}), bf16[16,32,448]{2,1,0:T(8,128)(2,1)}, u32[]{:S(2)}, u32[]{:S(2)}) %all-to-all-start.1) | async-done | bytes 458784 | tf_op jit(solution)/shard_map/all_to_all | solution.py:468
  63.2 1.4 middle.1
  64.6 13.5 %all_to_all.20 = bf16[16,32,512]{2,1,0:T(8,128)(2,1)S(1)} all-to-all(bf16[16,32,512]{2,1,0:T(8,128)(2,1)S(1)} %get-tuple-element.17), channel_id=1, replica_groups=mesh['z'=8,'core'=2,'y'=4,'x'=4] {'y','x'}, dimensions={0} | all-to-all | bytes 1048576 | tf_op jit(solution)/shard_map/all_to_all | solution.py:468
  78.1 2.1 %collective-permute-start.8 = (bf16[512,512]{1,0:T(8,128)(2,1)S(1)}, bf16[512,512]{1,0:T(8,128)(2,1)S(1)}, u32[]{:S(2)}, u32[]{:S(2)}) collective-permute-start(bf16[512,512]{1,0:T(8,128)(2,1)S(1)} %bitcast.13), channel_id=1, source_target_pairs={{0,16},{16,0},{1,17},{17,1},{2,18},{18,2},{3,19},{19,3},{4,20},{20... | collective-permute-start | bytes 1572872 | tf_op jit(solution)/shard_map/ppermute | solution.py:472
  80.1 1.0 first.1.part_ref
  81.1 0.5 collective-permute-done.8.other_ref
  81.7 0.8 widen.3
  82.5 1.0 collective-permute-start.11
  83.5 0.6 collective-permute-start.12
  84.1 1.0 collective-permute-start.13
  85.0 0.6 widen.2.keep_ref
  85.6 10.4 %collective-permute-done.13.far_ref = bf16[592,128]{1,0:T(8,128)(2,1)S(1)} collective-permute-done((bf16[592,128]{1,0:T(8,128)(2,1)S(1)}, bf16[592,128]{1,0:T(8,128)(2,1)S(1)}, u32[]{:S(2)}, u32[]{:S(2)}) %collective-permute-start.13) | collective-permute-done | bytes 151584 | tf_op jit(solution)/shard_map/ppermute | solution.py:481
  96.2 1.8 %collective-permute-start.14 = (bf16[592,128]{1,0:T(8,128)(2,1)S(1)}, bf16[592,128]{1,0:T(8,128)(2,1)S(1)}, u32[]{:S(2)}, u32[]{:S(2)}) collective-permute-start(bf16[592,128]{1,0:T(8,128)(2,1)S(1)} %get-tuple-element.22), channel_id=1, source_target_pairs={{0,192},{32,224},{64,0},{96,32},{128,64},{160,96},{192,128},{224,1... | collective-permute-start | bytes 454664 | tf_op jit(solution)/shard_map/ppermute | solution.py:476
  98.0 1.0 collective-permute-start.15
  99.0 4.1 %collective-permute-done.14.above_ref = bf16[592,128]{1,0:T(8,128)(2,1)S(1)} collective-permute-done((bf16[592,128]{1,0:T(8,128)(2,1)S(1)}, bf16[592,128]{1,0:T(8,128)(2,1)S(1)}, u32[]{:S(2)}, u32[]{:S(2)}) %collective-permute-start.14) | collective-permute-done | bytes 151584 | tf_op jit(solution)/shard_map/ppermute | solution.py:476
  103.1 2.2 %collective-permute-done.15.below_ref = bf16[592,128]{1,0:T(8,128)(2,1)S(1)} collective-permute-done((bf16[592,128]{1,0:T(8,128)(2,1)S(1)}, bf16[592,128]{1,0:T(8,128)(2,1)S(1)}, u32[]{:S(2)}, u32[]{:S(2)}) %collective-permute-start.15) | collective-permute-done | bytes 151584 | tf_op jit(solution)/shard_map/ppermute | solution.py:476
  105.5 1.8 %collective-permute-start.19 = (bf16[288,128]{1,0:T(8,128)(2,1)S(1)}, bf16[288,128]{1,0:T(8,128)(2,1)S(1)}, u32[]{:S(2)}, u32[]{:S(2)}) collective-permute-start(bf16[288,128]{1,0:T(8,128)(2,1)S(1)} %hidden.1.refs_0_), channel_id=1, source_target_pairs={{0,64},{32,96},{64,128},{96,160},{128,192},{160,224},{192,0},{224,... | collective-permute-start | bytes 221192 | tf_op jit(solution)/shard_map/ppermute | solution.py:476
  107.3 1.8 %collective-permute-start.18 = (bf16[288,128]{1,0:T(8,128)(2,1)S(1)}, bf16[288,128]{1,0:T(8,128)(2,1)S(1)}, u32[]{:S(2)}, u32[]{:S(2)}) collective-permute-start(bf16[288,128]{1,0:T(8,128)(2,1)S(1)} %hidden.1.refs_0_), channel_id=1, source_target_pairs={{0,192},{32,224},{64,0},{96,32},{128,64},{160,96},{192,128},{224,1... | collective-permute-start | bytes 221192 | tf_op jit(solution)/shard_map/ppermute | solution.py:476
  109.1 2.7 %collective-permute-start.16 = (bf16[288,128]{1,0:T(8,128)(2,1)S(1)}, bf16[288,128]{1,0:T(8,128)(2,1)S(1)}, u32[]{:S(2)}, u32[]{:S(2)}) collective-permute-start(bf16[288,128]{1,0:T(8,128)(2,1)S(1)} %hidden.1.refs_0_), channel_id=1, source_target_pairs={{0,224},{32,0},{64,32},{96,64},{128,96},{160,128},{192,160},{224,1... | collective-permute-start | bytes 221192 | tf_op jit(solution)/shard_map/ppermute | solution.py:476
  111.8 0.7 collective-permute-done.18.refs_3_
  112.5 2.0 %collective-permute-start.22 = (bf16[288,128]{1,0:T(8,128)(2,1)S(1)}, bf16[288,128]{1,0:T(8,128)(2,1)S(1)}, u32[]{:S(2)}, u32[]{:S(2)}) collective-permute-start(bf16[288,128]{1,0:T(8,128)(2,1)S(1)} %broadcast_select_fusion), channel_id=1, source_target_pairs={{0,64},{16,208},{32,96},{48,240},{64,128},{80,16},{96,160},{112,48... | collective-permute-start | bytes 221192 | tf_op jit(solution)/shard_map/ppermute | solution.py:481
  114.7 2.3 %collective-permute-done.21.refs_6_ = bf16[288,128]{1,0:T(8,128)(2,1)S(1)} collective-permute-done((bf16[288,128]{1,0:T(8,128)(2,1)S(1)}, bf16[288,128]{1,0:T(8,128)(2,1)S(1)}, u32[]{:S(2)}, u32[]{:S(2)}) %collective-permute-start.21) | collective-permute-done | bytes 73760 | tf_op jit(solution)/shard_map/ppermute | solution.py:476
  117.0 2.3 %collective-permute-done.22.refs_7_ = bf16[288,128]{1,0:T(8,128)(2,1)S(1)} collective-permute-done((bf16[288,128]{1,0:T(8,128)(2,1)S(1)}, bf16[288,128]{1,0:T(8,128)(2,1)S(1)}, u32[]{:S(2)}, u32[]{:S(2)}) %collective-permute-start.22) | collective-permute-done | bytes 73760 | tf_op jit(solution)/shard_map/ppermute | solution.py:481
  119.4 0.8 collective-permute-done.20.refs_5_
  120.2 3.6 %collective-permute-start.23 = (bf16[2304,128]{1,0:T(8,128)(2,1)S(1)}, bf16[2304,128]{1,0:T(8,128)(2,1)S(1)}, u32[]{:S(2)}, u32[]{:S(2)}) collective-permute-start(bf16[2304,128]{1,0:T(8,128)(2,1)S(1)} %pack.3), channel_id=1, source_target_pairs={{0,16},{16,0},{1,17},{17,1},{2,18},{18,2},{3,19},{19,3},{4,20},{20... | collective-permute-start | bytes 1769480 | tf_op jit(solution)/shard_map/ppermute | solution.py:472
  123.8 0.6 downa.1.rest_0_
  124.4 1.0 collective-permute-done.23
  125.5 0.7 downb.1
  126.1 13.4 %all_to_all.21.parts_ref = bf16[16,32,448]{2,1,0:T(8,128)(2,1)S(1)} all-to-all(bf16[16,32,448]{2,1,0:T(8,128)(2,1)S(1)} %bitcast.22), channel_id=1, replica_groups=mesh['z'=8,'core'=2,'y'=4,'x'=4] {'y','x'}, dimensions={0} | all-to-all | bytes 917504 | tf_op jit(solution)/shard_map/all_to_all | solution.py:468
  139.5 0.7 last.1
  (38 shorter events, 1.6 us)
Async XLA Ops:
  0.0 24.5 %copy-start.2 = (bf16[8,512,128]{2,1,0:T(8,128)(2,1)S(1)}, bf16[8,512,128]{2,1,0:T(8,128)(2,1)}, u32[]{:S(2)}) copy-start(bf16[8,512,128]{2,1,0:T(8,128)(2,1)} %w_ref.1) | copy-start | bytes 3145732
  0.0 44.8 %copy-start.1 = (bf16[1024,448]{0,1:T(8,128)(2,1)S(1)}, bf16[1024,448]{0,1:T(8,128)(2,1)}, u32[]{:S(2)}) copy-start(bf16[1024,448]{0,1:T(8,128)(2,1)} %param.18) | copy-start | bytes 2752516
  7.4 44.5 %copy-start.3 = (bf16[448,1152]{1,0:T(8,128)(2,1)S(1)}, bf16[448,1152]{1,0:T(8,128)(2,1)}, u32[]{:S(2)}) copy-start(bf16[448,1152]{1,0:T(8,128)(2,1)} %g_ref.1) | copy-start | bytes 3096580
  7.4 45.2 %copy-start.6 = (bf16[448]{0:T(512)(128)(2,1)S(1)}, bf16[448]{0:T(512)(128)(2,1)}, u32[]{:S(2)}) copy-start(bf16[448]{0:T(512)(128)(2,1)} %param.20) | copy-start | bytes 2692
  7.4 17.0 %all-to-all-start = ((bf16[32,8,512]{2,1,0:T(8,128)(2,1)}), bf16[32,8,512]{2,1,0:T(8,128)(2,1)S(1)}, u32[]{:S(2)}, u32[]{:S(2)}) async-start(bf16[32,8,512]{2,1,0:T(8,128)(2,1)} %bitcast.26), calls=%async_computation | async-start | bytes 524288 | tf_op jit(solution)/shard_map/all_to_all | solution.py:468
  24.9 8.9 %collective-permute-start.3 = (bf16[64,512]{1,0:T(8,128)(2,1)S(1)}, bf16[64,512]{1,0:T(8,128)(2,1)S(1)}, u32[]{:S(2)}, u32[]{:S(2)}) collective-permute-start(bf16[64,512]{1,0:T(8,128)(2,1)S(1)} %heads.1.refs_0_), channel_id=1, source_target_pairs={{0,64},{32,96},{64,128},{96,160},{128,192},{160,224},{192,0},{224,... | collective-permute-start | bytes 196616 | tf_op jit(solution)/shard_map/ppermute | solution.py:476
  27.9 6.8 %collective-permute-start.2 = (bf16[64,512]{1,0:T(8,128)(2,1)S(1)}, bf16[64,512]{1,0:T(8,128)(2,1)S(1)}, u32[]{:S(2)}, u32[]{:S(2)}) collective-permute-start(bf16[64,512]{1,0:T(8,128)(2,1)S(1)} %heads.1.refs_0_), channel_id=1, source_target_pairs={{0,192},{32,224},{64,0},{96,32},{128,64},{160,96},{192,128},{224,1... | collective-permute-start | bytes 196616 | tf_op jit(solution)/shard_map/ppermute | solution.py:476
  31.1 6.5 %collective-permute-start.1 = (bf16[64,512]{1,0:T(8,128)(2,1)S(1)}, bf16[64,512]{1,0:T(8,128)(2,1)S(1)}, u32[]{:S(2)}, u32[]{:S(2)}) collective-permute-start(bf16[64,512]{1,0:T(8,128)(2,1)S(1)} %heads.1.refs_0_), channel_id=1, source_target_pairs={{0,32},{32,64},{64,96},{96,128},{128,160},{160,192},{192,224},{224... | collective-permute-start | bytes 196616 | tf_op jit(solution)/shard_map/ppermute | solution.py:476
  31.8 5.7 %collective-permute-start = (bf16[64,512]{1,0:T(8,128)(2,1)S(1)}, bf16[64,512]{1,0:T(8,128)(2,1)S(1)}, u32[]{:S(2)}, u32[]{:S(2)}) collective-permute-start(bf16[64,512]{1,0:T(8,128)(2,1)S(1)} %heads.1.refs_0_), channel_id=1, source_target_pairs={{0,224},{32,0},{64,32},{96,64},{128,96},{160,128},{192,160},{224,1... | collective-permute-start | bytes 196616 | tf_op jit(solution)/shard_map/ppermute | solution.py:476
  33.7 4.3 %collective-permute-start.5 = (bf16[64,512]{1,0:T(8,128)(2,1)S(1)}, bf16[64,512]{1,0:T(8,128)(2,1)S(1)}, u32[]{:S(2)}, u32[]{:S(2)}) collective-permute-start(bf16[64,512]{1,0:T(8,128)(2,1)S(1)} %collective-permute-done.3.refs_4_), channel_id=1, source_target_pairs={{0,32},{32,64},{64,96},{96,128},{128,160},{160,192},{192,224},{224... | collective-permute-start | bytes 196616 | tf_op jit(solution)/shard_map/ppermute | solution.py:476
  34.8 6.0 %collective-permute-start.6 = (bf16[64,512]{1,0:T(8,128)(2,1)S(1)}, bf16[64,512]{1,0:T(8,128)(2,1)S(1)}, u32[]{:S(2)}, u32[]{:S(2)}) collective-permute-start(bf16[64,512]{1,0:T(8,128)(2,1)S(1)} %broadcast_select_fusion.1), channel_id=1, source_target_pairs={{0,64},{16,208},{32,96},{48,240},{64,128},{80,16},{96,160},{112,48... | collective-permute-start | bytes 196616 | tf_op jit(solution)/shard_map/ppermute | solution.py:481
  36.9 3.9 %collective-permute-start.4 = (bf16[64,512]{1,0:T(8,128)(2,1)S(1)}, bf16[64,512]{1,0:T(8,128)(2,1)S(1)}, u32[]{:S(2)}, u32[]{:S(2)}) collective-permute-start(bf16[64,512]{1,0:T(8,128)(2,1)S(1)} %collective-permute-done.2.refs_3_), channel_id=1, source_target_pairs={{0,224},{32,0},{64,32},{96,64},{128,96},{160,128},{192,160},{224,1... | collective-permute-start | bytes 196616 | tf_op jit(solution)/shard_map/ppermute | solution.py:476
  40.8 5.7 %collective-permute-start.7 = (bf16[512,512]{1,0:T(8,128)(2,1)S(1)}, bf16[512,512]{1,0:T(8,128)(2,1)S(1)}, u32[]{:S(2)}, u32[]{:S(2)}) collective-permute-start(bf16[512,512]{1,0:T(8,128)(2,1)S(1)} %pack.2.heads_ref), channel_id=1, source_target_pairs={{0,16},{16,0},{1,17},{17,1},{2,18},{18,2},{3,19},{19,3},{4,20},{20... | collective-permute-start | bytes 1572872 | tf_op jit(solution)/shard_map/ppermute | solution.py:472
  44.8 1.0 copy-start.5
  47.7 15.4 %all-to-all-start.1 = ((bf16[16,32,448]{2,1,0:T(8,128)(2,1)}), bf16[16,32,448]{2,1,0:T(8,128)(2,1)}, u32[]{:S(2)}, u32[]{:S(2)}) async-start(bf16[16,32,448]{2,1,0:T(8,128)(2,1)} %bitcast.7), calls=%async_computation.1 | async-start | bytes 1048576 | tf_op jit(solution)/shard_map/all_to_all | solution.py:468
  52.0 29.1 %collective-permute-start.9 = (bf16[448,1152]{1,0:T(8,128)(2,1)S(1)}, bf16[448,1152]{1,0:T(8,128)(2,1)S(1)}, u32[]{:S(2)}, u32[]{:S(2)}) collective-permute-start(bf16[448,1152]{1,0:T(8,128)(2,1)S(1)} %copy-done.3), channel_id=1, source_target_pairs={{0,16},{16,0},{1,17},{17,1},{2,18},{18,2},{3,19},{19,3},{4,20},{20... | collective-permute-start | bytes 3096584 | tf_op jit(solution)/shard_map/ppermute | solution.py:472
  52.3 28.8 %collective-permute-start.10 = (bf16[448,1152]{1,0:T(8,128)(2,1)}, bf16[448,1152]{1,0:T(8,128)(2,1)S(1)}, u32[]{:S(2)}, u32[]{:S(2)}) collective-permute-start(bf16[448,1152]{1,0:T(8,128)(2,1)} %u_ref.1), channel_id=1, source_target_pairs={{0,16},{16,0},{1,17},{17,1},{2,18},{18,2},{3,19},{19,3},{4,20},{20... | collective-permute-start | bytes 3096584 | tf_op jit(solution)/shard_map/ppermute | solution.py:472
  63.2 16.9 %copy-start.4 = (bf16[448,1152]{1,0:T(8,128)(2,1)S(1)}, bf16[448,1152]{1,0:T(8,128)(2,1)}, u32[]{:S(2)}) copy-start(bf16[448,1152]{1,0:T(8,128)(2,1)} %u_ref.1) | copy-start | bytes 3096580
  78.1 3.6 %collective-permute-start.8 = (bf16[512,512]{1,0:T(8,128)(2,1)S(1)}, bf16[512,512]{1,0:T(8,128)(2,1)S(1)}, u32[]{:S(2)}, u32[]{:S(2)}) collective-permute-start(bf16[512,512]{1,0:T(8,128)(2,1)S(1)} %bitcast.13), channel_id=1, source_target_pairs={{0,16},{16,0},{1,17},{17,1},{2,18},{18,2},{3,19},{19,3},{4,20},{20... | collective-permute-start | bytes 1572872 | tf_op jit(solution)/shard_map/ppermute | solution.py:472
  82.4 41.4 %copy-start = (bf16[1152,448]{0,1:T(8,128)(2,1)S(1)}, bf16[1152,448]{0,1:T(8,128)(2,1)}, u32[]{:S(2)}) copy-start(bf16[1152,448]{0,1:T(8,128)(2,1)} %param.23) | copy-start | bytes 3096580
  82.5 13.5 %collective-permute-start.11 = (bf16[1184,128]{1,0:T(8,128)(2,1)S(1)}, bf16[1184,128]{1,0:T(8,128)(2,1)S(1)}, u32[]{:S(2)}, u32[]{:S(2)}) collective-permute-start(bf16[1184,128]{1,0:T(8,128)(2,1)S(1)} %get-tuple-element.18), channel_id=1, source_target_pairs={{0,224},{32,0},{64,32},{96,64},{128,96},{160,128},{192,160},{224,1... | collective-permute-start | bytes 909320 | tf_op jit(solution)/shard_map/ppermute | solution.py:476
  83.5 12.5 %collective-permute-start.12 = (bf16[1184,128]{1,0:T(8,128)(2,1)S(1)}, bf16[1184,128]{1,0:T(8,128)(2,1)S(1)}, u32[]{:S(2)}, u32[]{:S(2)}) collective-permute-start(bf16[1184,128]{1,0:T(8,128)(2,1)S(1)} %get-tuple-element.19), channel_id=1, source_target_pairs={{0,32},{32,64},{64,96},{96,128},{128,160},{160,192},{192,224},{224... | collective-permute-start | bytes 909320 | tf_op jit(solution)/shard_map/ppermute | solution.py:476
  84.1 11.9 %collective-permute-start.13 = (bf16[592,128]{1,0:T(8,128)(2,1)S(1)}, bf16[592,128]{1,0:T(8,128)(2,1)S(1)}, u32[]{:S(2)}, u32[]{:S(2)}) collective-permute-start(bf16[592,128]{1,0:T(8,128)(2,1)S(1)} %get-tuple-element.20), channel_id=1, source_target_pairs={{0,64},{16,208},{32,96},{48,240},{64,128},{80,16},{96,160},{112,48... | collective-permute-start | bytes 454664 | tf_op jit(solution)/shard_map/ppermute | solution.py:481
  96.2 6.9 %collective-permute-start.14 = (bf16[592,128]{1,0:T(8,128)(2,1)S(1)}, bf16[592,128]{1,0:T(8,128)(2,1)S(1)}, u32[]{:S(2)}, u32[]{:S(2)}) collective-permute-start(bf16[592,128]{1,0:T(8,128)(2,1)S(1)} %get-tuple-element.22), channel_id=1, source_target_pairs={{0,192},{32,224},{64,0},{96,32},{128,64},{160,96},{192,128},{224,1... | collective-permute-start | bytes 454664 | tf_op jit(solution)/shard_map/ppermute | solution.py:476
  98.0 7.3 %collective-permute-start.15 = (bf16[592,128]{1,0:T(8,128)(2,1)S(1)}, bf16[592,128]{1,0:T(8,128)(2,1)S(1)}, u32[]{:S(2)}, u32[]{:S(2)}) collective-permute-start(bf16[592,128]{1,0:T(8,128)(2,1)S(1)} %get-tuple-element.23), channel_id=1, source_target_pairs={{0,64},{32,96},{64,128},{96,160},{128,192},{160,224},{192,0},{224,... | collective-permute-start | bytes 454664 | tf_op jit(solution)/shard_map/ppermute | solution.py:476
  105.5 6.3 %collective-permute-start.19 = (bf16[288,128]{1,0:T(8,128)(2,1)S(1)}, bf16[288,128]{1,0:T(8,128)(2,1)S(1)}, u32[]{:S(2)}, u32[]{:S(2)}) collective-permute-start(bf16[288,128]{1,0:T(8,128)(2,1)S(1)} %hidden.1.refs_0_), channel_id=1, source_target_pairs={{0,64},{32,96},{64,128},{96,160},{128,192},{160,224},{192,0},{224,... | collective-permute-start | bytes 221192 | tf_op jit(solution)/shard_map/ppermute | solution.py:476
  107.3 5.2 %collective-permute-start.18 = (bf16[288,128]{1,0:T(8,128)(2,1)S(1)}, bf16[288,128]{1,0:T(8,128)(2,1)S(1)}, u32[]{:S(2)}, u32[]{:S(2)}) collective-permute-start(bf16[288,128]{1,0:T(8,128)(2,1)S(1)} %hidden.1.refs_0_), channel_id=1, source_target_pairs={{0,192},{32,224},{64,0},{96,32},{128,64},{160,96},{192,128},{224,1... | collective-permute-start | bytes 221192 | tf_op jit(solution)/shard_map/ppermute | solution.py:476
  109.1 5.5 %collective-permute-start.17 = (bf16[288,128]{1,0:T(8,128)(2,1)S(1)}, bf16[288,128]{1,0:T(8,128)(2,1)S(1)}, u32[]{:S(2)}, u32[]{:S(2)}) collective-permute-start(bf16[288,128]{1,0:T(8,128)(2,1)S(1)} %hidden.1.refs_0_), channel_id=1, source_target_pairs={{0,32},{32,64},{64,96},{96,128},{128,160},{160,192},{192,224},{224... | collective-permute-start | bytes 221192 | tf_op jit(solution)/shard_map/ppermute | solution.py:476
  109.1 5.5 %collective-permute-start.16 = (bf16[288,128]{1,0:T(8,128)(2,1)S(1)}, bf16[288,128]{1,0:T(8,128)(2,1)S(1)}, u32[]{:S(2)}, u32[]{:S(2)}) collective-permute-start(bf16[288,128]{1,0:T(8,128)(2,1)S(1)} %hidden.1.refs_0_), channel_id=1, source_target_pairs={{0,224},{32,0},{64,32},{96,64},{128,96},{160,128},{192,160},{224,1... | collective-permute-start | bytes 221192 | tf_op jit(solution)/shard_map/ppermute | solution.py:476
  111.8 5.2 %collective-permute-start.21 = (bf16[288,128]{1,0:T(8,128)(2,1)S(1)}, bf16[288,128]{1,0:T(8,128)(2,1)S(1)}, u32[]{:S(2)}, u32[]{:S(2)}) collective-permute-start(bf16[288,128]{1,0:T(8,128)(2,1)S(1)} %collective-permute-done.19.refs_4_), channel_id=1, source_target_pairs={{0,32},{32,64},{64,96},{96,128},{128,160},{160,192},{192,224},{224... | collective-permute-start | bytes 221192 | tf_op jit(solution)/shard_map/ppermute | solution.py:476
  112.5 6.8 %collective-permute-start.22 = (bf16[288,128]{1,0:T(8,128)(2,1)S(1)}, bf16[288,128]{1,0:T(8,128)(2,1)S(1)}, u32[]{:S(2)}, u32[]{:S(2)}) collective-permute-start(bf16[288,128]{1,0:T(8,128)(2,1)S(1)} %broadcast_select_fusion), channel_id=1, source_target_pairs={{0,64},{16,208},{32,96},{48,240},{64,128},{80,16},{96,160},{112,48... | collective-permute-start | bytes 221192 | tf_op jit(solution)/shard_map/ppermute | solution.py:481
  114.6 5.5 %collective-permute-start.20 = (bf16[288,128]{1,0:T(8,128)(2,1)S(1)}, bf16[288,128]{1,0:T(8,128)(2,1)S(1)}, u32[]{:S(2)}, u32[]{:S(2)}) collective-permute-start(bf16[288,128]{1,0:T(8,128)(2,1)S(1)} %collective-permute-done.18.refs_3_), channel_id=1, source_target_pairs={{0,224},{32,0},{64,32},{96,64},{128,96},{160,128},{192,160},{224,1... | collective-permute-start | bytes 221192 | tf_op jit(solution)/shard_map/ppermute | solution.py:476
  120.2 5.3 %collective-permute-start.23 = (bf16[2304,128]{1,0:T(8,128)(2,1)S(1)}, bf16[2304,128]{1,0:T(8,128)(2,1)S(1)}, u32[]{:S(2)}, u32[]{:S(2)}) collective-permute-start(bf16[2304,128]{1,0:T(8,128)(2,1)S(1)} %pack.3), channel_id=1, source_target_pairs={{0,16},{16,0},{1,17},{17,1},{2,18},{18,2},{3,19},{19,3},{4,20},{20... | collective-permute-start | bytes 1769480 | tf_op jit(solution)/shard_map/ppermute | solution.py:472
